TPU v7x, 32 devices: a whole 2x2x4 slice. The times are simulated.
32 devices in a mesh: frame: 4 (over z), pos: 8 (over y, x, core).
Axes of the slice: x: 2, y: 2, z: 4, core: 2. Of those that a mesh axis runs over, the one named last changes fastest.
Arguments:
- latents: bfloat16 [128, 512, 256], P('frame', 'pos'), as said below
- gain_one: float32 [256], replicated, may hold values from 0.5 to 1.5
- query_one: bfloat16 [256, 256], replicated, as said below
- key_one: bfloat16 [256, 256], replicated, as said below
- value_one: bfloat16 [256, 256], replicated, may hold values from -0.375 to 0.375
- out_one: bfloat16 [256, 256], replicated, may hold values from -0.75 to 0.75
- gain_two: float32 [256], replicated, may hold values from 0.5 to 1.5
- query_two: bfloat16 [256, 256], replicated, as said below
- key_two: bfloat16 [256, 256], replicated, as said below
- value_two: bfloat16 [256, 256], replicated, may hold values from -0.375 to 0.375
- out_two: bfloat16 [256, 256], replicated, may hold values from -0.75 to 0.75
Outputs:
- decoded: bfloat16 [128, 512, 256], P('frame', 'pos')
Inputs may be any that keep to these rules, and one draw needn't show every extreme that they name: `latents`: latent features of the video. `query_one`: A projection of the spatial block. `key_one`: A projection of the spatial block. `query_two`: A projection of the temporal block. `key_two`: A projection of the temporal block.
All inputs are finite; a program needn't handle non-finite values.
Results may differ from a plain program's by a relative error of at most 0.015.
The roundings to bfloat16 on the way count: a program that leaves them out, or rounds other values in their place, can miss the bound.
Values may be sent and summed in bfloat16 or wider, within the bound.
No kernel may reach another device: no remote copies, remote signals or barrier semaphores. Data moves between devices by JAX's collectives and lax.ppermute only.
A program may use at most 320 MiB of HBM per device.

v0:
```python
import jax
import jax.numpy as jnp
from jax import lax
from jax.sharding import PartitionSpec as P

HEADS = 4


def broadcast(value, axis, source):
    kept = jnp.where(lax.axis_index(axis) == source, value, 0).astype(value.dtype)
    return lax.psum(kept, axis)


def normed(values, gain):
    wide = values.astype(jnp.float32)
    factor = lax.rsqrt(jnp.mean(wide * wide, axis=-1, keepdims=True) + 1e-06)
    return (wide * factor * gain).astype(jnp.bfloat16)


def project(values, weight):
    flat = values.reshape(-1, values.shape[-1])
    result = jnp.dot(flat, weight, preferred_element_type=jnp.float32).astype(jnp.bfloat16)
    return result.reshape(values.shape[:-1] + (weight.shape[1],))


def heads_of(values):
    return values.reshape(values.shape[:-1] + (HEADS, values.shape[-1] // HEADS))


def soft_step(carry, query, keys, vals, score_form, value_form):
    highest, totals, summed = carry
    scale = query.shape[-1] ** (-0.5)
    scores = jnp.einsum(score_form, query, keys, preferred_element_type=jnp.float32) * scale
    new_high = jnp.maximum(highest, jnp.max(scores, axis=-1))
    keep = jnp.exp(highest - new_high)
    weights = jnp.exp(scores - new_high[..., None])
    totals = totals * keep + jnp.sum(weights, axis=-1)
    summed = summed * keep[..., None] + jnp.einsum(
        value_form, weights.astype(jnp.bfloat16), vals, preferred_element_type=jnp.float32
    )
    return (new_high, totals, summed)


def empty_carry(lead, depth):
    return (
        jnp.full(lead, -1e30, jnp.float32),
        jnp.zeros(lead, jnp.float32),
        jnp.zeros(lead + (depth,), jnp.float32),
    )


def shards(
    latents,
    gain_one,
    query_one,
    key_one,
    value_one,
    out_one,
    gain_two,
    query_two,
    key_two,
    value_two,
    out_two,
):
    frames, places, width = latents.shape
    depth = width // HEADS
    normed_one = normed(latents, gain_one)
    q_one = heads_of(project(normed_one, query_one))
    k_one = project(normed_one, key_one)
    v_one = project(normed_one, value_one)
    first_keys, first_vals = (k_one[0], v_one[0])
    first_keys, first_vals = (broadcast(first_keys, "frame", 0), broadcast(first_vals, "frame", 0))
    first_keys, first_vals = (
        lax.all_gather(first_keys, "pos", axis=0, tiled=True),
        lax.all_gather(first_vals, "pos", axis=0, tiled=True),
    )
    carry = empty_carry((frames, HEADS, places), depth)
    carry = soft_step(
        carry, q_one, heads_of(first_keys), heads_of(first_vals), "fphd,khd->fhpk", "fhpk,khd->fhpd"
    )
    pieces = (
        lax.all_gather(k_one, "pos", axis=1, tiled=True),
        lax.all_gather(v_one, "pos", axis=1, tiled=True),
    )
    carry = soft_step(
        carry, q_one, heads_of(pieces[0]), heads_of(pieces[1]), "fphd,fkhd->fhpk", "fhpk,fkhd->fhpd"
    )
    attended_one = (
        (carry[2] / carry[1][..., None])
        .transpose(0, 2, 1, 3)
        .reshape(frames, places, width)
        .astype(jnp.bfloat16)
    )
    mixed_one = jnp.dot(
        attended_one.reshape(-1, width), out_one, preferred_element_type=jnp.float32
    ).reshape(frames, places, width)
    middle = (latents.astype(jnp.float32) + mixed_one).astype(jnp.bfloat16)
    normed_two = normed(middle, gain_two)
    q_two = heads_of(project(normed_two, query_two))
    carry_two = empty_carry((places, HEADS, frames), depth)
    k_two = project(normed_two, key_two)
    v_two = project(normed_two, value_two)
    pieces = (
        lax.all_gather(k_two, "frame", axis=0, tiled=True),
        lax.all_gather(v_two, "frame", axis=0, tiled=True),
    )
    carry_two = soft_step(
        carry_two,
        q_two,
        heads_of(pieces[0]),
        heads_of(pieces[1]),
        "fphd,kphd->phfk",
        "phfk,kphd->phfd",
    )
    attended_two = (
        (carry_two[2] / carry_two[1][..., None])
        .transpose(2, 0, 1, 3)
        .reshape(frames, places, width)
        .astype(jnp.bfloat16)
    )
    mixed_two = jnp.dot(
        attended_two.reshape(-1, width), out_two, preferred_element_type=jnp.float32
    ).reshape(frames, places, width)
    return (middle.astype(jnp.float32) + mixed_two).astype(jnp.bfloat16)


def solution(mesh):
    return jax.shard_map(
        shards,
        mesh=mesh,
        in_specs=(P("frame", "pos", None), P(), P(), P(), P(), P(), P(), P(), P(), P(), P()),
        out_specs=P("frame", "pos", None),
        check_vma=False,
    )
```

profile of v0, /device:TPU:0, one launch (start us, length us, event | category | flops | bytes accessed | tf_op | source)
XLA Modules:
  0.0 353.1 jit_solution(12768922150554338850)
XLA Ops:
  7.4 1.6 fusion.23
  9.0 1.6 fusion.25
  10.6 1.4 convolution_convert_fusion.3
  12.0 0.4 convolution_convert_fusion.5
  12.4 0.7 slice_select_fusion
  13.2 0.2 copy-done.3
  13.4 0.3 all-gather.5.cloned.1.call-update
  13.8 1.6 copy.78
  15.4 1.4 convolution_convert_fusion.4
  16.9 3.3 reshape_reshape.6
  20.2 1.9 copy.71
  22.1 28.0 %all-reduce.3.cloned.1.call-done = (bf16[64,256]{1,0:T(8,128)(2,1)}, bf16[64,256]{1,0:T(8,128)(2,1)}) async-done(((bf16[64,256]{1,0:T(8,128)(2,1)}, bf16[64,256]{1,0:T(8,128)(2,1)}), (bf16[64,256]{1,0:T(8,128)(2,1)}, bf16[64,256]{1,0:T(8,128)(2,1)})) %all-reduce.3.cloned.1.call-update) | async-done | bytes 65552 | tf_op jit(solution)/shard_map/psum | solution.py:11
  50.1 10.4 %all_gather.18 = bf16[512,256]{1,0:T(8,128)(2,1)S(1)} all-gather(bf16[64,256]{1,0:T(8,128)(2,1)} %get-tuple-element.6), channel_id=1, replica_groups=mesh['frame'=4,'pos'=8] {'pos'}, dimensions={0}, use_global_device_ids=true | all-gather | bytes 294912 | tf_op jit(solution)/shard_map/all_gather | solution.py:74
  60.5 0.1 copy.70
  60.7 10.1 %all_gather.19 = bf16[512,256]{1,0:T(8,128)(2,1)S(1)} all-gather(bf16[64,256]{1,0:T(8,128)(2,1)} %get-tuple-element.5), channel_id=1, replica_groups=mesh['frame'=4,'pos'=8] {'pos'}, dimensions={0}, use_global_device_ids=true | all-gather | bytes 294912 | tf_op jit(solution)/shard_map/all_gather | solution.py:75
  70.7 0.1 copy.72
  70.9 9.7 %fusion.47 = f32[4,512,2048]{1,2,0} fusion(bf16[4,64,2048]{1,2,0:T(8,128)(2,1)} %bitcast.114, bf16[512,4,64]{0,2,1:T(8,128)(2,1)S(1)} %bitcast.121), kind=kOutput, calls=%fused_computation.74 | convolution fusion | flops 536870912 | bytes 18087936
  80.5 8.1 %bitcast_reduce_fusion = f32[32,4,64]{2,0,1:T(8,128)S(1)} fusion(f32[4,512,32,64]{1,3,2,0:T(8,128)} %bitcast.103), kind=kLoop, calls=%fused_computation.1 | loop fusion | flops 8380416 | bytes 16809984 | tf_op jit(solution)/shard_map/reduce_max | solution.py:34
  88.6 12.2 %copy.73 = bf16[32,512,256]{1,2,0:T(8,128)(2,1)} copy(bf16[32,512,256]{2,1,0:T(8,128)(2,1)} %all-gather.5.cloned.1.call-done) | data formatting | bytes 16777216 | tf_op jit(solution)/shard_map/all_gather | solution.py:82
  100.8 14.4 %multiply_reduce_fusion = (f32[32,4,64]{2,1,0:T(4,128)S(1)}, f32[32,4,64,512]{3,2,1,0:T(8,128)}) fusion(bf16[32,512,4,64]{1,3,2,0:T(8,128)(2,1)} %bitcast.106, bf16[32,64,4,64]{3,2,1,0:T(4,128)(2,1)S(1)} %reshape_reshape.6), kind=kOutput, calls=%fused_computation.4 | convolution fusion | flops 545251328 | bytes 26247168 | tf_op jit(solution)/shard_map/fphd,fkhd->fhpk/dot_general | solution.py:33
  115.3 1.1 copy-done.1
  116.4 4.1 %fusion.3 = f32[32,4,64]{2,0,1:T(8,128)S(1)} fusion(f32[4,512,32,64]{1,3,2,0:T(8,128)S(1)} %bitcast.104, f32[32,4,64]{2,0,1:T(8,128)S(1)} %get-tuple-element.15), kind=kLoop, calls=%fused_computation.7 | loop fusion | flops 12574720 | bytes 16842752 | tf_op jit(solution)/shard_map/reduce_sum | solution.py:37
  120.5 1.9 copy-done.2
  122.3 5.3 %fusion.1 = (f32[32,4,64]{2,1,0:T(4,128)S(1)}, bf16[32,4,64,512]{3,2,1,0:T(8,128)(2,1)}) fusion(f32[32,4,64,512]{3,2,1,0:T(8,128)S(1)} %copy-done.2, f32[32,4,64]{2,1,0:T(4,128)S(1)} %copy.77), kind=kLoop, calls=%fused_computation.5 | loop fusion | flops 16769024 | bytes 25231360 | tf_op jit(solution)/shard_map/reduce_sum | solution.py:37
  127.7 6.0 %fusion.5 = f32[4,64,32,64]{3,1,2,0:T(8,128)} fusion(bf16[512,4,64,1]{0,2,3,1:T(8,128)(2,1)S(1)} %bitcast.122, f32[4,512,32,64]{1,3,2,0:T(8,128)S(1)} %bitcast.105, f32[32,4,64]{2,0,1:T(8,128)S(1)} %get-tuple-element.15), kind=kOutput, calls=%fused_computation.9 | convolution fusion | flops 549453824 | bytes 19169280 | tf_op jit(solution)/shard_map/fhpk,khd->fhpd/dot_general | solution.py:38
  133.6 13.8 %copy.79 = bf16[32,512,256]{1,2,0:T(8,128)(2,1)} copy(bf16[32,512,256]{2,0,1:T(8,128)(2,1)} %all-gather.7.cloned.1.call-done) | data formatting | bytes 16777216 | tf_op jit(solution)/shard_map/all_gather | solution.py:83
  147.4 10.9 %fusion.15 = bf16[32,64,4,64]{1,3,0,2:T(8,128)(2,1)} fusion(f32[4,64,32,64]{3,1,2,0:T(8,128)} %fusion.5, bf16[32,512,4,64]{1,3,2,0:T(8,128)(2,1)} %bitcast.115, bf16[32,4,64,512]{3,2,1,0:T(8,128)(2,1)} %get-tuple-element.10, f32[32,64,4]{1,0,2:T(8,128)S(1)} %get-tuple-element.7, f32[32,64,4]{1,0,2:T(8,128)S(1)} %get-tuple-element.8, ...), kind=kOutput, calls=%fused_computation.20 | convolution fusion | flops 539492352 | bytes 20021248 | tf_op jit(solution)/shard_map/fhpk,fkhd->fhpd/dot_general | solution.py:38
  158.3 3.2 copy.84
  161.5 2.2 convert_element_type.74
  163.7 1.8 fusion.27
  165.5 0.9 copy-done.4
  166.5 0.3 fusion.29
  166.8 1.5 convolution_convert_fusion.1
  168.4 1.5 convolution_convert_fusion
  169.9 0.4 convolution_convert_fusion.2
  170.4 1.1 reshape_reshape.7
  171.4 75.7 %all-gather.9.cloned.1.call-done = bf16[128,64,256]{2,1,0:T(8,128)(2,1)} async-done(((bf16[32,64,256]{2,1,0:T(8,128)(2,1)}), bf16[128,64,256]{2,1,0:T(8,128)(2,1)}) %all-gather.9.cloned.1.call-update) | async-done | bytes 4194320 | tf_op jit(solution)/shard_map/all_gather | solution.py:104
  247.1 6.8 %copy.85 = bf16[128,64,256]{0,2,1:T(8,128)(2,1)} copy(bf16[128,64,256]{2,1,0:T(8,128)(2,1)} %all-gather.9.cloned.1.call-done) | data formatting | bytes 8388608 | tf_op jit(solution)/shard_map/all_gather | solution.py:104
  253.9 6.5 %multiply_reduce_fusion.1 = (f32[64,4,32]{2,1,0:T(4,128)S(1)}, f32[64,4,32,128]{3,2,1,0:T(8,128)}) fusion(bf16[128,64,4,64]{0,3,2,1:T(8,128)(2,1)} %bitcast.113, bf16[32,64,4,64]{3,2,1,0:T(4,128)(2,1)S(1)} %reshape_reshape.7), kind=kOutput, calls=%fused_computation.24 | convolution fusion | flops 136306688 | bytes 9469952 | tf_op jit(solution)/shard_map/fphd,kphd->phfk/dot_general | solution.py:33
  260.4 0.1 multiply_bitcast_fusion
  260.4 4.0 %fusion.17 = f32[64,4,32]{2,1,0:T(4,128)S(1)} fusion(f32[64,4,32,128]{3,2,1,0:T(8,128)} %get-tuple-element.21, f32[64,4,32]{2,1,0:T(4,128)S(1)} %get-tuple-element.12), kind=kLoop, calls=%fused_computation.25 | loop fusion | flops 3137536 | bytes 4259840 | tf_op jit(solution)/shard_map/reduce_sum | solution.py:37
  264.5 0.1 bitcast_add_fusion.3
  264.5 63.5 %all-gather.11.cloned.1.call-done = bf16[128,64,256]{2,1,0:T(8,128)(2,1)} async-done(((bf16[32,64,256]{2,1,0:T(8,128)(2,1)}), bf16[128,64,256]{2,1,0:T(8,128)(2,1)}) %all-gather.11.cloned.1.call-update) | async-done | bytes 4194320 | tf_op jit(solution)/shard_map/all_gather | solution.py:105
  328.1 6.8 %copy.87 = bf16[128,64,256]{0,2,1:T(8,128)(2,1)} copy(bf16[128,64,256]{2,1,0:T(8,128)(2,1)} %all-gather.11.cloned.1.call-done) | data formatting | bytes 8388608 | tf_op jit(solution)/shard_map/all_gather | solution.py:105
  334.9 6.0 %fusion.13 = bf16[32,64,4,64]{3,0,2,1:T(8,128)(2,1)S(1)} fusion(bf16[128,64,4,64]{0,3,2,1:T(8,128)(2,1)} %bitcast.118, f32[64,4,32,128]{3,2,1,0:T(8,128)} %get-tuple-element.21, f32[32,64,4]{0,2,1:T(4,128)S(1)} %bitcast_add_fusion.3, f32[64,4,32]{2,1,0:T(4,128)S(1)} %get-tuple-element.12, f32[32,64,4]{0,2,1:T(4,128)S(1)} %get-tuple-element.11), kind=kOutput, calls=%fused_computation.17 | convolution fusion | flops 138936320 | bytes 9535488 | tf_op jit(solution)/shard_map/phfk,kphd->phfd/dot_general | solution.py:38
  340.9 1.1 copy.88
  341.9 1.4 convert_element_type.83
  343.3 2.6 fusion.30
  (38 shorter events, 0.4 us)
Async XLA Ops:
  7.4 156.3 %copy-start = (bf16[256,256]{1,0:T(8,128)(2,1)S(1)}, bf16[256,256]{1,0:T(8,128)(2,1)}, u32[]{:S(2)}) copy-start(bf16[256,256]{1,0:T(8,128)(2,1)} %param.16) | copy-start | bytes 393220
  7.4 4.6 %copy-start.6 = (bf16[256,256]{1,0:T(8,128)(2,1)S(1)}, bf16[256,256]{1,0:T(8,128)(2,1)}, u32[]{:S(2)}) copy-start(bf16[256,256]{1,0:T(8,128)(2,1)} %param.14) | copy-start | bytes 393220
  7.4 42.7 %all-reduce.3.cloned.1.call-start = ((), (), s32[]{:S(2)}) async-start(), calls=%async_computation.4 | async-start | bytes 131072 | tf_op jit(solution)/shard_map/psum | solution.py:11
  10.6 4.8 %copy-start.7 = (bf16[256,256]{1,0:T(8,128)(2,1)S(1)}, bf16[256,256]{1,0:T(8,128)(2,1)}, u32[]{:S(2)}) copy-start(bf16[256,256]{1,0:T(8,128)(2,1)} %param.13) | copy-start | bytes 393220
  12.4 1.0 copy-start.3
  13.2 75.5 %all-gather.5.cloned.1.call-start = ((), (), s32[]{:S(2)}) async-start(), calls=%async_computation | async-start | bytes 9437184 | tf_op jit(solution)/shard_map/all_gather | solution.py:82
  13.7 119.9 %all-gather.7.cloned.1.call-start = ((), (), s32[]{:S(2)}) async-start(), calls=%async_computation.1 | async-start | bytes 9437184 | tf_op jit(solution)/shard_map/all_gather | solution.py:83
  15.4 231.7 %all-gather.9.cloned.1.call-start = ((), (), s32[]{:S(2)}) async-start(), calls=%async_computation.2 | async-start | bytes 5242880 | tf_op jit(solution)/shard_map/all_gather | solution.py:104
  100.8 15.6 %copy-start.1 = (f32[4,512,2048]{1,2,0:S(1)}, f32[4,512,2048]{1,2,0}, u32[]{:S(2)}) copy-start(f32[4,512,2048]{1,2,0} %fusion.47) | copy-start | bytes 50331652
  116.4 5.9 %copy-start.2 = (f32[32,4,64,512]{3,2,1,0:T(8,128)S(1)}, f32[32,4,64,512]{3,2,1,0:T(8,128)}, u32[]{:S(2)}) copy-start(f32[32,4,64,512]{3,2,1,0:T(8,128)} %get-tuple-element.17) | copy-start | bytes 50331652
  158.3 5.4 %copy-start.5 = (bf16[32,64,256]{2,1,0:T(8,128)(2,1)S(1)}, bf16[32,64,256]{2,1,0:T(8,128)(2,1)}, u32[]{:S(2)}) copy-start(bf16[32,64,256]{2,1,0:T(8,128)(2,1)} %param.11) | copy-start | bytes 3145732
  161.5 5.0 %copy-start.12 = (f32[256]{0:T(256)S(1)}, f32[256]{0:T(256)}, u32[]{:S(2)}) copy-start(f32[256]{0:T(256)} %param.17) | copy-start | bytes 3076
  161.5 5.3 %copy-start.8 = (bf16[256,256]{1,0:T(8,128)(2,1)S(1)}, bf16[256,256]{1,0:T(8,128)(2,1)}, u32[]{:S(2)}) copy-start(bf16[256,256]{1,0:T(8,128)(2,1)} %param.19) | copy-start | bytes 393220
  163.7 4.7 %copy-start.9 = (bf16[256,256]{1,0:T(8,128)(2,1)S(1)}, bf16[256,256]{1,0:T(8,128)(2,1)}, u32[]{:S(2)}) copy-start(bf16[256,256]{1,0:T(8,128)(2,1)} %param.20) | copy-start | bytes 393220
  165.5 1.0 copy-start.4
  166.5 3.5 copy-start.10
  168.3 159.7 %all-gather.11.cloned.1.call-start = ((), (), s32[]{:S(2)}) async-start(), calls=%async_computation.3 | async-start | bytes 5242880 | tf_op jit(solution)/shard_map/all_gather | solution.py:105
  340.8 2.5 copy-start.11
Sparse Core Ops, SparseCore 0:
  13.3 36.7 all-reduce.2
  168.5 78.5 all-gather.8
  248.8 79.2 all-gather.10
Sparse Core Ops, SparseCore 1:
  15.7 59.0 all-gather.4
  76.7 54.2 all-gather.6
where the time goes:
time: 355 us; the launch traced here: 353 us
  waiting for transfers between devices  168 us (47%)
  matrix products  64.4 us (18%)
  local copies, waits for them, and re-layouts  59.7 us (17%)
  other arithmetic  25.9 us (7%)
  blocking collectives  20.5 us (6%)
  between operations  14.9 us (4%)
    all_gather x1, waiting for transfers between devices, shards(): lax.all_gather(k_two, 'frame', axis=0, tiled=True)  75.7 us
    all_gather x1, waiting for transfers between devices, shards(): lax.all_gather(v_two, 'frame', axis=0, tiled=True)  63.5 us
    psum x1, waiting for transfers between devices, broadcast(): return lax.psum(kept, axis)  28 us
    dot_general x3, matrix products, soft_step(): jnp.einsum(value_form, weights.astype(jnp.bfloat16), vals, preferred_elem...  22.8 us
    dot_general x2, matrix products, soft_step(): jnp.einsum(score_form, query, keys, preferred_element_type=jnp.float32)  20.8 us
    all_gather x1, local copies, waits for them, and re-layouts, shards(): lax.all_gather(v_one, 'pos', axis=1, tiled=True)  13.8 us
    reduce_sum x3, other arithmetic, soft_step(): totals = totals * keep + jnp.sum(weights, axis=-1)  13.3 us
    all_gather x1, local copies, waits for them, and re-layouts, shards(): lax.all_gather(k_one, 'pos', axis=1, tiled=True)  12.2 us
  transfers between devices with their start and end apart: 5, of which 3 were waited for; matrix products, arithmetic and copies ran while one was open for 25% of the time, Pallas kernels for 0%

commit v1 on v0

v1 whole, which is shorter than its diff:
```python
import functools

import jax
import jax.numpy as jnp
from jax import lax
from jax.experimental import pallas as pl
from jax.experimental.pallas import tpu as pltpu
from jax.sharding import PartitionSpec as P

HEADS = 4
LANES = 128
LOG2E = 1.4426950408889634


def normed(wide, gain):
    factor = lax.rsqrt(jnp.mean(wide * wide, axis=-1, keepdims=True) + 1e-06)
    return (wide * factor * gain).astype(jnp.bfloat16)


def dot(left, right):
    return jnp.dot(left, right, preferred_element_type=jnp.float32)


def dot_t(left, right):
    return lax.dot_general(
        left, right, (((1,), (1,)), ((), ())), preferred_element_type=jnp.float32
    )


def head_mask(rows, width, head):
    depth = width // HEADS
    lane = lax.broadcasted_iota(jnp.int32, (rows, width), 1)
    return (lane >= head * depth) & (lane < (head + 1) * depth)


def spatial_kernel(
    chips, shards, zf_ref, *refs
):
    mine, refs = refs[:chips], refs[chips:]
    other, refs = refs[:chips], refs[chips:]
    x0_ref, gain_ref, wq_ref, wk_ref, wv_ref, wo_ref = refs[:6]
    outs = refs[6 : 6 + shards]
    k_s, v_s, mid_s = refs[6 + shards :]
    width = wq_ref.shape[0]
    depth = width // HEADS
    half = width // 2
    gain = gain_ref[...]
    places = x0_ref.shape[0]
    local = mine[0].shape[1]

    @pl.when(pl.program_id(0) == 0)
    def _():
        n0 = normed(x0_ref[...].astype(jnp.float32), gain)
        k_s[places:, :] = dot(n0, wk_ref[...]).astype(jnp.bfloat16)
        v0 = dot(n0, wv_ref[...]).astype(jnp.bfloat16)
        ones = jnp.ones((2 * places, half), jnp.bfloat16)
        for pair in range(2):
            v_s[pair, places:, :half] = v0[:, pair * half : (pair + 1) * half]
            v_s[pair, :, half:] = ones

    x_mine = jnp.concatenate([r[0] for r in mine], axis=0).astype(jnp.float32)
    x_other = jnp.concatenate([r[0] for r in other], axis=0).astype(jnp.float32)
    n_mine = normed(x_mine, gain)
    n_all = jnp.concatenate([n_mine, normed(x_other, gain)], axis=0)
    k_s[:places, :] = dot(n_all, wk_ref[...]).astype(jnp.bfloat16)
    v = dot(n_all, wv_ref[...]).astype(jnp.bfloat16)
    for pair in range(2):
        v_s[pair, :places, :half] = v[:, pair * half : (pair + 1) * half]
    q = dot(n_mine, wq_ref[...]).astype(jnp.bfloat16)
    rows = q.shape[0]
    low = lax.broadcasted_iota(jnp.int32, (rows, half), 1) < depth
    keys = k_s[...]
    parts = []
    for pair in range(2):
        res = []
        for head in (2 * pair, 2 * pair + 1):
            qm = jnp.where(head_mask(rows, width, head), q, jnp.zeros_like(q))
            s = dot_t(qm, keys)
            m = jnp.max(s, axis=-1, keepdims=True)
            w = jnp.exp2((s - m) * (depth**-0.5 * LOG2E)).astype(jnp.bfloat16)
            res.append(dot(w, v_s[pair]))
        top = jnp.where(low, res[0][:, :half], res[1][:, :half])
        bottom = jnp.where(low, res[0][:, half:], res[1][:, half:])
        parts.append(top / bottom)
    attended = jnp.concatenate(parts, axis=1).astype(jnp.bfloat16)
    mid_s[...] = x_mine + dot(attended, wo_ref[...])
    zf = zf_ref[0]
    share = local // shards
    for t in range(shards):
        for s in range(chips):
            at = pl.multiple_of(s * local + (t ^ zf) * share, share)
            outs[t][s, 0] = mid_s[pl.ds(at, share), :].astype(jnp.bfloat16)


def spatial(zf, mine, other, x0, gain, wq, wk, wv, wo, shards):
    chips = len(mine)
    frames, local, width = mine[0].shape
    places = x0.shape[0]
    share = local // shards
    piece = pl.BlockSpec((1, local, width), lambda f, z: (f, 0, 0))
    full = lambda a: pl.BlockSpec(a.shape, lambda f, z, n=a.ndim: (0,) * n)
    return pl.pallas_call(
        functools.partial(spatial_kernel, chips, shards),
        grid_spec=pltpu.PrefetchScalarGridSpec(
            num_scalar_prefetch=1,
            grid=(frames,),
            in_specs=[piece] * (2 * chips) + [full(a) for a in (x0, gain, wq, wk, wv, wo)],
            out_specs=[pl.BlockSpec((chips, 1, share, width), lambda f, z: (0, f, 0, 0))] * shards,
            scratch_shapes=[
                pltpu.VMEM((2 * places, width), jnp.bfloat16),
                pltpu.VMEM((2, 2 * places, width), jnp.bfloat16),
                pltpu.VMEM((chips * local, width), jnp.float32),
            ],
        ),
        out_shape=[jax.ShapeDtypeStruct((chips, frames, share, width), jnp.bfloat16)] * shards,
        compiler_params=pltpu.CompilerParams(vmem_limit_bytes=48 * 2**20),
        name="spatial",
    )(zf, *mine, *other, x0, gain, wq, wk, wv, wo)


def take(ref, rows):
    return jnp.concatenate([ref[i, rows, :] for i in range(ref.shape[0])], axis=1)


def put(ref, rows, value):
    for i in range(ref.shape[0]):
        ref[i, rows, :] = value[:, i * LANES : (i + 1) * LANES]


def temporal_kernel(chips, shards, share, *refs):
    own, refs = refs[:shards], refs[shards:]
    came, refs = refs[: chips - 1], refs[chips - 1 :]
    gain_ref, wq_ref, wk_ref, wv_ref, wo_ref = refs[:5]
    outs = refs[5 : 5 + shards]
    x_s, q_s, k_s, v_s, a_s = refs[5 + shards :]
    width = wq_ref.shape[0]
    depth = width // HEADS
    half = width // 2
    block = own[0].shape[0]
    frames = block // share * chips * shards
    for t in range(shards):
        for s in range(chips):
            piece = own[t][...] if s == 0 else came[s - 1][t]
            put(x_s, pl.ds((t * chips + s) * block, block), piece.astype(jnp.float32))
    gain = gain_ref[...]
    for p in range(share):
        n = normed(take(x_s, pl.ds(p, frames, stride=share)), gain)
        q_s[p] = dot(n, wq_ref[...]).astype(jnp.bfloat16)
        k_s[p] = dot(n, wk_ref[...]).astype(jnp.bfloat16)
        v_s[p] = dot(n, wv_ref[...]).astype(jnp.bfloat16)
    lane = lax.broadcasted_iota(jnp.int32, (frames, half), 1)
    low, high = lane < depth, lane >= depth
    ones = [c.astype(jnp.float32).astype(jnp.bfloat16) for c in (low, high)]

    for p in range(share):
        q, k, v = q_s[p], k_s[p], v_s[p]
        parts = []
        for pair in range(2):
            cols = slice(pair * half, (pair + 1) * half)
            zero = jnp.zeros((frames, half), jnp.bfloat16)
            kp, vp = k[:, cols], v[:, cols]
            k2 = jnp.concatenate([jnp.where(low, kp, zero), jnp.where(high, kp, zero)], axis=0)
            v2 = jnp.concatenate(
                [
                    jnp.concatenate([jnp.where(low, vp, zero), ones[0]], axis=1),
                    jnp.concatenate([jnp.where(high, vp, zero), ones[1]], axis=1),
                ],
                axis=0,
            )
            s = dot_t(q[:, cols], k2)
            m0 = jnp.max(s[:, :frames], axis=-1, keepdims=True)
            m1 = jnp.max(s[:, frames:], axis=-1, keepdims=True)
            c = depth**-0.5 * LOG2E
            w = jnp.concatenate(
                [jnp.exp2((s[:, :frames] - m0) * c), jnp.exp2((s[:, frames:] - m1) * c)], axis=1
            ).astype(jnp.bfloat16)
            r = dot(w, v2)
            parts.append(r[:, :half] / r[:, half:])
        a = jnp.concatenate(parts, axis=1).astype(jnp.bfloat16)
        rows = pl.ds(p, frames, stride=share)
        put(a_s, rows, take(x_s, rows) + dot(a, wo_ref[...]))
    for t in range(shards):
        for s in range(chips):
            outs[t][s] = take(a_s, pl.ds((t * chips + s) * block, block)).astype(jnp.bfloat16)


def temporal(own, came, gain, wq, wk, wv, wo, share):
    shards, chips = len(own), len(came) + 1
    block, width = own[0].shape
    rows = block * chips * shards
    frames = rows // share
    return pl.pallas_call(
        functools.partial(temporal_kernel, chips, shards, share),
        out_shape=[jax.ShapeDtypeStruct((chips, block, width), jnp.bfloat16)] * shards,
        scratch_shapes=[
            pltpu.VMEM((width // LANES, rows, LANES), jnp.float32),
            pltpu.VMEM((share, frames, width), jnp.bfloat16),
            pltpu.VMEM((share, frames, width), jnp.bfloat16),
            pltpu.VMEM((share, frames, width), jnp.bfloat16),
            pltpu.VMEM((width // LANES, rows, LANES), jnp.float32),
        ],
        compiler_params=pltpu.CompilerParams(vmem_limit_bytes=48 * 2**20),
        name="temporal",
    )(*own, *came, gain, wq, wk, wv, wo)


def assemble_kernel(shards, share, ids_ref, *refs):
    pieces, out_ref, wide = refs[:shards], refs[shards], refs[shards + 1]
    for t in range(shards):
        at = pl.multiple_of((t ^ ids_ref[0]) * share, share)
        wide[:, pl.ds(at, share), :] = pieces[t][0].astype(jnp.float32)
    out_ref[...] = wide[...].astype(jnp.bfloat16)


def assemble(ids, pieces):
    shards = len(pieces)
    chips, frames, share, width = pieces[0].shape
    return pl.pallas_call(
        functools.partial(assemble_kernel, shards, share),
        grid_spec=pltpu.PrefetchScalarGridSpec(
            num_scalar_prefetch=1,
            grid=(chips,),
            in_specs=[pl.BlockSpec((1, frames, share, width), lambda s, ids: (s, 0, 0, 0))] * shards,
            out_specs=pl.BlockSpec(
                (frames, shards * share, width), lambda s, ids: (s ^ ids[1], 0, 0)
            ),
            scratch_shapes=[pltpu.VMEM((frames, shards * share, width), jnp.float32)],
        ),
        out_shape=jax.ShapeDtypeStruct((chips * frames, shards * share, width), jnp.bfloat16),
        name="assemble",
    )(ids, *pieces)


def swap(value, axis, size, mask):
    return lax.ppermute(value, axis, [(i, i ^ mask) for i in range(size)])


def shards_fn(
    shards,
    spots,
    latents,
    gain_one,
    query_one,
    key_one,
    value_one,
    out_one,
    gain_two,
    query_two,
    key_two,
    value_two,
    out_two,
):
    frames, local, width = latents.shape
    chips = spots // 2
    each = frames // chips
    share = local // shards
    zf = lax.axis_index("frame")
    chip = lax.axis_index("pos") // 2
    ids = jnp.stack([zf, chip]).astype(jnp.int32)

    first = latents[0]
    found = first
    for s in range(1, shards):
        sent = lax.ppermute(first, "frame", [(0, s)])
        found = jnp.where(zf == s, sent, found)
    x0 = lax.all_gather(found, "pos", axis=0, tiled=True)

    mine = [lax.dynamic_slice_in_dim(latents, (chip ^ s) * each, each, 0) for s in range(chips)]
    mine = [mine[0]] + [swap(mine[s], "pos", spots, 2 * s) for s in range(1, chips)]
    other = [swap(m, "pos", spots, 1) for m in mine]
    row = lambda g: g.reshape(1, -1)
    mid = spatial(
        ids, mine, other, x0, row(gain_one), query_one, key_one, value_one, out_one, shards
    )
    mid = [mid[0]] + [swap(mid[t], "frame", shards, t) for t in range(1, shards)]
    flat = [m.reshape(chips, each * share, width) for m in mid]
    own = [m[0] for m in flat]
    came = [
        swap(jnp.stack([m[s] for m in flat]), "pos", spots, 2 * s) for s in range(1, chips)
    ]
    done = temporal(
        own, came, row(gain_two), query_two, key_two, value_two, out_two, share
    )
    done = [done[0]] + [swap(done[t], "frame", shards, t) for t in range(1, shards)]
    return assemble(ids, [d.reshape(chips, each, share, width) for d in done])


def solution(mesh):
    return jax.shard_map(
        functools.partial(shards_fn, mesh.shape["frame"], mesh.shape["pos"]),
        mesh=mesh,
        in_specs=(P("frame", "pos", None), P(), P(), P(), P(), P(), P(), P(), P(), P(), P()),
        out_specs=P("frame", "pos", None),
        check_vma=False,
    )
```

time: 355 us -> 125 us (0.35)
  waiting for transfers between devices: 168 us -> 48.9 us
  matrix products: 64.4 us -> 0 us
  local copies, waits for them, and re-layouts: 59.7 us -> 4.91 us
  Pallas kernels: 0 us -> 30.3 us
  starting transfers between devices: 0.17 us -> 29.3 us
  other arithmetic: 25.9 us -> 0.99 us
  between operations: 14.9 us -> 0.25 us
  blocking collectives: 20.5 us -> 9.64 us
    all_gather x4 -> x0, waiting for transfers between devices: 139 us -> none  [the longest x1 75.7 us: shards(): lax.all_gather(k_two, 'frame', axis=0, tiled=True)]
    dot_general x13 -> x0, matrix products: 54.7 us -> none  [the longest x3 22.8 us: soft_step(): jnp.einsum(value_form, weights.astype(jnp.bfloat16), vals, preferred_elem...]
    ppermute x0 -> x19, waiting for transfers between devices: none -> 48.9 us  [the longest x16 48.9 us: swap(): return lax.ppermute(value, axis, [(i, i ^ mask) for i in range(size)])]
    all_gather x6 -> x0, local copies, waits for them, and re-layouts: 39.8 us -> none  [the longest x1 13.8 us: shards(): lax.all_gather(v_one, 'pos', axis=1, tiled=True)]
    pallas_call x0 -> x3, Pallas kernels: none -> 30.3 us  [the longest x1 18.6 us: spatial(): pl.pallas_call(functools.partial(spatial_kernel, chips, shards), grid_spe...]
    ppermute x0 -> x19, starting transfers between devices: none -> 29.3 us  [the longest x16 22.1 us: swap(): return lax.ppermute(value, axis, [(i, i ^ mask) for i in range(size)])]
    psum x1 -> x0, waiting for transfers between devices: 28 us -> none  [broadcast(): return lax.psum(kept, axis)]
    reduce_sum x4 -> x0, other arithmetic: 15 us -> none  [the longest x3 13.3 us: soft_step(): totals = totals * keep + jnp.sum(weights, axis=-1)]
  transfers between devices with their start and end apart: 5 -> 19, of which waited for: 3 -> 8; matrix products, arithmetic and copies ran while one was open for 25% -> 1% of each run, Pallas kernels for 0% -> 0%
where the time goes in v1:
time: 125 us; the launch traced here: 124 us
  waiting for transfers between devices  48.9 us (39%)
  Pallas kernels  30.3 us (24%)
  starting transfers between devices  29.3 us (23%)
  blocking collectives  9.64 us (8%)
  local copies, waits for them, and re-layouts  4.91 us (4%)
    ppermute x16, waiting for transfers between devices, swap(): return lax.ppermute(value, axis, [(i, i ^ mask) for i in range(size)])  48.9 us
    ppermute x16, starting transfers between devices, swap(): return lax.ppermute(value, axis, [(i, i ^ mask) for i in range(size)])  22.1 us
    pallas_call x1, Pallas kernels, spatial(): pl.pallas_call(functools.partial(spatial_kernel, chips, shards), grid_spe...  18.6 us
    all_gather x1, blocking collectives, shards_fn(): x0 = lax.all_gather(found, 'pos', axis=0, tiled=True)  9.64 us
    pallas_call x1, Pallas kernels, temporal(): pl.pallas_call(functools.partial(temporal_kernel, chips, shards, share),...  7.66 us
    ppermute x3, starting transfers between devices, shards_fn(): sent = lax.ppermute(first, 'frame', [(0, s)])  7.22 us
    pallas_call x1, Pallas kernels, assemble(): pl.pallas_call(functools.partial(assemble_kernel, shards, share), grid_sp...  4.11 us
    unnamed x30, local copies, waits for them, and re-layouts  2.79 us
  transfers between devices with their start and end apart: 19, of which 8 were waited for; matrix products, arithmetic and copies ran while one was open for 1% of the time, Pallas kernels for 0%

profile of v1, /device:TPU:0, one launch (start us, length us, event | category | flops | bytes accessed | tf_op | source)
XLA Modules:
  0.0 124.3 jit_solution(4474129769550383261)
XLA Ops:
  0.0 1.3 %constant_dynamic-slice_fusion = (bf16[8,64,256]{2,1,0:T(8,128)(2,1)S(1)}, bf16[8,64,256]{2,1,0:T(8,128)(2,1)S(1)}, bf16[8,64,256]{2,1,0:T(8,128)(2,1)S(1)}, bf16[8,64,256]{2,1,0:T(8,128)(2,1)S(1)}) fusion(bf16[32,64,256]{2,1,0:T(8,128)(2,1)} %param.11, s32[]{:T(128)S(6)} %select_n.41, s32[]{:T(128)S(6)} %select_n.40, s32[]{:T(128)S(6)} %select_n.39, ...), kind=kLoop, calls=%fused_computation.5 | loop fusion | bytes 2097168 | tf_op jit(solution)/shard_map/dynamic_slice | solution.py:268
  1.3 4.0 %collective-permute-start.2 = (bf16[8,64,256]{2,1,0:T(8,128)(2,1)S(1)}, bf16[8,64,256]{2,1,0:T(8,128)(2,1)S(1)}, u32[]{:S(2)}, u32[]{:S(2)}) collective-permute-start(bf16[8,64,256]{2,1,0:T(8,128)(2,1)S(1)} %get-tuple-element.21), channel_id=1, source_target_pairs={{0,6},{1,7},{2,4},{3,5},{4,2},{5,3},{6,0},{7,1},{8,14},{9,15},{10,... | collective-permute-start | bytes 786440 | tf_op jit(solution)/shard_map/ppermute | solution.py:235
  5.2 0.5 collective-permute-start.1
  5.7 0.1 collective-permute-start
  5.9 0.8 slice_bitcast_fusion
  6.7 3.9 %collective-permute-start.9 = (bf16[64,256]{1,0:T(8,128)(2,1)S(1)}, bf16[64,256]{1,0:T(8,128)(2,1)S(1)}, u32[]{:S(2)}, u32[]{:S(2)}) collective-permute-start(bf16[64,256]{1,0:T(8,128)(2,1)S(1)} %slice_bitcast_fusion), channel_id=1, source_target_pairs={{0,8},{1,9},{2,10},{3,11},{4,12},{5,13},{6,14},{7,15}} | collective-permute-start | bytes 98312 | tf_op jit(solution)/shard_map/ppermute | solution.py:264
  10.5 1.7 %collective-permute-start.8 = (bf16[64,256]{1,0:T(8,128)(2,1)S(1)}, bf16[64,256]{1,0:T(8,128)(2,1)S(1)}, u32[]{:S(2)}, u32[]{:S(2)}) collective-permute-start(bf16[64,256]{1,0:T(8,128)(2,1)S(1)} %slice_bitcast_fusion), channel_id=1, source_target_pairs={{0,16},{1,17},{2,18},{3,19},{4,20},{5,21},{6,22},{7,23}} | collective-permute-start | bytes 98312 | tf_op jit(solution)/shard_map/ppermute | solution.py:264
  12.2 0.0 collective-permute-done.9
  12.2 1.7 %collective-permute-start.7 = (bf16[64,256]{1,0:T(8,128)(2,1)S(1)}, bf16[64,256]{1,0:T(8,128)(2,1)S(1)}, u32[]{:S(2)}, u32[]{:S(2)}) collective-permute-start(bf16[64,256]{1,0:T(8,128)(2,1)S(1)} %slice_bitcast_fusion), channel_id=1, source_target_pairs={{0,24},{1,25},{2,26},{3,27},{4,28},{5,29},{6,30},{7,31}} | collective-permute-start | bytes 98312 | tf_op jit(solution)/shard_map/ppermute | solution.py:264
  13.9 0.1 pad_add_fusion.zf_ref.ids_ref
  14.0 0.0 collective-permute-done.8
  14.0 0.0 collective-permute-start.3
  14.0 0.0 collective-permute-done.2.refs_3_
  14.1 0.5 collective-permute-start.6
  14.5 2.6 %collective-permute-done.1.refs_2_ = bf16[8,64,256]{2,1,0:T(8,128)(2,1)S(1)} collective-permute-done((bf16[8,64,256]{2,1,0:T(8,128)(2,1)S(1)}, bf16[8,64,256]{2,1,0:T(8,128)(2,1)S(1)}, u32[]{:S(2)}, u32[]{:S(2)}) %collective-permute-start.1) | collective-permute-done | bytes 262176 | tf_op jit(solution)/shard_map/ppermute | solution.py:235
  17.1 0.0 collective-permute-start.5
  17.2 0.3 collective-permute-done.refs_1_
  17.4 0.2 collective-permute-start.4
  17.7 0.0 collective-permute-done.7
  17.7 0.8 select_select_fusion
  18.5 0.0 copy-start.2
  18.5 9.6 %all_gather.3.refs_8_ = bf16[512,256]{1,0:T(8,128)(2,1)S(1)} all-gather(bf16[64,256]{1,0:T(8,128)(2,1)S(1)} %select_select_fusion), channel_id=1, replica_groups=mesh['frame'=4,'pos'=8] {'pos'}, dimensions={0}, use_global_device_ids=true | all-gather | bytes 294912 | tf_op jit(solution)/shard_map/all_gather | solution.py:266
  28.1 0.0 collective-permute-done.3.refs_4_
  28.2 0.6 copy-done.10
  28.8 18.6 %spatial.1 = (bf16[4,8,16,256]{3,2,1,0:T(8,128)(2,1)S(1)}, bf16[4,8,16,256]{3,2,1,0:T(8,128)(2,1)S(1)}, bf16[4,8,16,256]{3,2,1,0:T(8,128)(2,1)S(1)}, bf16[4,8,16,256]{3,2,1,0:T(8,128)(2,1)S(1)}) custom-call(s32[2]{0:T(128)S(1)} %pad_add_fusion.zf_ref.ids_ref, bf16[8,64,256]{2,1,0:T(8,128)(2,1)S(1)} %get-tuple-element.24.refs_0_, ...), custom_call_target="tpu_custom_call" | custom-call | tf_op jit(solution)/shard_map/spatial/pallas_call | solution.py:102
  47.4 1.6 %collective-permute-start.10 = (bf16[4,8,16,256]{3,2,1,0:T(8,128)(2,1)S(1)}, bf16[4,8,16,256]{3,2,1,0:T(8,128)(2,1)S(1)}, u32[]{:S(2)}, u32[]{:S(2)}) collective-permute-start(bf16[4,8,16,256]{3,2,1,0:T(8,128)(2,1)S(1)} %get-tuple-element.14), channel_id=1, source_target_pairs={{0,8},{8,0},{16,24},{24,16},{1,9},{9,1},{17,25},{25,17},{2,10},{10... | collective-permute-start | bytes 786440 | tf_op jit(solution)/shard_map/ppermute | solution.py:235
  49.0 2.6 %collective-permute-start.11 = (bf16[4,8,16,256]{3,2,1,0:T(8,128)(2,1)S(1)}, bf16[4,8,16,256]{3,2,1,0:T(8,128)(2,1)S(1)}, u32[]{:S(2)}, u32[]{:S(2)}) collective-permute-start(bf16[4,8,16,256]{3,2,1,0:T(8,128)(2,1)S(1)} %get-tuple-element.15), channel_id=1, source_target_pairs={{0,16},{8,24},{16,0},{24,8},{1,17},{9,25},{17,1},{25,9},{2,18},{10... | collective-permute-start | bytes 786440 | tf_op jit(solution)/shard_map/ppermute | solution.py:235
  51.7 0.3 collective-permute-start.12
  51.9 9.2 %collective-permute-done.10 = bf16[4,8,16,256]{3,2,1,0:T(8,128)(2,1)S(1)} collective-permute-done((bf16[4,8,16,256]{3,2,1,0:T(8,128)(2,1)S(1)}, bf16[4,8,16,256]{3,2,1,0:T(8,128)(2,1)S(1)}, u32[]{:S(2)}, u32[]{:S(2)}) %collective-permute-start.10) | collective-permute-done | bytes 262176 | tf_op jit(solution)/shard_map/ppermute | solution.py:235
  61.2 9.2 %collective-permute-done.11 = bf16[4,8,16,256]{3,2,1,0:T(8,128)(2,1)S(1)} collective-permute-done((bf16[4,8,16,256]{3,2,1,0:T(8,128)(2,1)S(1)}, bf16[4,8,16,256]{3,2,1,0:T(8,128)(2,1)S(1)}, u32[]{:S(2)}, u32[]{:S(2)}) %collective-permute-start.11) | collective-permute-done | bytes 262176 | tf_op jit(solution)/shard_map/ppermute | solution.py:235
  70.4 0.0 collective-permute-done.12
  70.5 0.9 collective-permute-start.13
  71.4 1.3 %collective-permute-start.14 = (bf16[4,128,256]{2,1,0:T(8,128)(2,1)S(1)}, bf16[4,128,256]{2,1,0:T(8,128)(2,1)S(1)}, u32[]{:S(2)}, u32[]{:S(2)}) collective-permute-start(bf16[4,128,256]{2,1,0:T(8,128)(2,1)S(1)} %pad_maximum_fusion.1), channel_id=1, source_target_pairs={{0,4},{1,5},{2,6},{3,7},{4,0},{5,1},{6,2},{7,3},{8,12},{9,13},{10,... | collective-permute-start | bytes 786440 | tf_op jit(solution)/shard_map/ppermute | solution.py:235
  72.7 1.5 %collective-permute-start.15 = (bf16[4,128,256]{2,1,0:T(8,128)(2,1)S(1)}, bf16[4,128,256]{2,1,0:T(8,128)(2,1)S(1)}, u32[]{:S(2)}, u32[]{:S(2)}) collective-permute-start(bf16[4,128,256]{2,1,0:T(8,128)(2,1)S(1)} %pad_maximum_fusion.2), channel_id=1, source_target_pairs={{0,6},{1,7},{2,4},{3,5},{4,2},{5,3},{6,0},{7,1},{8,14},{9,15},{10,... | collective-permute-start | bytes 786440 | tf_op jit(solution)/shard_map/ppermute | solution.py:235
  74.3 5.5 %collective-permute-done.13.refs_4_ = bf16[4,128,256]{2,1,0:T(8,128)(2,1)S(1)} collective-permute-done((bf16[4,128,256]{2,1,0:T(8,128)(2,1)S(1)}, bf16[4,128,256]{2,1,0:T(8,128)(2,1)S(1)}, u32[]{:S(2)}, u32[]{:S(2)}) %collective-permute-start.13) | collective-permute-done | bytes 262176 | tf_op jit(solution)/shard_map/ppermute | solution.py:235
  79.8 3.6 %collective-permute-done.14.refs_5_ = bf16[4,128,256]{2,1,0:T(8,128)(2,1)S(1)} collective-permute-done((bf16[4,128,256]{2,1,0:T(8,128)(2,1)S(1)}, bf16[4,128,256]{2,1,0:T(8,128)(2,1)S(1)}, u32[]{:S(2)}, u32[]{:S(2)}) %collective-permute-start.14) | collective-permute-done | bytes 262176 | tf_op jit(solution)/shard_map/ppermute | solution.py:235
  83.4 0.0 collective-permute-done.15.refs_6_
  83.5 0.6 copy-done.11
  84.1 7.7 %temporal.1 = (bf16[4,128,256]{2,1,0:T(8,128)(2,1)S(1)}, bf16[4,128,256]{2,1,0:T(8,128)(2,1)S(1)}, bf16[4,128,256]{2,1,0:T(8,128)(2,1)S(1)}, bf16[4,128,256]{2,1,0:T(8,128)(2,1)S(1)}) custom-call(bf16[128,256]{1,0:T(8,128)(2,1)S(1)} %bitcast.29, bf16[128,256]{1,0:T(8,128)(2,1)S(1)} %bitcast.30, bf16[128,256]{1,0:T(8,128)(2,1)S(1)} %bitcast.31, ...), custom_call_target="tpu_custom_call" | custom-call | tf_op jit(solution)/shard_map/temporal/pallas_call | solution.py:192
  91.8 0.7 copy-done
  92.5 6.0 %collective-permute-start.16 = (bf16[4,128,256]{2,1,0:T(8,128)(2,1)S(1)}, bf16[4,128,256]{2,1,0:T(8,128)(2,1)S(1)}, u32[]{:S(2)}, u32[]{:S(2)}) collective-permute-start(bf16[4,128,256]{2,1,0:T(8,128)(2,1)S(1)} %get-tuple-element.18), channel_id=1, source_target_pairs={{0,8},{8,0},{16,24},{24,16},{1,9},{9,1},{17,25},{25,17},{2,10},{10... | collective-permute-start | bytes 786440 | tf_op jit(solution)/shard_map/ppermute | solution.py:235
  98.5 1.0 collective-permute-start.17
  99.6 1.5 %collective-permute-start.18 = (bf16[4,128,256]{2,1,0:T(8,128)(2,1)S(1)}, bf16[4,128,256]{2,1,0:T(8,128)(2,1)S(1)}, u32[]{:S(2)}, u32[]{:S(2)}) collective-permute-start(bf16[4,128,256]{2,1,0:T(8,128)(2,1)S(1)} %get-tuple-element.20), channel_id=1, source_target_pairs={{0,24},{8,16},{16,8},{24,0},{1,25},{9,17},{17,9},{25,1},{2,26},{10... | collective-permute-start | bytes 786440 | tf_op jit(solution)/shard_map/ppermute | solution.py:235
  101.0 5.6 %collective-permute-done.16 = bf16[4,128,256]{2,1,0:T(8,128)(2,1)S(1)} collective-permute-done((bf16[4,128,256]{2,1,0:T(8,128)(2,1)S(1)}, bf16[4,128,256]{2,1,0:T(8,128)(2,1)S(1)}, u32[]{:S(2)}, u32[]{:S(2)}) %collective-permute-start.16) | collective-permute-done | bytes 262176 | tf_op jit(solution)/shard_map/ppermute | solution.py:235
  106.7 12.8 %collective-permute-done.17 = bf16[4,128,256]{2,1,0:T(8,128)(2,1)S(1)} collective-permute-done((bf16[4,128,256]{2,1,0:T(8,128)(2,1)S(1)}, bf16[4,128,256]{2,1,0:T(8,128)(2,1)S(1)}, u32[]{:S(2)}, u32[]{:S(2)}) %collective-permute-start.17) | collective-permute-done | bytes 262176 | tf_op jit(solution)/shard_map/ppermute | solution.py:235
  119.4 0.7 copy-done.13
  120.1 0.1 copy-done.14
  120.2 4.1 %assemble.1 = bf16[32,64,256]{2,1,0:T(8,128)(2,1)} custom-call(s32[2]{0:T(128)} %copy-done.9, bf16[4,8,16,256]{3,2,1,0:T(8,128)(2,1)} %bitcast.28, bf16[4,8,16,256]{3,2,1,0:T(8,128)(2,1)} %bitcast.35, bf16[4,8,16,256]{3,2,1,0:T(8,128)(2,1)} %bitcast.36, bf16[4,8,16,256]{3,2,1,0:T(8,128)(2,1)} %bitcast.37), custom_call_target="tpu_custom_call" | custom-call | tf_op jit(solution)/shard_map/assemble/pallas_call | solution.py:218
  (35 shorter events, 0.2 us)
Async XLA Ops:
  1.3 12.8 %collective-permute-start.2 = (bf16[8,64,256]{2,1,0:T(8,128)(2,1)S(1)}, bf16[8,64,256]{2,1,0:T(8,128)(2,1)S(1)}, u32[]{:S(2)}, u32[]{:S(2)}) collective-permute-start(bf16[8,64,256]{2,1,0:T(8,128)(2,1)S(1)} %get-tuple-element.21), channel_id=1, source_target_pairs={{0,6},{1,7},{2,4},{3,5},{4,2},{5,3},{6,0},{7,1},{8,14},{9,15},{10,... | collective-permute-start | bytes 786440 | tf_op jit(solution)/shard_map/ppermute | solution.py:235
  5.2 11.9 %collective-permute-start.1 = (bf16[8,64,256]{2,1,0:T(8,128)(2,1)S(1)}, bf16[8,64,256]{2,1,0:T(8,128)(2,1)S(1)}, u32[]{:S(2)}, u32[]{:S(2)}) collective-permute-start(bf16[8,64,256]{2,1,0:T(8,128)(2,1)S(1)} %get-tuple-element.22), channel_id=1, source_target_pairs={{0,4},{1,5},{2,6},{3,7},{4,0},{5,1},{6,2},{7,3},{8,12},{9,13},{10,... | collective-permute-start | bytes 786440 | tf_op jit(solution)/shard_map/ppermute | solution.py:235
  5.7 11.7 %collective-permute-start = (bf16[8,64,256]{2,1,0:T(8,128)(2,1)S(1)}, bf16[8,64,256]{2,1,0:T(8,128)(2,1)S(1)}, u32[]{:S(2)}, u32[]{:S(2)}) collective-permute-start(bf16[8,64,256]{2,1,0:T(8,128)(2,1)S(1)} %get-tuple-element.23), channel_id=1, source_target_pairs={{0,2},{1,3},{2,0},{3,1},{4,6},{5,7},{6,4},{7,5},{8,10},{9,11},{10,... | collective-permute-start | bytes 786440 | tf_op jit(solution)/shard_map/ppermute | solution.py:235
  5.9 22.3 %copy-start.4 = (bf16[256,256]{1,0:T(8,128)(2,1)S(1)}, bf16[256,256]{1,0:T(8,128)(2,1)}, u32[]{:S(2)}) copy-start(bf16[256,256]{1,0:T(8,128)(2,1)} %refs_13_.1) | copy-start | bytes 393220
  6.7 5.6 %collective-permute-start.9 = (bf16[64,256]{1,0:T(8,128)(2,1)S(1)}, bf16[64,256]{1,0:T(8,128)(2,1)S(1)}, u32[]{:S(2)}, u32[]{:S(2)}) collective-permute-start(bf16[64,256]{1,0:T(8,128)(2,1)S(1)} %slice_bitcast_fusion), channel_id=1, source_target_pairs={{0,8},{1,9},{2,10},{3,11},{4,12},{5,13},{6,14},{7,15}} | collective-permute-start | bytes 98312 | tf_op jit(solution)/shard_map/ppermute | solution.py:264
  10.5 3.5 %collective-permute-start.8 = (bf16[64,256]{1,0:T(8,128)(2,1)S(1)}, bf16[64,256]{1,0:T(8,128)(2,1)S(1)}, u32[]{:S(2)}, u32[]{:S(2)}) collective-permute-start(bf16[64,256]{1,0:T(8,128)(2,1)S(1)} %slice_bitcast_fusion), channel_id=1, source_target_pairs={{0,16},{1,17},{2,18},{3,19},{4,20},{5,21},{6,22},{7,23}} | collective-permute-start | bytes 98312 | tf_op jit(solution)/shard_map/ppermute | solution.py:264
  12.2 5.4 %collective-permute-start.7 = (bf16[64,256]{1,0:T(8,128)(2,1)S(1)}, bf16[64,256]{1,0:T(8,128)(2,1)S(1)}, u32[]{:S(2)}, u32[]{:S(2)}) collective-permute-start(bf16[64,256]{1,0:T(8,128)(2,1)S(1)} %slice_bitcast_fusion), channel_id=1, source_target_pairs={{0,24},{1,25},{2,26},{3,27},{4,28},{5,29},{6,30},{7,31}} | collective-permute-start | bytes 98312 | tf_op jit(solution)/shard_map/ppermute | solution.py:264
  14.0 14.2 %copy-start.9 = (s32[2]{0:T(128)}, s32[2]{0:T(128)S(1)}, u32[]{:S(2)}) copy-start(s32[2]{0:T(128)S(1)} %pad_add_fusion.zf_ref.ids_ref) | copy-start | bytes 28
  14.0 14.1 %collective-permute-start.3 = (bf16[8,64,256]{2,1,0:T(8,128)(2,1)S(1)}, bf16[8,64,256]{2,1,0:T(8,128)(2,1)S(1)}, u32[]{:S(2)}, u32[]{:S(2)}) collective-permute-start(bf16[8,64,256]{2,1,0:T(8,128)(2,1)S(1)} %get-tuple-element.24.refs_0_), channel_id=1, source_target_pairs={{0,1},{1,0},{2,3},{3,2},{4,5},{5,4},{6,7},{7,6},{8,9},{9,8},{10,11... | collective-permute-start | bytes 786440 | tf_op jit(solution)/shard_map/ppermute | solution.py:235
  14.1 14.1 %collective-permute-start.6 = (bf16[8,64,256]{2,1,0:T(8,128)(2,1)S(1)}, bf16[8,64,256]{2,1,0:T(8,128)(2,1)S(1)}, u32[]{:S(2)}, u32[]{:S(2)}) collective-permute-start(bf16[8,64,256]{2,1,0:T(8,128)(2,1)S(1)} %collective-permute-done.2.refs_3_), channel_id=1, source_target_pairs={{0,1},{1,0},{2,3},{3,2},{4,5},{5,4},{6,7},{7,6},{8,9},{9,8},{10,11... | collective-permute-start | bytes 786440 | tf_op jit(solution)/shard_map/ppermute | solution.py:235
  17.1 11.0 %collective-permute-start.5 = (bf16[8,64,256]{2,1,0:T(8,128)(2,1)S(1)}, bf16[8,64,256]{2,1,0:T(8,128)(2,1)S(1)}, u32[]{:S(2)}, u32[]{:S(2)}) collective-permute-start(bf16[8,64,256]{2,1,0:T(8,128)(2,1)S(1)} %collective-permute-done.1.refs_2_), channel_id=1, source_target_pairs={{0,1},{1,0},{2,3},{3,2},{4,5},{5,4},{6,7},{7,6},{8,9},{9,8},{10,11... | collective-permute-start | bytes 786440 | tf_op jit(solution)/shard_map/ppermute | solution.py:235
  17.4 10.7 %collective-permute-start.4 = (bf16[8,64,256]{2,1,0:T(8,128)(2,1)S(1)}, bf16[8,64,256]{2,1,0:T(8,128)(2,1)S(1)}, u32[]{:S(2)}, u32[]{:S(2)}) collective-permute-start(bf16[8,64,256]{2,1,0:T(8,128)(2,1)S(1)} %collective-permute-done.refs_1_), channel_id=1, source_target_pairs={{0,1},{1,0},{2,3},{3,2},{4,5},{5,4},{6,7},{7,6},{8,9},{9,8},{10,11... | collective-permute-start | bytes 786440 | tf_op jit(solution)/shard_map/ppermute | solution.py:235
  17.7 10.5 %copy-start.3 = (bf16[256,256]{1,0:T(8,128)(2,1)S(1)}, bf16[256,256]{1,0:T(8,128)(2,1)}, u32[]{:S(2)}) copy-start(bf16[256,256]{1,0:T(8,128)(2,1)} %refs_12_.1) | copy-start | bytes 393220
  18.5 9.7 %copy-start.1 = (bf16[256,256]{1,0:T(8,128)(2,1)S(1)}, bf16[256,256]{1,0:T(8,128)(2,1)}, u32[]{:S(2)}) copy-start(bf16[256,256]{1,0:T(8,128)(2,1)} %refs_10_.2) | copy-start | bytes 393220
  18.5 9.7 %copy-start.2 = (bf16[256,256]{1,0:T(8,128)(2,1)S(1)}, bf16[256,256]{1,0:T(8,128)(2,1)}, u32[]{:S(2)}) copy-start(bf16[256,256]{1,0:T(8,128)(2,1)} %refs_11_.2) | copy-start | bytes 393220
  28.1 0.7 copy-start.10
  47.4 13.7 %collective-permute-start.10 = (bf16[4,8,16,256]{3,2,1,0:T(8,128)(2,1)S(1)}, bf16[4,8,16,256]{3,2,1,0:T(8,128)(2,1)S(1)}, u32[]{:S(2)}, u32[]{:S(2)}) collective-permute-start(bf16[4,8,16,256]{3,2,1,0:T(8,128)(2,1)S(1)} %get-tuple-element.14), channel_id=1, source_target_pairs={{0,8},{8,0},{16,24},{24,16},{1,9},{9,1},{17,25},{25,17},{2,10},{10... | collective-permute-start | bytes 786440 | tf_op jit(solution)/shard_map/ppermute | solution.py:235
  49.0 21.3 %collective-permute-start.11 = (bf16[4,8,16,256]{3,2,1,0:T(8,128)(2,1)S(1)}, bf16[4,8,16,256]{3,2,1,0:T(8,128)(2,1)S(1)}, u32[]{:S(2)}, u32[]{:S(2)}) collective-permute-start(bf16[4,8,16,256]{3,2,1,0:T(8,128)(2,1)S(1)} %get-tuple-element.15), channel_id=1, source_target_pairs={{0,16},{8,24},{16,0},{24,8},{1,17},{9,25},{17,1},{25,9},{2,18},{10... | collective-permute-start | bytes 786440 | tf_op jit(solution)/shard_map/ppermute | solution.py:235
  51.7 18.7 %collective-permute-start.12 = (bf16[4,8,16,256]{3,2,1,0:T(8,128)(2,1)S(1)}, bf16[4,8,16,256]{3,2,1,0:T(8,128)(2,1)S(1)}, u32[]{:S(2)}, u32[]{:S(2)}) collective-permute-start(bf16[4,8,16,256]{3,2,1,0:T(8,128)(2,1)S(1)} %get-tuple-element.16), channel_id=1, source_target_pairs={{0,24},{8,16},{16,8},{24,0},{1,25},{9,17},{17,9},{25,1},{2,26},{10... | collective-permute-start | bytes 786440 | tf_op jit(solution)/shard_map/ppermute | solution.py:235
  70.5 9.3 %collective-permute-start.13 = (bf16[4,128,256]{2,1,0:T(8,128)(2,1)S(1)}, bf16[4,128,256]{2,1,0:T(8,128)(2,1)S(1)}, u32[]{:S(2)}, u32[]{:S(2)}) collective-permute-start(bf16[4,128,256]{2,1,0:T(8,128)(2,1)S(1)} %pad_maximum_fusion), channel_id=1, source_target_pairs={{0,2},{1,3},{2,0},{3,1},{4,6},{5,7},{6,4},{7,5},{8,10},{9,11},{10,... | collective-permute-start | bytes 786440 | tf_op jit(solution)/shard_map/ppermute | solution.py:235
  71.4 12.1 %collective-permute-start.14 = (bf16[4,128,256]{2,1,0:T(8,128)(2,1)S(1)}, bf16[4,128,256]{2,1,0:T(8,128)(2,1)S(1)}, u32[]{:S(2)}, u32[]{:S(2)}) collective-permute-start(bf16[4,128,256]{2,1,0:T(8,128)(2,1)S(1)} %pad_maximum_fusion.1), channel_id=1, source_target_pairs={{0,4},{1,5},{2,6},{3,7},{4,0},{5,1},{6,2},{7,3},{8,12},{9,13},{10,... | collective-permute-start | bytes 786440 | tf_op jit(solution)/shard_map/ppermute | solution.py:235
  72.7 10.8 %copy-start.5 = (bf16[256,256]{1,0:T(8,128)(2,1)S(1)}, bf16[256,256]{1,0:T(8,128)(2,1)}, u32[]{:S(2)}) copy-start(bf16[256,256]{1,0:T(8,128)(2,1)} %refs_8_.1) | copy-start | bytes 393220
  72.7 10.8 %copy-start.6 = (bf16[256,256]{1,0:T(8,128)(2,1)S(1)}, bf16[256,256]{1,0:T(8,128)(2,1)}, u32[]{:S(2)}) copy-start(bf16[256,256]{1,0:T(8,128)(2,1)} %refs_9_.1) | copy-start | bytes 393220
  72.7 10.8 %copy-start.7 = (bf16[256,256]{1,0:T(8,128)(2,1)S(1)}, bf16[256,256]{1,0:T(8,128)(2,1)}, u32[]{:S(2)}) copy-start(bf16[256,256]{1,0:T(8,128)(2,1)} %refs_10_.3) | copy-start | bytes 393220
  72.7 10.8 %copy-start.8 = (bf16[256,256]{1,0:T(8,128)(2,1)S(1)}, bf16[256,256]{1,0:T(8,128)(2,1)}, u32[]{:S(2)}) copy-start(bf16[256,256]{1,0:T(8,128)(2,1)} %refs_11_.3) | copy-start | bytes 393220
  72.7 10.7 %collective-permute-start.15 = (bf16[4,128,256]{2,1,0:T(8,128)(2,1)S(1)}, bf16[4,128,256]{2,1,0:T(8,128)(2,1)S(1)}, u32[]{:S(2)}, u32[]{:S(2)}) collective-permute-start(bf16[4,128,256]{2,1,0:T(8,128)(2,1)S(1)} %pad_maximum_fusion.2), channel_id=1, source_target_pairs={{0,6},{1,7},{2,4},{3,5},{4,2},{5,3},{6,0},{7,1},{8,14},{9,15},{10,... | collective-permute-start | bytes 786440 | tf_op jit(solution)/shard_map/ppermute | solution.py:235
  83.4 0.7 copy-start.11
  91.8 0.7 copy-start
  92.5 14.2 %collective-permute-start.16 = (bf16[4,128,256]{2,1,0:T(8,128)(2,1)S(1)}, bf16[4,128,256]{2,1,0:T(8,128)(2,1)S(1)}, u32[]{:S(2)}, u32[]{:S(2)}) collective-permute-start(bf16[4,128,256]{2,1,0:T(8,128)(2,1)S(1)} %get-tuple-element.18), channel_id=1, source_target_pairs={{0,8},{8,0},{16,24},{24,16},{1,9},{9,1},{17,25},{25,17},{2,10},{10... | collective-permute-start | bytes 786440 | tf_op jit(solution)/shard_map/ppermute | solution.py:235
  98.5 20.9 %collective-permute-start.17 = (bf16[4,128,256]{2,1,0:T(8,128)(2,1)S(1)}, bf16[4,128,256]{2,1,0:T(8,128)(2,1)S(1)}, u32[]{:S(2)}, u32[]{:S(2)}) collective-permute-start(bf16[4,128,256]{2,1,0:T(8,128)(2,1)S(1)} %get-tuple-element.19), channel_id=1, source_target_pairs={{0,16},{8,24},{16,0},{24,8},{1,17},{9,25},{17,1},{25,9},{2,18},{10... | collective-permute-start | bytes 786440 | tf_op jit(solution)/shard_map/ppermute | solution.py:235
  99.6 19.9 %collective-permute-start.18 = (bf16[4,128,256]{2,1,0:T(8,128)(2,1)S(1)}, bf16[4,128,256]{2,1,0:T(8,128)(2,1)S(1)}, u32[]{:S(2)}, u32[]{:S(2)}) collective-permute-start(bf16[4,128,256]{2,1,0:T(8,128)(2,1)S(1)} %get-tuple-element.20), channel_id=1, source_target_pairs={{0,24},{8,16},{16,8},{24,0},{1,25},{9,17},{17,9},{25,1},{2,26},{10... | collective-permute-start | bytes 786440 | tf_op jit(solution)/shard_map/ppermute | solution.py:235
  106.7 12.8 %copy-start.12 = (bf16[4,128,256]{2,1,0:T(8,128)(2,1)}, bf16[4,128,256]{2,1,0:T(8,128)(2,1)S(1)}, u32[]{:S(2)}) copy-start(bf16[4,128,256]{2,1,0:T(8,128)(2,1)S(1)} %collective-permute-done.16) | copy-start | bytes 786436
  119.4 0.7 copy-start.13
  119.4 0.8 copy-start.14

commit v2 on v1

v2 whole, which is shorter than its diff:
```python
import functools

import jax
import jax.numpy as jnp
from jax import lax
from jax.experimental import pallas as pl
from jax.experimental.pallas import tpu as pltpu
from jax.sharding import PartitionSpec as P

HEADS = 4
LANES = 128
EARLY = 40
SPLIT = 8
LATER = 6.4
ROOM = 26 * 2**20
TURNS = 2
LOG2E = 1.4426950408889634


def normed(wide, gain):
    factor = lax.rsqrt(jnp.mean(wide * wide, axis=-1, keepdims=True) + 1e-06)
    return wide * factor * gain


def dot(left, right):
    return jnp.dot(left, right, preferred_element_type=jnp.float32)


def dot_t(left, right):
    return lax.dot_general(
        left, right, (((1,), (1,)), ((), ())), preferred_element_type=jnp.float32
    )


def project(mine, other, gain_ref, wq_ref, wk_ref, wv_ref, q_ref, k_ref, v_ref, turns):
    chips = len(mine)
    local, width = mine[0].shape[1:]
    asked, frames = q_ref.shape[0], k_ref.shape[0]
    gain = gain_ref[...]
    rows = [r[:frames] for r in mine] + [other[s] for s in range(chips)]
    normal = [normed(r.reshape(frames * local, width).astype(jnp.float32), gain) for r in rows]
    short = [n.astype(jnp.bfloat16) for n in normal]
    for weight, out in ((wk_ref, k_ref), (wv_ref, v_ref)):
        for s in range(2 * chips):
            got = dot(short[s], weight[...]).astype(jnp.bfloat16)
            out[:, s * local : (s + 1) * local, :] = got.reshape(frames, local, width)
    scale = (width // HEADS) ** -0.5 * LOG2E
    wide = [n.reshape(frames, local, width) for n in normal[:chips]]
    for f in range(asked):
        n = jnp.concatenate([w[f] for w in wide], axis=0)
        n = jnp.concatenate([pick(n, chips, turns, j) for j in range(turns)], axis=0)
        q_ref[f] = (dot(n.astype(jnp.bfloat16), wq_ref[...]) * scale).astype(jnp.bfloat16)


def pick(rows, chips, turns, turn):
    local = rows.shape[0] // chips
    run = local // turns
    return jnp.concatenate(
        [rows[s * local + turn * run : s * local + (turn + 1) * run] for s in range(chips)], axis=0
    )


def attend(turns, turn, zf, parts, wo_ref, outs, mid_s, by_shard):
    chips = len(parts[0][0])
    shards = len(outs) * outs[0].shape[0] // chips
    step, width = outs[0].shape[2:]
    half = width // 2
    depth = width // HEADS
    rows = chips * shards * step
    k0, v0 = parts[-1][2], parts[-1][3]
    last = k0.shape[0] - 1
    places = k0.shape[1]
    low = lax.broadcasted_iota(jnp.int32, (rows, half), 1) < depth
    ones = jnp.ones((2 * places, half), jnp.bfloat16)
    frames = [(part, f) for part in parts for f in range(part[1].shape[0])]
    together = max(1, min(len(frames), ROOM // (2 * (2 * rows) * (2 * places) * 6)))
    for start in range(0, len(frames), together):
        now = frames[start : start + together]
        items = [(part, f, slice(p * half, (p + 1) * half)) for part, f in now for p in range(2)]
        scores = []
        for (_, q_ref, k_ref, _), f, cols in items:
            q = q_ref[f, turn * rows : (turn + 1) * rows, cols]
            zero = jnp.zeros_like(q)
            q = jnp.concatenate([jnp.where(low, q, zero), jnp.where(low, zero, q)], axis=0)
            scores.append(dot_t(q, jnp.concatenate([k_ref[f, :, cols], k0[last, :, cols]], axis=0)))
        weights = [
            jnp.exp2(s - jnp.max(s, axis=-1, keepdims=True)).astype(jnp.bfloat16) for s in scores
        ]
        sums = []
        for w, ((_, _, _, v_ref), f, cols) in zip(weights, items):
            vals = jnp.concatenate([v_ref[f, :, cols], v0[last, :, cols]], axis=0)
            r = dot(w, jnp.concatenate([vals, ones], axis=1))
            top = jnp.where(low, r[:rows, :half], r[rows:, :half])
            bottom = jnp.where(low, r[:rows, half:], r[rows:, half:])
            sums.append(top / bottom)
        for u, ((pieces, *_), f) in enumerate(now):
            a = jnp.concatenate(sums[2 * u : 2 * u + 2], axis=1).astype(jnp.bfloat16)
            x = jnp.concatenate([r[f].astype(jnp.float32) for r in pieces], axis=0)
            mid_s[start + u] = pick(x, chips, turns, turn) + dot(a, wo_ref[...])
    for f in range(len(frames)):
        for t in range(shards):
            for s in range(chips):
                at = pl.multiple_of((s * shards + (t ^ zf)) * step, step)
                piece = mid_s[f, pl.ds(at, step), :].astype(jnp.bfloat16)
                if by_shard:
                    outs[t][s, f] = piece
                else:
                    outs[s][t, f] = piece


def early_kernel(chips, turns, *refs):
    mine, (other, gain, wq, wk, wv, q, k, v) = refs[:chips], refs[chips:]
    project(mine, other, gain, wq, wk, wv, q, k, v, turns)


def first_kernel(chips, shards, turns, ids_ref, *refs):
    early, refs = refs[:chips], refs[chips:]
    late, refs = refs[:chips], refs[chips:]
    other, gain, wq, wk, wv, wo, q1, k1, v1 = refs[:9]
    outs, (q2, k2, v2, mid_s) = refs[9 : 9 + shards], refs[9 + shards :]
    project(late, other, gain, wq, wk, wv, q2, k2, v2, turns)
    attend(turns, 0, ids_ref[0], [(early, q1, k1, v1), (late, q2, k2, v2)], wo, outs, mid_s, True)


def later_kernel(chips, shards, turns, turn, ids_ref, *refs):
    early, refs = refs[:chips], refs[chips:]
    late, refs = refs[:chips], refs[chips:]
    q1, k1, v1, q2, k2, v2, wo = refs[:7]
    outs, mid_s = refs[7:-1], refs[-1]
    attend(turns, turn, ids_ref[0], [(early, q1, k1, v1), (late, q2, k2, v2)], wo, outs, mid_s, False)


def vmem(count):
    return [pl.BlockSpec(memory_space=pltpu.VMEM)] * count


def cost(microseconds):
    return pl.CostEstimate(
        flops=int(microseconds * 1e9), bytes_accessed=int(microseconds * 3.6e6), transcendentals=0
    )


def params():
    return pltpu.CompilerParams(vmem_limit_bytes=40 * 2**20)


def shape(*sizes):
    return jax.ShapeDtypeStruct(sizes, jnp.bfloat16)


def saved_shapes(frames, asked, local, chips, width):
    return [
        shape(asked, chips * local, width),
        shape(frames, 2 * chips * local, width),
        shape(frames, 2 * chips * local, width),
    ]


def spatial_early(mine, other, gain, wq, wk, wv, shards, turns):
    chips = len(mine)
    frames, local, width = other.shape[1:]
    args = (*mine, other, gain, wq, wk, wv)
    return pl.pallas_call(
        functools.partial(early_kernel, chips, turns),
        in_specs=vmem(len(args)),
        out_specs=vmem(3),
        out_shape=saved_shapes(frames, frames, local, chips, width),
        compiler_params=params(),
        cost_estimate=cost(EARLY),
        name="spatial_early",
    )(*args)


def spatial_first(ids, early, late, other, gain, wq, wk, wv, wo, saved, shards, turns):
    chips = len(early)
    local, width = early[0].shape[1:]
    frames, extra = saved[0].shape[0], late[0].shape[0]
    step = local // shards // turns
    total = frames + extra - 1
    args = (*early, *late, other, gain, wq, wk, wv, wo, *saved)
    out = [shape(chips, total, step, width)] * shards
    out = out + saved_shapes(extra, extra - 1, local, chips, width)
    got = pl.pallas_call(
        functools.partial(first_kernel, chips, shards, turns),
        in_specs=[pl.BlockSpec(memory_space=pltpu.SMEM)] + vmem(len(args)),
        out_specs=vmem(len(out)),
        out_shape=out,
        scratch_shapes=[pltpu.VMEM((total, chips * shards * step, width), jnp.float32)],
        compiler_params=params(),
        cost_estimate=cost(7.5),
        name="spatial_first",
    )(ids, *args)
    return got[:shards], got[shards:]


def spatial_later(ids, early, late, saved, wo, shards, turns, turn):
    chips = len(early)
    local, width = early[0].shape[1:]
    total = saved[0].shape[0] + saved[3].shape[0]
    step = local // shards // turns
    args = (*early, *late, *saved, wo)
    return pl.pallas_call(
        functools.partial(later_kernel, chips, shards, turns, turn),
        in_specs=[pl.BlockSpec(memory_space=pltpu.SMEM)] + vmem(len(args)),
        out_specs=vmem(chips),
        out_shape=[shape(shards, total, step, width)] * chips,
        scratch_shapes=[pltpu.VMEM((total, chips * shards * step, width), jnp.float32)],
        compiler_params=params(),
        cost_estimate=cost(LATER),
        name="spatial_later",
    )(ids, *args)


def take(ref, rows):
    return jnp.concatenate([ref[i, rows, :] for i in range(ref.shape[0])], axis=1)


def put(ref, rows, value):
    for i in range(ref.shape[0]):
        ref[i, rows, :] = value[:, i * LANES : (i + 1) * LANES]


def temporal_kernel(chips, shards, share, by_shard, *refs):
    near, far = (shards, chips) if by_shard else (chips, shards)
    own, refs = refs[:near], refs[near:]
    came, refs = refs[: far - 1], refs[far - 1 :]
    gain_ref, wq_ref, wk_ref, wv_ref, wo_ref = refs[:5]
    outs = refs[5 : 5 + shards]
    x_s, q_s, k_s, v_s, a_s = refs[5 + shards :]
    width = wq_ref.shape[0]
    depth = width // HEADS
    half = width // 2
    block = own[0].shape[0]
    frames = block // share * chips * shards
    for t in range(shards):
        for s in range(chips):
            i, j = (t, s) if by_shard else (s, t)
            piece = own[i][...] if j == 0 else came[j - 1][i]
            put(x_s, pl.ds((t * chips + s) * block, block), piece.astype(jnp.float32))
    gain = gain_ref[...]
    for p in range(share):
        n = normed(take(x_s, pl.ds(p, frames, stride=share)), gain).astype(jnp.bfloat16)
        q_s[p] = (dot(n, wq_ref[...]) * (depth**-0.5 * LOG2E)).astype(jnp.bfloat16)
        k_s[p] = dot(n, wk_ref[...]).astype(jnp.bfloat16)
        v_s[p] = dot(n, wv_ref[...]).astype(jnp.bfloat16)
    lane = lax.broadcasted_iota(jnp.int32, (frames, half), 1)
    low, high = lane < depth, lane >= depth
    ones = [c.astype(jnp.float32).astype(jnp.bfloat16) for c in (low, high)]

    zero = jnp.zeros((frames, half), jnp.bfloat16)
    items = [(p, slice(i * half, (i + 1) * half)) for p in range(share) for i in range(2)]
    scores = []
    for p, cols in items:
        k = k_s[p, :, cols]
        k = jnp.concatenate([jnp.where(low, k, zero), jnp.where(high, k, zero)], axis=0)
        scores.append(dot_t(q_s[p, :, cols], k))
    weights = []
    for s in scores:
        tops = [jnp.max(s[:, i * frames : (i + 1) * frames], axis=-1, keepdims=True) for i in range(2)]
        w = [jnp.exp2(s[:, i * frames : (i + 1) * frames] - tops[i]) for i in range(2)]
        weights.append(jnp.concatenate(w, axis=1).astype(jnp.bfloat16))
    parts = []
    for w, (p, cols) in zip(weights, items):
        v = v_s[p, :, cols]
        v = jnp.concatenate(
            [
                jnp.concatenate([jnp.where(low, v, zero), ones[0]], axis=1),
                jnp.concatenate([jnp.where(high, v, zero), ones[1]], axis=1),
            ],
            axis=0,
        )
        r = dot(w, v)
        parts.append(r[:, :half] / r[:, half:])
    for p in range(share):
        a = jnp.concatenate(parts[2 * p : 2 * p + 2], axis=1).astype(jnp.bfloat16)
        rows = pl.ds(p, frames, stride=share)
        put(a_s, rows, take(x_s, rows) + dot(a, wo_ref[...]))
    for t in range(shards):
        for s in range(chips):
            outs[t][s] = take(a_s, pl.ds((t * chips + s) * block, block)).astype(jnp.bfloat16)


def temporal(own, came, gain, wq, wk, wv, wo, share, by_shard):
    shards, chips = len(own), len(came) + 1
    if not by_shard:
        shards, chips = chips, shards
    block, width = own[0].shape
    rows = block * chips * shards
    frames = rows // share
    return pl.pallas_call(
        functools.partial(temporal_kernel, chips, shards, share, by_shard),
        out_shape=[jax.ShapeDtypeStruct((chips, block, width), jnp.bfloat16)] * shards,
        scratch_shapes=[
            pltpu.VMEM((width // LANES, rows, LANES), jnp.float32),
            pltpu.VMEM((share, frames, width), jnp.bfloat16),
            pltpu.VMEM((share, frames, width), jnp.bfloat16),
            pltpu.VMEM((share, frames, width), jnp.bfloat16),
            pltpu.VMEM((width // LANES, rows, LANES), jnp.float32),
        ],
        compiler_params=pltpu.CompilerParams(vmem_limit_bytes=48 * 2**20),
        cost_estimate=cost(1.9),
        name="temporal",
    )(*own, *came, gain, wq, wk, wv, wo)


def assemble_kernel(turn, ids_ref, *refs):
    shards = len(refs) - 4
    pieces, (_, out_ref, held, sem) = refs[:shards], refs[shards:]
    chips, frames, step, _ = pieces[0].shape
    run = shards * step
    for z in range(shards):

        @pl.when(ids_ref[0] == z)
        def _():
            for s in range(chips):
                got = [pieces[g ^ z][s].astype(jnp.float32) for g in range(shards)]
                held[pl.ds((s ^ ids_ref[1]) * frames, frames)] = jnp.concatenate(got, axis=1).astype(
                    jnp.bfloat16
                )

    copy = pltpu.make_async_copy(held, out_ref.at[:, pl.ds(turn * run, run), :], sem)
    copy.start()
    copy.wait()


def assemble(ids, pieces, whole, turn):
    shards = len(pieces)
    chips, frames, step, width = pieces[0].shape
    return pl.pallas_call(
        functools.partial(assemble_kernel, turn),
        in_specs=[pl.BlockSpec(memory_space=pltpu.SMEM)]
        + vmem(shards)
        + [pl.BlockSpec(memory_space=pl.ANY)],
        out_specs=pl.BlockSpec(memory_space=pl.ANY),
        out_shape=jax.ShapeDtypeStruct(whole.shape, whole.dtype),
        scratch_shapes=[
            pltpu.VMEM((chips * frames, shards * step, width), jnp.bfloat16),
            pltpu.SemaphoreType.DMA(()),
        ],
        input_output_aliases={shards + 1: 0},
        compiler_params=params(),
        cost_estimate=cost(60 if turn == 0 else 1),
        name="assemble",
    )(ids, *pieces, whole)


def blank(sizes):
    return pl.pallas_call(
        lambda out_ref: None,
        out_specs=pl.BlockSpec(memory_space=pl.ANY),
        out_shape=shape(*sizes),
        name="blank",
    )()


def swap(value, axis, size, mask):
    return lax.ppermute(value, axis, [(i, i ^ mask) for i in range(size)])


def shards_fn(
    shards,
    spots,
    latents,
    gain_one,
    query_one,
    key_one,
    value_one,
    out_one,
    gain_two,
    query_two,
    key_two,
    value_two,
    out_two,
):
    frames, local, width = latents.shape
    chips = spots // 2
    each = frames // chips
    share = local // shards
    turns = TURNS if share % (8 * TURNS) == 0 else 1
    zf = lax.axis_index("frame")
    chip = lax.axis_index("pos") // 2
    ids = jnp.stack([zf, chip]).astype(jnp.int32)
    row = lambda g: g.reshape(1, -1)

    over_shards = lambda v: [v[0]] + [swap(v[t], "frame", shards, t) for t in range(1, shards)]
    over_chips = lambda v: [v[0]] + [swap(v[s], "pos", spots, 2 * s) for s in range(1, chips)]
    half = max(1, each // SPLIT)
    cut = lambda s, part: lax.dynamic_slice_in_dim(
        latents, (chip ^ s) * each + part * half, each - half if part else half, 0
    )
    early = [jnp.concatenate([cut(s, 0), latents[:1]], axis=0) for s in range(chips)]
    early = over_chips(early)
    late = over_chips([cut(s, 1) for s in range(chips)])
    found = jnp.stack([e[half] for e in early])
    hop = shards // 2
    while hop:
        sent = lax.ppermute(found, "frame", [(i, i + hop) for i in range(0, shards, 2 * hop)])
        found = jnp.where(zf % (2 * hop) == hop, sent, found)
        hop //= 2
    early_other = swap(jnp.stack([e[:half] for e in early]), "pos", spots, 1)
    saved = spatial_early(
        early, early_other, row(gain_one), query_one, key_one, value_one, shards, turns
    )
    late = [jnp.concatenate([l, found[s : s + 1]], axis=0) for s, l in enumerate(late)]
    late_other = swap(jnp.stack(late), "pos", spots, 1)
    mid, rest = spatial_first(
        ids, early, late, late_other, row(gain_one), query_one, key_one, value_one, out_one, saved,
        shards, turns,
    )
    saved = (*saved, *rest)
    step = share // turns
    flat = lambda v: [m.reshape(m.shape[0], each * step, width) for m in v]
    heads = lambda v: [m[0] for m in v]
    across = lambda v, n: [None] + [jnp.stack([m[i] for m in v]) for i in range(1, n)]
    whole = blank(latents.shape)
    weights = (row(gain_two), query_two, key_two, value_two, out_two)
    for turn in range(turns):
        if turn == 0:
            got = over_shards(mid)
            gate = got[1:]
            got = flat(got)
            came = over_chips([None] + across(got, chips)[1:])
        else:
            mid = spatial_later(ids, early, late, saved, out_one, shards, turns, turn)
            mid, _ = lax.optimization_barrier((mid, gate[0]))
            got = flat(over_chips(mid))
            came = over_shards([None] + across(got, shards)[1:])
        if turn:
            came, done = lax.optimization_barrier((came[1:], done))
            came = [None] + list(came)
        done = temporal(heads(got), came[1:], *weights, step, turn == 0)
        back = over_shards(done)
        whole = assemble(ids, [d.reshape(chips, each, step, width) for d in back], whole, turn)
    return whole


def solution(mesh):
    return jax.shard_map(
        functools.partial(shards_fn, mesh.shape["frame"], mesh.shape["pos"]),
        mesh=mesh,
        in_specs=(P("frame", "pos", None), P(), P(), P(), P(), P(), P(), P(), P(), P(), P()),
        out_specs=P("frame", "pos", None),
        check_vma=False,
    )
```

time: 125 us -> 93.6 us (0.75)
  waiting for transfers between devices: 48.9 us -> 24.6 us
  starting transfers between devices: 29.3 us -> 44.8 us
  blocking collectives: 9.64 us -> 0 us
  Pallas kernels: 30.3 us -> 21.6 us
  local copies, waits for them, and re-layouts: 4.91 us -> 1.19 us
    ppermute x16 -> x26, waiting for transfers between devices: 48.9 us -> 22.3 us  [swap(): return lax.ppermute(value, axis, [(i, i ^ mask) for i in range(size)])]
    ppermute x16 -> x26, starting transfers between devices: 22.1 us -> 39 us  [swap(): return lax.ppermute(value, axis, [(i, i ^ mask) for i in range(size)])]
    all_gather x1 -> x0, blocking collectives: 9.64 us -> none  [shards_fn(): x0 = lax.all_gather(found, 'pos', axis=0, tiled=True)]
    pallas_call x3 -> x8, Pallas kernels: 30.3 us -> 21.6 us  [the longest x1 7.93 us: spatial_first(): pl.pallas_call(functools.partial(first_kernel, chips, shards, turns), in_...]
    unnamed x30 -> x22, local copies, waits for them, and re-layouts: 2.79 us -> 0.06 us
    ppermute x3 -> x2, waiting for transfers between devices: 0.01 us -> 2.32 us  [shards_fn(): lax.ppermute(found, 'frame', [(i, i + hop) for i in range(0, shards, 2 *...]
    ppermute x3 -> x2, starting transfers between devices: 7.22 us -> 5.8 us  [shards_fn(): lax.ppermute(found, 'frame', [(i, i + hop) for i in range(0, shards, 2 *...]
  transfers between devices with their start and end apart: 19 -> 28, of which waited for: 8 -> 11; matrix products, arithmetic and copies ran while one was open for 1% -> 1% of each run, Pallas kernels for 0% -> 13%
where the time goes in v2:
time: 93.6 us; the launch traced here: 93.4 us
  starting transfers between devices  44.8 us (48%)
  waiting for transfers between devices  24.6 us (26%)
  Pallas kernels  21.6 us (23%)
  local copies, waits for them, and re-layouts  1.19 us (1%)
    ppermute x26, starting transfers between devices, swap(): return lax.ppermute(value, axis, [(i, i ^ mask) for i in range(size)])  39 us
    ppermute x26, waiting for transfers between devices, swap(): return lax.ppermute(value, axis, [(i, i ^ mask) for i in range(size)])  22.3 us
    pallas_call x1, Pallas kernels, spatial_first(): pl.pallas_call(functools.partial(first_kernel, chips, shards, turns), in_...  7.93 us
    pallas_call x1, Pallas kernels, spatial_later(): pl.pallas_call(functools.partial(later_kernel, chips, shards, turns, turn...  6.41 us
    ppermute x2, starting transfers between devices, shards_fn(): lax.ppermute(found, 'frame', [(i, i + hop) for i in range(0, shards, 2 *...  5.8 us
    pallas_call x2, Pallas kernels, temporal(): pl.pallas_call(functools.partial(temporal_kernel, chips, shards, share, b...  3.8 us
    pallas_call x2, Pallas kernels, assemble(): pl.pallas_call(functools.partial(assemble_kernel, turn), in_specs=[pl.Blo...  2.82 us
    ppermute x2, waiting for transfers between devices, shards_fn(): lax.ppermute(found, 'frame', [(i, i + hop) for i in range(0, shards, 2 *...  2.32 us
  transfers between devices with their start and end apart: 28, of which 11 were waited for; matrix products, arithmetic and copies ran while one was open for 1% of the time, Pallas kernels for 13%

profile of v2, /device:TPU:0, one launch (start us, length us, event | category | flops | bytes accessed | tf_op | source)
XLA Modules:
  0.0 93.4 jit_solution(11702368729920862705)
XLA Ops:
  0.0 0.9 constant_dynamic-slice_fusion.4
  1.0 4.0 %collective-permute-start.2 = (bf16[2,64,256]{2,1,0:T(8,128)(2,1)S(1)}, bf16[2,64,256]{2,1,0:T(8,128)(2,1)S(1)}, u32[]{:S(2)}, u32[]{:S(2)}) collective-permute-start(bf16[2,64,256]{2,1,0:T(8,128)(2,1)S(1)} %get-tuple-element.122), channel_id=1, source_target_pairs={{0,6},{1,7},{2,4},{3,5},{4,2},{5,3},{6,0},{7,1},{8,14},{9,15},{10,... | collective-permute-start | bytes 196616 | tf_op jit(solution)/shard_map/ppermute | solution.py:357
  4.9 0.5 collective-permute-start
  5.5 0.1 collective-permute-start.1
  5.6 1.8 %collective-permute-done.2.refs_3_ = bf16[2,64,256]{2,1,0:T(8,128)(2,1)S(1)} collective-permute-done((bf16[2,64,256]{2,1,0:T(8,128)(2,1)S(1)}, bf16[2,64,256]{2,1,0:T(8,128)(2,1)S(1)}, u32[]{:S(2)}, u32[]{:S(2)}) %collective-permute-start.2) | collective-permute-done | bytes 65568 | tf_op jit(solution)/shard_map/ppermute | solution.py:357
  7.4 2.3 %collective-permute-done.1.refs_2_ = bf16[2,64,256]{2,1,0:T(8,128)(2,1)S(1)} collective-permute-done((bf16[2,64,256]{2,1,0:T(8,128)(2,1)S(1)}, bf16[2,64,256]{2,1,0:T(8,128)(2,1)S(1)}, u32[]{:S(2)}, u32[]{:S(2)}) %collective-permute-start.1) | collective-permute-done | bytes 65568 | tf_op jit(solution)/shard_map/ppermute | solution.py:357
  9.8 4.5 %collective-permute-start.3 = (bf16[4,64,256]{2,1,0:T(8,128)(2,1)S(1)}, bf16[4,64,256]{2,1,0:T(8,128)(2,1)S(1)}, u32[]{:S(2)}, u32[]{:S(2)}) collective-permute-start(bf16[4,64,256]{2,1,0:T(8,128)(2,1)S(1)} %pad_maximum_fusion.5), channel_id=1, source_target_pairs={{0,16},{1,17},{2,18},{3,19},{4,20},{5,21},{6,22},{7,23}} | collective-permute-start | bytes 393224 | tf_op jit(solution)/shard_map/ppermute | solution.py:397
  14.3 0.1 constant_dynamic-slice_fusion
  14.4 1.6 %collective-permute-start.5 = (bf16[7,64,256]{2,1,0:T(8,128)(2,1)S(1)}, bf16[7,64,256]{2,1,0:T(8,128)(2,1)S(1)}, u32[]{:S(2)}, u32[]{:S(2)}) collective-permute-start(bf16[7,64,256]{2,1,0:T(8,128)(2,1)S(1)} %get-tuple-element.64), channel_id=1, source_target_pairs={{0,2},{1,3},{2,0},{3,1},{4,6},{5,7},{6,4},{7,5},{8,10},{9,11},{10,... | collective-permute-start | bytes 688136 | tf_op jit(solution)/shard_map/ppermute | solution.py:357
  16.0 0.5 collective-permute-start.6
  16.5 1.5 %collective-permute-start.7 = (bf16[7,64,256]{2,1,0:T(8,128)(2,1)S(1)}, bf16[7,64,256]{2,1,0:T(8,128)(2,1)S(1)}, u32[]{:S(2)}, u32[]{:S(2)}) collective-permute-start(bf16[7,64,256]{2,1,0:T(8,128)(2,1)S(1)} %get-tuple-element.63), channel_id=1, source_target_pairs={{0,6},{1,7},{2,4},{3,5},{4,2},{5,3},{6,0},{7,1},{8,14},{9,15},{10,... | collective-permute-start | bytes 688136 | tf_op jit(solution)/shard_map/ppermute | solution.py:357
  18.0 1.3 %collective-permute-start.4 = (bf16[4,64,256]{2,1,0:T(8,128)(2,1)S(1)}, bf16[4,64,256]{2,1,0:T(8,128)(2,1)S(1)}, u32[]{:S(2)}, u32[]{:S(2)}) collective-permute-start(bf16[4,64,256]{2,1,0:T(8,128)(2,1)S(1)} %broadcast_select_fusion), channel_id=1, source_target_pairs={{0,8},{16,24},{1,9},{17,25},{2,10},{18,26},{3,11},{19,27},{4,12},{... | collective-permute-start | bytes 393224 | tf_op jit(solution)/shard_map/ppermute | solution.py:397
  19.3 0.1 pad_add_fusion.ids_ref
  19.4 0.1 collective-permute-start.8
  19.5 2.3 %collective-permute-done.4 = bf16[4,64,256]{2,1,0:T(8,128)(2,1)S(1)} collective-permute-done((bf16[4,64,256]{2,1,0:T(8,128)(2,1)S(1)}, bf16[4,64,256]{2,1,0:T(8,128)(2,1)S(1)}, u32[]{:S(2)}, u32[]{:S(2)}) %collective-permute-start.4) | collective-permute-done | bytes 131104 | tf_op jit(solution)/shard_map/ppermute | solution.py:397
  21.9 1.1 %collective-permute-done.5 = bf16[7,64,256]{2,1,0:T(8,128)(2,1)S(1)} collective-permute-done((bf16[7,64,256]{2,1,0:T(8,128)(2,1)S(1)}, bf16[7,64,256]{2,1,0:T(8,128)(2,1)S(1)}, u32[]{:S(2)}, u32[]{:S(2)}) %collective-permute-start.5) | collective-permute-done | bytes 229408 | tf_op jit(solution)/shard_map/ppermute | solution.py:357
  23.1 3.7 %collective-permute-done.6 = bf16[7,64,256]{2,1,0:T(8,128)(2,1)S(1)} collective-permute-done((bf16[7,64,256]{2,1,0:T(8,128)(2,1)S(1)}, bf16[7,64,256]{2,1,0:T(8,128)(2,1)S(1)}, u32[]{:S(2)}, u32[]{:S(2)}) %collective-permute-start.6) | collective-permute-done | bytes 229408 | tf_op jit(solution)/shard_map/ppermute | solution.py:357
  26.9 0.1 pad_maximum_fusion
  27.0 0.1 collective-permute-start.9
  27.1 0.6 spatial_early.1
  27.8 2.0 %collective-permute-done.9.refs_8_ = bf16[4,8,64,256]{3,2,1,0:T(8,128)(2,1)S(1)} collective-permute-done((bf16[4,8,64,256]{3,2,1,0:T(8,128)(2,1)S(1)}, bf16[4,8,64,256]{3,2,1,0:T(8,128)(2,1)S(1)}, u32[]{:S(2)}, u32[]{:S(2)}) %collective-permute-start.9) | collective-permute-done | bytes 1048608 | tf_op jit(solution)/shard_map/ppermute | solution.py:357
  29.7 7.9 %spatial_first.1 = (bf16[4,8,8,256]{3,2,1,0:T(8,128)(2,1)S(1)}, bf16[4,8,8,256]{3,2,1,0:T(8,128)(2,1)S(1)}, bf16[4,8,8,256]{3,2,1,0:T(8,128)(2,1)S(1)}, bf16[4,8...) custom-call(s32[2]{0:T(128)S(1)} %pad_add_fusion.ids_ref, ...), custom_call_target="tpu_custom_call" | custom-call | flops 7500000256 | bytes 27000000 | tf_op jit(solution)/shard_map/spatial_first/pallas_call | solution.py:183
  37.7 0.1 collective-permute-start.10
  37.7 0.6 collective-permute-start.17
  38.3 3.8 %collective-permute-start.18 = (bf16[4,8,8,256]{3,2,1,0:T(8,128)(2,1)S(1)}, bf16[4,8,8,256]{3,2,1,0:T(8,128)(2,1)S(1)}, u32[]{:S(2)}, u32[]{:S(2)}) collective-permute-start(bf16[4,8,8,256]{3,2,1,0:T(8,128)(2,1)S(1)} %get-tuple-element.51), channel_id=1, source_target_pairs={{0,24},{8,16},{16,8},{24,0},{1,25},{9,17},{17,9},{25,1},{2,26},{10... | collective-permute-start | bytes 393224 | tf_op jit(solution)/shard_map/ppermute | solution.py:357
  42.1 6.4 %spatial_later.1 = (bf16[4,8,8,256]{3,2,1,0:T(8,128)(2,1)S(1)}, bf16[4,8,8,256]{3,2,1,0:T(8,128)(2,1)S(1)}, bf16[4,8,8,256]{3,2,1,0:T(8,128)(2,1)S(1)}, bf16[4,8,8,256]{3,2,1,0:T(8,128)(2,1)S(1)}) custom-call(s32[2]{0:T(128)S(1)} %pad_add_fusion.ids_ref, bf16[2,64,256]{2,1,0:T(8,128)(2,1)S(1)} %get-tuple-element.125.refs_0_, ...), custom_call_target="tpu_custom_call" | custom-call | flops 6400000000 | bytes 23040000 | tf_op jit(solution)/shard_map/spatial_later/pallas_call | solution.py:202
  48.7 0.6 collective-permute-start.11
  49.2 1.2 %collective-permute-start.12 = (bf16[4,8,8,256]{3,2,1,0:T(8,128)(2,1)S(1)}, bf16[4,8,8,256]{3,2,1,0:T(8,128)(2,1)S(1)}, u32[]{:S(2)}, u32[]{:S(2)}) collective-permute-start(bf16[4,8,8,256]{3,2,1,0:T(8,128)(2,1)S(1)} %get-tuple-element.47), channel_id=1, source_target_pairs={{0,4},{1,5},{2,6},{3,7},{4,0},{5,1},{6,2},{7,3},{8,12},{9,13},{10,... | collective-permute-start | bytes 393224 | tf_op jit(solution)/shard_map/ppermute | solution.py:357
  50.4 1.8 %collective-permute-start.13 = (bf16[4,8,8,256]{3,2,1,0:T(8,128)(2,1)S(1)}, bf16[4,8,8,256]{3,2,1,0:T(8,128)(2,1)S(1)}, u32[]{:S(2)}, u32[]{:S(2)}) collective-permute-start(bf16[4,8,8,256]{3,2,1,0:T(8,128)(2,1)S(1)} %get-tuple-element.48), channel_id=1, source_target_pairs={{0,6},{1,7},{2,4},{3,5},{4,2},{5,3},{6,0},{7,1},{8,14},{9,15},{10,... | collective-permute-start | bytes 393224 | tf_op jit(solution)/shard_map/ppermute | solution.py:357
  52.3 0.6 collective-permute-start.19
  52.9 1.3 %collective-permute-start.20 = (bf16[4,64,256]{2,1,0:T(8,128)(2,1)S(1)}, bf16[4,64,256]{2,1,0:T(8,128)(2,1)S(1)}, u32[]{:S(2)}, u32[]{:S(2)}) collective-permute-start(bf16[4,64,256]{2,1,0:T(8,128)(2,1)S(1)} %pad_maximum_fusion.11), channel_id=1, source_target_pairs={{0,4},{1,5},{2,6},{3,7},{4,0},{5,1},{6,2},{7,3},{8,12},{9,13},{10,... | collective-permute-start | bytes 393224 | tf_op jit(solution)/shard_map/ppermute | solution.py:357
  54.2 1.0 %collective-permute-done.11 = bf16[4,8,8,256]{3,2,1,0:T(8,128)(2,1)S(1)} collective-permute-done((bf16[4,8,8,256]{3,2,1,0:T(8,128)(2,1)S(1)}, bf16[4,8,8,256]{3,2,1,0:T(8,128)(2,1)S(1)}, u32[]{:S(2)}, u32[]{:S(2)}) %collective-permute-start.11) | collective-permute-done | bytes 131104 | tf_op jit(solution)/shard_map/ppermute | solution.py:357
  55.1 1.0 %collective-permute-start.21 = (bf16[4,64,256]{2,1,0:T(8,128)(2,1)S(1)}, bf16[4,64,256]{2,1,0:T(8,128)(2,1)S(1)}, u32[]{:S(2)}, u32[]{:S(2)}) collective-permute-start(bf16[4,64,256]{2,1,0:T(8,128)(2,1)S(1)} %pad_maximum_fusion.12), channel_id=1, source_target_pairs={{0,6},{1,7},{2,4},{3,5},{4,2},{5,3},{6,0},{7,1},{8,14},{9,15},{10,... | collective-permute-start | bytes 393224 | tf_op jit(solution)/shard_map/ppermute | solution.py:357
  56.2 1.6 %collective-permute-done.12 = bf16[4,8,8,256]{3,2,1,0:T(8,128)(2,1)S(1)} collective-permute-done((bf16[4,8,8,256]{3,2,1,0:T(8,128)(2,1)S(1)}, bf16[4,8,8,256]{3,2,1,0:T(8,128)(2,1)S(1)}, u32[]{:S(2)}, u32[]{:S(2)}) %collective-permute-start.12) | collective-permute-done | bytes 131104 | tf_op jit(solution)/shard_map/ppermute | solution.py:357
  58.0 1.2 %collective-permute-start.15 = (bf16[4,64,256]{2,1,0:T(8,128)(2,1)S(1)}, bf16[4,64,256]{2,1,0:T(8,128)(2,1)S(1)}, u32[]{:S(2)}, u32[]{:S(2)}) collective-permute-start(bf16[4,64,256]{2,1,0:T(8,128)(2,1)S(1)} %pad_maximum_fusion.8), channel_id=1, source_target_pairs={{0,16},{8,24},{16,0},{24,8},{1,17},{9,25},{17,1},{25,9},{2,18},{10... | collective-permute-start | bytes 393224 | tf_op jit(solution)/shard_map/ppermute | solution.py:357
  59.2 1.3 %collective-permute-done.19.refs_4_ = bf16[4,64,256]{2,1,0:T(8,128)(2,1)S(1)} collective-permute-done((bf16[4,64,256]{2,1,0:T(8,128)(2,1)S(1)}, bf16[4,64,256]{2,1,0:T(8,128)(2,1)S(1)}, u32[]{:S(2)}, u32[]{:S(2)}) %collective-permute-start.19) | collective-permute-done | bytes 131104 | tf_op jit(solution)/shard_map/ppermute | solution.py:357
  60.4 2.1 %collective-permute-start.16 = (bf16[4,64,256]{2,1,0:T(8,128)(2,1)S(1)}, bf16[4,64,256]{2,1,0:T(8,128)(2,1)S(1)}, u32[]{:S(2)}, u32[]{:S(2)}) collective-permute-start(bf16[4,64,256]{2,1,0:T(8,128)(2,1)S(1)} %pad_maximum_fusion.9), channel_id=1, source_target_pairs={{0,24},{8,16},{16,8},{24,0},{1,25},{9,17},{17,9},{25,1},{2,26},{10... | collective-permute-start | bytes 393224 | tf_op jit(solution)/shard_map/ppermute | solution.py:357
  62.6 1.9 %temporal.2 = (bf16[4,64,256]{2,1,0:T(8,128)(2,1)S(1)}, bf16[4,64,256]{2,1,0:T(8,128)(2,1)S(1)}, bf16[4,64,256]{2,1,0:T(8,128)(2,1)S(1)}, bf16[4,64,256]{2,1,0:T(8,128)(2,1)S(1)}) custom-call(bf16[64,256]{1,0:T(8,128)(2,1)S(1)} %get-tuple-element.83.refs_0_, bf16[64,256]{1,0:T(8,128)(2,1)S(1)} %get-tuple-element.87.refs_1_, ...), custom_call_target="tpu_custom_call" | custom-call | flops 1900000000 | bytes 6840000 | tf_op jit(solution)/shard_map/temporal/pallas_call | solution.py:290
  64.5 0.1 collective-permute-start.25
  64.6 2.3 %collective-permute-start.26 = (bf16[4,64,256]{2,1,0:T(8,128)(2,1)S(1)}, bf16[4,64,256]{2,1,0:T(8,128)(2,1)S(1)}, u32[]{:S(2)}, u32[]{:S(2)}) collective-permute-start(bf16[4,64,256]{2,1,0:T(8,128)(2,1)S(1)} %get-tuple-element.54), channel_id=1, source_target_pairs={{0,16},{8,24},{16,0},{24,8},{1,17},{9,25},{17,1},{25,9},{2,18},{10... | collective-permute-start | bytes 393224 | tf_op jit(solution)/shard_map/ppermute | solution.py:357
  66.9 2.1 %collective-permute-start.27 = (bf16[4,64,256]{2,1,0:T(8,128)(2,1)S(1)}, bf16[4,64,256]{2,1,0:T(8,128)(2,1)S(1)}, u32[]{:S(2)}, u32[]{:S(2)}) collective-permute-start(bf16[4,64,256]{2,1,0:T(8,128)(2,1)S(1)} %get-tuple-element.55), channel_id=1, source_target_pairs={{0,24},{8,16},{16,8},{24,0},{1,25},{9,17},{17,9},{25,1},{2,26},{10... | collective-permute-start | bytes 393224 | tf_op jit(solution)/shard_map/ppermute | solution.py:357
  68.9 2.9 %collective-permute-done.15.refs_5_ = bf16[4,64,256]{2,1,0:T(8,128)(2,1)S(1)} collective-permute-done((bf16[4,64,256]{2,1,0:T(8,128)(2,1)S(1)}, bf16[4,64,256]{2,1,0:T(8,128)(2,1)S(1)}, u32[]{:S(2)}, u32[]{:S(2)}) %collective-permute-start.15) | collective-permute-done | bytes 131104 | tf_op jit(solution)/shard_map/ppermute | solution.py:357
  71.9 1.9 %temporal.3 = (bf16[4,64,256]{2,1,0:T(8,128)(2,1)S(1)}, bf16[4,64,256]{2,1,0:T(8,128)(2,1)S(1)}, bf16[4,64,256]{2,1,0:T(8,128)(2,1)S(1)}, bf16[4,64,256]{2,1,0:T(8,128)(2,1)S(1)}) custom-call(bf16[64,256]{1,0:T(8,128)(2,1)S(1)} %get-tuple-element.99.refs_0_, bf16[64,256]{1,0:T(8,128)(2,1)S(1)} %get-tuple-element.103.refs_1_, ...), custom_call_target="tpu_custom_call" | custom-call | flops 1900000000 | bytes 6840000 | tf_op jit(solution)/shard_map/temporal/pallas_call | solution.py:290
  73.8 9.6 %collective-permute-start.22 = (bf16[4,64,256]{2,1,0:T(8,128)(2,1)S(1)}, bf16[4,64,256]{2,1,0:T(8,128)(2,1)S(1)}, u32[]{:S(2)}, u32[]{:S(2)}) collective-permute-start(bf16[4,64,256]{2,1,0:T(8,128)(2,1)S(1)} %get-tuple-element.60), channel_id=1, source_target_pairs={{0,8},{8,0},{16,24},{24,16},{1,9},{9,1},{17,25},{25,17},{2,10},{10... | collective-permute-start | bytes 393224 | tf_op jit(solution)/shard_map/ppermute | solution.py:357
  83.4 2.4 %collective-permute-start.24 = (bf16[4,64,256]{2,1,0:T(8,128)(2,1)S(1)}, bf16[4,64,256]{2,1,0:T(8,128)(2,1)S(1)}, u32[]{:S(2)}, u32[]{:S(2)}) collective-permute-start(bf16[4,64,256]{2,1,0:T(8,128)(2,1)S(1)} %get-tuple-element.62), channel_id=1, source_target_pairs={{0,24},{8,16},{16,8},{24,0},{1,25},{9,17},{17,9},{25,1},{2,26},{10... | collective-permute-start | bytes 393224 | tf_op jit(solution)/shard_map/ppermute | solution.py:357
  85.9 1.4 %assemble.2.refs_4_ = bf16[32,64,256]{2,1,0:T(8,128)(2,1)} custom-call(s32[2]{0:T(128)S(1)} %pad_add_fusion.ids_ref, bf16[4,8,8,256]{3,2,1,0:T(8,128)(2,1)S(1)} %bitcast.101, bf16[4,8,8,256]{3,2,1,0:T(8,128)(2,1)S(1)} %bitcast.91, bf16[4,8,8,256]{3,2,1,0:T(8,128)(2,1)S(1)} %bitcast.92, ...), custom_call_target="tpu_custom_call", output_to_operand_aliasing={{}: (5, {})} | custom-call | flops 60000002048 | bytes 216000000 | tf_op jit(solution)/shard_map/assemble/pallas_call | solution.py:329
  87.3 4.5 %collective-permute-done.23 = bf16[4,64,256]{2,1,0:T(8,128)(2,1)S(1)} collective-permute-done((bf16[4,64,256]{2,1,0:T(8,128)(2,1)S(1)}, bf16[4,64,256]{2,1,0:T(8,128)(2,1)S(1)}, u32[]{:S(2)}, u32[]{:S(2)}) %collective-permute-start.23) | collective-permute-done | bytes 131104 | tf_op jit(solution)/shard_map/ppermute | solution.py:357
  91.8 1.4 %assemble.3 = bf16[32,64,256]{2,1,0:T(8,128)(2,1)} custom-call(s32[2]{0:T(128)S(1)} %pad_add_fusion.ids_ref, bf16[4,8,8,256]{3,2,1,0:T(8,128)(2,1)S(1)} %bitcast.102, bf16[4,8,8,256]{3,2,1,0:T(8,128)(2,1)S(1)} %bitcast.94, bf16[4,8,8,256]{3,2,1,0:T(8,128)(2,1)S(1)} %bitcast.95, bf16[4,8,8,256]{3,2,1,0:T(8,128)(2,1)S(1)} %bitcast.96, ...), custom_call_target="tpu_custom_call", output_to_operand_aliasing={{}: (5, {})} | custom-call | flops 1000000000 | bytes 3600000 | tf_op jit(solution)/shard_map/assemble/pallas_call | solution.py:329
  (69 shorter events, 0.7 us)
Async XLA Ops:
  0.0 14.3 %copy-start.10 = (bf16[32,64,256]{2,1,0:T(8,128)(2,1)S(1)}, bf16[32,64,256]{2,1,0:T(8,128)(2,1)}, u32[]{:S(2)}) copy-start(bf16[32,64,256]{2,1,0:T(8,128)(2,1)} %param.11) | copy-start | bytes 3145732
  1.0 6.4 %collective-permute-start.2 = (bf16[2,64,256]{2,1,0:T(8,128)(2,1)S(1)}, bf16[2,64,256]{2,1,0:T(8,128)(2,1)S(1)}, u32[]{:S(2)}, u32[]{:S(2)}) collective-permute-start(bf16[2,64,256]{2,1,0:T(8,128)(2,1)S(1)} %get-tuple-element.122), channel_id=1, source_target_pairs={{0,6},{1,7},{2,4},{3,5},{4,2},{5,3},{6,0},{7,1},{8,14},{9,15},{10,... | collective-permute-start | bytes 196616 | tf_op jit(solution)/shard_map/ppermute | solution.py:357
  4.9 4.8 %collective-permute-start = (bf16[2,64,256]{2,1,0:T(8,128)(2,1)S(1)}, bf16[2,64,256]{2,1,0:T(8,128)(2,1)S(1)}, u32[]{:S(2)}, u32[]{:S(2)}) collective-permute-start(bf16[2,64,256]{2,1,0:T(8,128)(2,1)S(1)} %get-tuple-element.123), channel_id=1, source_target_pairs={{0,2},{1,3},{2,0},{3,1},{4,6},{5,7},{6,4},{7,5},{8,10},{9,11},{10,... | collective-permute-start | bytes 196616 | tf_op jit(solution)/shard_map/ppermute | solution.py:357
  5.5 4.3 %collective-permute-start.1 = (bf16[2,64,256]{2,1,0:T(8,128)(2,1)S(1)}, bf16[2,64,256]{2,1,0:T(8,128)(2,1)S(1)}, u32[]{:S(2)}, u32[]{:S(2)}) collective-permute-start(bf16[2,64,256]{2,1,0:T(8,128)(2,1)S(1)} %get-tuple-element.124), channel_id=1, source_target_pairs={{0,4},{1,5},{2,6},{3,7},{4,0},{5,1},{6,2},{7,3},{8,12},{9,13},{10,... | collective-permute-start | bytes 196616 | tf_op jit(solution)/shard_map/ppermute | solution.py:357
  9.8 8.2 %collective-permute-start.3 = (bf16[4,64,256]{2,1,0:T(8,128)(2,1)S(1)}, bf16[4,64,256]{2,1,0:T(8,128)(2,1)S(1)}, u32[]{:S(2)}, u32[]{:S(2)}) collective-permute-start(bf16[4,64,256]{2,1,0:T(8,128)(2,1)S(1)} %pad_maximum_fusion.5), channel_id=1, source_target_pairs={{0,16},{1,17},{2,18},{3,19},{4,20},{5,21},{6,22},{7,23}} | collective-permute-start | bytes 393224 | tf_op jit(solution)/shard_map/ppermute | solution.py:397
  14.4 8.6 %collective-permute-start.5 = (bf16[7,64,256]{2,1,0:T(8,128)(2,1)S(1)}, bf16[7,64,256]{2,1,0:T(8,128)(2,1)S(1)}, u32[]{:S(2)}, u32[]{:S(2)}) collective-permute-start(bf16[7,64,256]{2,1,0:T(8,128)(2,1)S(1)} %get-tuple-element.64), channel_id=1, source_target_pairs={{0,2},{1,3},{2,0},{3,1},{4,6},{5,7},{6,4},{7,5},{8,10},{9,11},{10,... | collective-permute-start | bytes 688136 | tf_op jit(solution)/shard_map/ppermute | solution.py:357
  16.0 10.8 %collective-permute-start.6 = (bf16[7,64,256]{2,1,0:T(8,128)(2,1)S(1)}, bf16[7,64,256]{2,1,0:T(8,128)(2,1)S(1)}, u32[]{:S(2)}, u32[]{:S(2)}) collective-permute-start(bf16[7,64,256]{2,1,0:T(8,128)(2,1)S(1)} %get-tuple-element.66), channel_id=1, source_target_pairs={{0,4},{1,5},{2,6},{3,7},{4,0},{5,1},{6,2},{7,3},{8,12},{9,13},{10,... | collective-permute-start | bytes 688136 | tf_op jit(solution)/shard_map/ppermute | solution.py:357
  16.5 10.3 %collective-permute-start.7 = (bf16[7,64,256]{2,1,0:T(8,128)(2,1)S(1)}, bf16[7,64,256]{2,1,0:T(8,128)(2,1)S(1)}, u32[]{:S(2)}, u32[]{:S(2)}) collective-permute-start(bf16[7,64,256]{2,1,0:T(8,128)(2,1)S(1)} %get-tuple-element.63), channel_id=1, source_target_pairs={{0,6},{1,7},{2,4},{3,5},{4,2},{5,3},{6,0},{7,1},{8,14},{9,15},{10,... | collective-permute-start | bytes 688136 | tf_op jit(solution)/shard_map/ppermute | solution.py:357
  18.0 3.8 %collective-permute-start.4 = (bf16[4,64,256]{2,1,0:T(8,128)(2,1)S(1)}, bf16[4,64,256]{2,1,0:T(8,128)(2,1)S(1)}, u32[]{:S(2)}, u32[]{:S(2)}) collective-permute-start(bf16[4,64,256]{2,1,0:T(8,128)(2,1)S(1)} %broadcast_select_fusion), channel_id=1, source_target_pairs={{0,8},{16,24},{1,9},{17,25},{2,10},{18,26},{3,11},{19,27},{4,12},{... | collective-permute-start | bytes 393224 | tf_op jit(solution)/shard_map/ppermute | solution.py:397
  19.4 7.7 %collective-permute-start.8 = (bf16[4,1,64,256]{3,2,1,0:T(8,128)(2,1)S(1)}, bf16[4,1,64,256]{3,2,1,0:T(8,128)(2,1)S(1)}, u32[]{:S(2)}, u32[]{:S(2)}) collective-permute-start(bf16[4,1,64,256]{3,2,1,0:T(8,128)(2,1)S(1)} %pad_maximum_fusion.6), channel_id=1, source_target_pairs={{0,1},{1,0},{2,3},{3,2},{4,5},{5,4},{6,7},{7,6},{8,9},{9,8},{10,11... | collective-permute-start | bytes 393224 | tf_op jit(solution)/shard_map/ppermute | solution.py:357
  23.0 4.1 %copy-start = (bf16[256,256]{1,0:T(8,128)(2,1)S(1)}, bf16[256,256]{1,0:T(8,128)(2,1)}, u32[]{:S(2)}) copy-start(bf16[256,256]{1,0:T(8,128)(2,1)} %refs_10_.3) | copy-start | bytes 393220
  23.0 4.1 %copy-start.1 = (bf16[256,256]{1,0:T(8,128)(2,1)S(1)}, bf16[256,256]{1,0:T(8,128)(2,1)}, u32[]{:S(2)}) copy-start(bf16[256,256]{1,0:T(8,128)(2,1)} %refs_11_.3) | copy-start | bytes 393220
  23.0 4.1 %copy-start.2 = (bf16[256,256]{1,0:T(8,128)(2,1)S(1)}, bf16[256,256]{1,0:T(8,128)(2,1)}, u32[]{:S(2)}) copy-start(bf16[256,256]{1,0:T(8,128)(2,1)} %refs_12_.1) | copy-start | bytes 393220
  23.0 4.1 %copy-start.8 = (f32[256]{0:T(256)S(1)}, f32[256]{0:T(256)}, u32[]{:S(2)}) copy-start(f32[256]{0:T(256)} %param.12) | copy-start | bytes 3076
  27.0 2.7 %collective-permute-start.9 = (bf16[4,8,64,256]{3,2,1,0:T(8,128)(2,1)S(1)}, bf16[4,8,64,256]{3,2,1,0:T(8,128)(2,1)S(1)}, u32[]{:S(2)}, u32[]{:S(2)}) collective-permute-start(bf16[4,8,64,256]{3,2,1,0:T(8,128)(2,1)S(1)} %pad_maximum_fusion), channel_id=1, source_target_pairs={{0,1},{1,0},{2,3},{3,2},{4,5},{5,4},{6,7},{7,6},{8,9},{9,8},{10,11... | collective-permute-start | bytes 3145736 | tf_op jit(solution)/shard_map/ppermute | solution.py:357
  27.1 2.6 %copy-start.3 = (bf16[256,256]{1,0:T(8,128)(2,1)S(1)}, bf16[256,256]{1,0:T(8,128)(2,1)}, u32[]{:S(2)}) copy-start(bf16[256,256]{1,0:T(8,128)(2,1)} %refs_14_.1) | copy-start | bytes 393220
  37.7 11.0 %collective-permute-start.10 = (bf16[4,8,8,256]{3,2,1,0:T(8,128)(2,1)S(1)}, bf16[4,8,8,256]{3,2,1,0:T(8,128)(2,1)S(1)}, u32[]{:S(2)}, u32[]{:S(2)}) collective-permute-start(bf16[4,8,8,256]{3,2,1,0:T(8,128)(2,1)S(1)} %get-tuple-element.44), channel_id=1, source_target_pairs={{0,8},{8,0},{16,24},{24,16},{1,9},{9,1},{17,25},{25,17},{2,10},{10... | collective-permute-start | bytes 393224 | tf_op jit(solution)/shard_map/ppermute | solution.py:357
  37.7 14.5 %collective-permute-start.17 = (bf16[4,8,8,256]{3,2,1,0:T(8,128)(2,1)S(1)}, bf16[4,8,8,256]{3,2,1,0:T(8,128)(2,1)S(1)}, u32[]{:S(2)}, u32[]{:S(2)}) collective-permute-start(bf16[4,8,8,256]{3,2,1,0:T(8,128)(2,1)S(1)} %get-tuple-element.50), channel_id=1, source_target_pairs={{0,16},{8,24},{16,0},{24,8},{1,17},{9,25},{17,1},{25,9},{2,18},{10... | collective-permute-start | bytes 393224 | tf_op jit(solution)/shard_map/ppermute | solution.py:357
  38.3 13.9 %collective-permute-start.18 = (bf16[4,8,8,256]{3,2,1,0:T(8,128)(2,1)S(1)}, bf16[4,8,8,256]{3,2,1,0:T(8,128)(2,1)S(1)}, u32[]{:S(2)}, u32[]{:S(2)}) collective-permute-start(bf16[4,8,8,256]{3,2,1,0:T(8,128)(2,1)S(1)} %get-tuple-element.51), channel_id=1, source_target_pairs={{0,24},{8,16},{16,8},{24,0},{1,25},{9,17},{17,9},{25,1},{2,26},{10... | collective-permute-start | bytes 393224 | tf_op jit(solution)/shard_map/ppermute | solution.py:357
  48.5 14.0 %copy-start.4 = (bf16[256,256]{1,0:T(8,128)(2,1)S(1)}, bf16[256,256]{1,0:T(8,128)(2,1)}, u32[]{:S(2)}) copy-start(bf16[256,256]{1,0:T(8,128)(2,1)} %refs_8_.5) | copy-start | bytes 393220
  48.6 14.0 %copy-start.5 = (bf16[256,256]{1,0:T(8,128)(2,1)S(1)}, bf16[256,256]{1,0:T(8,128)(2,1)}, u32[]{:S(2)}) copy-start(bf16[256,256]{1,0:T(8,128)(2,1)} %refs_9_.3) | copy-start | bytes 393220
  48.6 14.0 %copy-start.6 = (bf16[256,256]{1,0:T(8,128)(2,1)S(1)}, bf16[256,256]{1,0:T(8,128)(2,1)}, u32[]{:S(2)}) copy-start(bf16[256,256]{1,0:T(8,128)(2,1)} %refs_10_.5) | copy-start | bytes 393220
  48.6 14.0 %copy-start.7 = (bf16[256,256]{1,0:T(8,128)(2,1)S(1)}, bf16[256,256]{1,0:T(8,128)(2,1)}, u32[]{:S(2)}) copy-start(bf16[256,256]{1,0:T(8,128)(2,1)} %refs_11_.5) | copy-start | bytes 393220
  48.6 14.0 %copy-start.9 = (f32[256]{0:T(256)S(1)}, f32[256]{0:T(256)}, u32[]{:S(2)}) copy-start(f32[256]{0:T(256)} %param.17) | copy-start | bytes 3076
  48.7 6.5 %collective-permute-start.11 = (bf16[4,8,8,256]{3,2,1,0:T(8,128)(2,1)S(1)}, bf16[4,8,8,256]{3,2,1,0:T(8,128)(2,1)S(1)}, u32[]{:S(2)}, u32[]{:S(2)}) collective-permute-start(bf16[4,8,8,256]{3,2,1,0:T(8,128)(2,1)S(1)} %get-tuple-element.46), channel_id=1, source_target_pairs={{0,2},{1,3},{2,0},{3,1},{4,6},{5,7},{6,4},{7,5},{8,10},{9,11},{10,... | collective-permute-start | bytes 393224 | tf_op jit(solution)/shard_map/ppermute | solution.py:357
  49.2 8.6 %collective-permute-start.12 = (bf16[4,8,8,256]{3,2,1,0:T(8,128)(2,1)S(1)}, bf16[4,8,8,256]{3,2,1,0:T(8,128)(2,1)S(1)}, u32[]{:S(2)}, u32[]{:S(2)}) collective-permute-start(bf16[4,8,8,256]{3,2,1,0:T(8,128)(2,1)S(1)} %get-tuple-element.47), channel_id=1, source_target_pairs={{0,4},{1,5},{2,6},{3,7},{4,0},{5,1},{6,2},{7,3},{8,12},{9,13},{10,... | collective-permute-start | bytes 393224 | tf_op jit(solution)/shard_map/ppermute | solution.py:357
  50.4 7.4 %collective-permute-start.13 = (bf16[4,8,8,256]{3,2,1,0:T(8,128)(2,1)S(1)}, bf16[4,8,8,256]{3,2,1,0:T(8,128)(2,1)S(1)}, u32[]{:S(2)}, u32[]{:S(2)}) collective-permute-start(bf16[4,8,8,256]{3,2,1,0:T(8,128)(2,1)S(1)} %get-tuple-element.48), channel_id=1, source_target_pairs={{0,6},{1,7},{2,4},{3,5},{4,2},{5,3},{6,0},{7,1},{8,14},{9,15},{10,... | collective-permute-start | bytes 393224 | tf_op jit(solution)/shard_map/ppermute | solution.py:357
  52.3 8.1 %collective-permute-start.19 = (bf16[4,64,256]{2,1,0:T(8,128)(2,1)S(1)}, bf16[4,64,256]{2,1,0:T(8,128)(2,1)S(1)}, u32[]{:S(2)}, u32[]{:S(2)}) collective-permute-start(bf16[4,64,256]{2,1,0:T(8,128)(2,1)S(1)} %pad_maximum_fusion.10), channel_id=1, source_target_pairs={{0,2},{1,3},{2,0},{3,1},{4,6},{5,7},{6,4},{7,5},{8,10},{9,11},{10,... | collective-permute-start | bytes 393224 | tf_op jit(solution)/shard_map/ppermute | solution.py:357
  52.9 9.6 %collective-permute-start.20 = (bf16[4,64,256]{2,1,0:T(8,128)(2,1)S(1)}, bf16[4,64,256]{2,1,0:T(8,128)(2,1)S(1)}, u32[]{:S(2)}, u32[]{:S(2)}) collective-permute-start(bf16[4,64,256]{2,1,0:T(8,128)(2,1)S(1)} %pad_maximum_fusion.11), channel_id=1, source_target_pairs={{0,4},{1,5},{2,6},{3,7},{4,0},{5,1},{6,2},{7,3},{8,12},{9,13},{10,... | collective-permute-start | bytes 393224 | tf_op jit(solution)/shard_map/ppermute | solution.py:357
  55.1 7.4 %collective-permute-start.21 = (bf16[4,64,256]{2,1,0:T(8,128)(2,1)S(1)}, bf16[4,64,256]{2,1,0:T(8,128)(2,1)S(1)}, u32[]{:S(2)}, u32[]{:S(2)}) collective-permute-start(bf16[4,64,256]{2,1,0:T(8,128)(2,1)S(1)} %pad_maximum_fusion.12), channel_id=1, source_target_pairs={{0,6},{1,7},{2,4},{3,5},{4,2},{5,3},{6,0},{7,1},{8,14},{9,15},{10,... | collective-permute-start | bytes 393224 | tf_op jit(solution)/shard_map/ppermute | solution.py:357
  57.9 9.0 %collective-permute-start.14 = (bf16[4,64,256]{2,1,0:T(8,128)(2,1)S(1)}, bf16[4,64,256]{2,1,0:T(8,128)(2,1)S(1)}, u32[]{:S(2)}, u32[]{:S(2)}) collective-permute-start(bf16[4,64,256]{2,1,0:T(8,128)(2,1)S(1)} %pad_maximum_fusion.7), channel_id=1, source_target_pairs={{0,8},{8,0},{16,24},{24,16},{1,9},{9,1},{17,25},{25,17},{2,10},{10... | collective-permute-start | bytes 393224 | tf_op jit(solution)/shard_map/ppermute | solution.py:357
  58.0 13.9 %collective-permute-start.15 = (bf16[4,64,256]{2,1,0:T(8,128)(2,1)S(1)}, bf16[4,64,256]{2,1,0:T(8,128)(2,1)S(1)}, u32[]{:S(2)}, u32[]{:S(2)}) collective-permute-start(bf16[4,64,256]{2,1,0:T(8,128)(2,1)S(1)} %pad_maximum_fusion.8), channel_id=1, source_target_pairs={{0,16},{8,24},{16,0},{24,8},{1,17},{9,25},{17,1},{25,9},{2,18},{10... | collective-permute-start | bytes 393224 | tf_op jit(solution)/shard_map/ppermute | solution.py:357
  60.4 11.4 %collective-permute-start.16 = (bf16[4,64,256]{2,1,0:T(8,128)(2,1)S(1)}, bf16[4,64,256]{2,1,0:T(8,128)(2,1)S(1)}, u32[]{:S(2)}, u32[]{:S(2)}) collective-permute-start(bf16[4,64,256]{2,1,0:T(8,128)(2,1)S(1)} %pad_maximum_fusion.9), channel_id=1, source_target_pairs={{0,24},{8,16},{16,8},{24,0},{1,25},{9,17},{17,9},{25,1},{2,26},{10... | collective-permute-start | bytes 393224 | tf_op jit(solution)/shard_map/ppermute | solution.py:357
  64.5 18.9 %collective-permute-start.25 = (bf16[4,64,256]{2,1,0:T(8,128)(2,1)S(1)}, bf16[4,64,256]{2,1,0:T(8,128)(2,1)S(1)}, u32[]{:S(2)}, u32[]{:S(2)}) collective-permute-start(bf16[4,64,256]{2,1,0:T(8,128)(2,1)S(1)} %get-tuple-element.53), channel_id=1, source_target_pairs={{0,8},{8,0},{16,24},{24,16},{1,9},{9,1},{17,25},{25,17},{2,10},{10... | collective-permute-start | bytes 393224 | tf_op jit(solution)/shard_map/ppermute | solution.py:357
  64.6 21.3 %collective-permute-start.26 = (bf16[4,64,256]{2,1,0:T(8,128)(2,1)S(1)}, bf16[4,64,256]{2,1,0:T(8,128)(2,1)S(1)}, u32[]{:S(2)}, u32[]{:S(2)}) collective-permute-start(bf16[4,64,256]{2,1,0:T(8,128)(2,1)S(1)} %get-tuple-element.54), channel_id=1, source_target_pairs={{0,16},{8,24},{16,0},{24,8},{1,17},{9,25},{17,1},{25,9},{2,18},{10... | collective-permute-start | bytes 393224 | tf_op jit(solution)/shard_map/ppermute | solution.py:357
  66.9 19.0 %collective-permute-start.27 = (bf16[4,64,256]{2,1,0:T(8,128)(2,1)S(1)}, bf16[4,64,256]{2,1,0:T(8,128)(2,1)S(1)}, u32[]{:S(2)}, u32[]{:S(2)}) collective-permute-start(bf16[4,64,256]{2,1,0:T(8,128)(2,1)S(1)} %get-tuple-element.55), channel_id=1, source_target_pairs={{0,24},{8,16},{16,8},{24,0},{1,25},{9,17},{17,9},{25,1},{2,26},{10... | collective-permute-start | bytes 393224 | tf_op jit(solution)/shard_map/ppermute | solution.py:357
  73.8 13.5 %collective-permute-start.22 = (bf16[4,64,256]{2,1,0:T(8,128)(2,1)S(1)}, bf16[4,64,256]{2,1,0:T(8,128)(2,1)S(1)}, u32[]{:S(2)}, u32[]{:S(2)}) collective-permute-start(bf16[4,64,256]{2,1,0:T(8,128)(2,1)S(1)} %get-tuple-element.60), channel_id=1, source_target_pairs={{0,8},{8,0},{16,24},{24,16},{1,9},{9,1},{17,25},{25,17},{2,10},{10... | collective-permute-start | bytes 393224 | tf_op jit(solution)/shard_map/ppermute | solution.py:357
  83.4 8.4 %collective-permute-start.23 = (bf16[4,64,256]{2,1,0:T(8,128)(2,1)S(1)}, bf16[4,64,256]{2,1,0:T(8,128)(2,1)S(1)}, u32[]{:S(2)}, u32[]{:S(2)}) collective-permute-start(bf16[4,64,256]{2,1,0:T(8,128)(2,1)S(1)} %get-tuple-element.61), channel_id=1, source_target_pairs={{0,16},{8,24},{16,0},{24,8},{1,17},{9,25},{17,1},{25,9},{2,18},{10... | collective-permute-start | bytes 393224 | tf_op jit(solution)/shard_map/ppermute | solution.py:357
  83.4 8.4 %collective-permute-start.24 = (bf16[4,64,256]{2,1,0:T(8,128)(2,1)S(1)}, bf16[4,64,256]{2,1,0:T(8,128)(2,1)S(1)}, u32[]{:S(2)}, u32[]{:S(2)}) collective-permute-start(bf16[4,64,256]{2,1,0:T(8,128)(2,1)S(1)} %get-tuple-element.62), channel_id=1, source_target_pairs={{0,24},{8,16},{16,8},{24,0},{1,25},{9,17},{17,9},{25,1},{2,26},{10... | collective-permute-start | bytes 393224 | tf_op jit(solution)/shard_map/ppermute | solution.py:357

commit v3 on v2

--- a/solution.py
+++ b/solution.py
@@ -9,7 +9,7 @@
 
 HEADS = 4
 LANES = 128
-EARLY = 40
+READY = 40
 SPLIT = 8
 LATER = 6.4
 ROOM = 26 * 2**20
@@ -32,24 +32,16 @@
     )
 
 
-def project(mine, other, gain_ref, wq_ref, wk_ref, wv_ref, q_ref, k_ref, v_ref, turns):
-    chips = len(mine)
-    local, width = mine[0].shape[1:]
-    asked, frames = q_ref.shape[0], k_ref.shape[0]
+def project(pieces, gain_ref, wk_ref, wv_ref, k_ref, v_ref):
+    frames, local, width = pieces[0].shape
     gain = gain_ref[...]
-    rows = [r[:frames] for r in mine] + [other[s] for s in range(chips)]
-    normal = [normed(r.reshape(frames * local, width).astype(jnp.float32), gain) for r in rows]
+    normal = [normed(r.reshape(frames * local, width).astype(jnp.float32), gain) for r in pieces]
     short = [n.astype(jnp.bfloat16) for n in normal]
     for weight, out in ((wk_ref, k_ref), (wv_ref, v_ref)):
-        for s in range(2 * chips):
-            got = dot(short[s], weight[...]).astype(jnp.bfloat16)
+        for s, n in enumerate(short):
+            got = dot(n, weight[...]).astype(jnp.bfloat16)
             out[:, s * local : (s + 1) * local, :] = got.reshape(frames, local, width)
-    scale = (width // HEADS) ** -0.5 * LOG2E
-    wide = [n.reshape(frames, local, width) for n in normal[:chips]]
-    for f in range(asked):
-        n = jnp.concatenate([w[f] for w in wide], axis=0)
-        n = jnp.concatenate([pick(n, chips, turns, j) for j in range(turns)], axis=0)
-        q_ref[f] = (dot(n.astype(jnp.bfloat16), wq_ref[...]) * scale).astype(jnp.bfloat16)
+    return [n.reshape(frames, local, width) for n in normal]
 
 
 def pick(rows, chips, turns, turn):
@@ -60,74 +52,76 @@
     )
 
 
-def attend(turns, turn, zf, parts, wo_ref, outs, mid_s, by_shard):
-    chips = len(parts[0][0])
-    shards = len(outs) * outs[0].shape[0] // chips
-    step, width = outs[0].shape[2:]
+def attend(turns, turn, zf, pieces, q_ref, k_refs, v_refs, wo_ref, outs, mid_s):
+    chips = len(pieces)
+    shards, step, width = len(outs), *outs[0].shape[2:]
     half = width // 2
     depth = width // HEADS
     rows = chips * shards * step
-    k0, v0 = parts[-1][2], parts[-1][3]
-    last = k0.shape[0] - 1
-    places = k0.shape[1]
+    frames = q_ref.shape[0]
+    places = 2 * k_refs[0].shape[1]
     low = lax.broadcasted_iota(jnp.int32, (rows, half), 1) < depth
     ones = jnp.ones((2 * places, half), jnp.bfloat16)
-    frames = [(part, f) for part in parts for f in range(part[1].shape[0])]
-    together = max(1, min(len(frames), ROOM // (2 * (2 * rows) * (2 * places) * 6)))
-    for start in range(0, len(frames), together):
-        now = frames[start : start + together]
-        items = [(part, f, slice(p * half, (p + 1) * half)) for part, f in now for p in range(2)]
+    both = lambda refs, f, cols: jnp.concatenate(
+        [refs[0][f, :, cols], refs[1][f, :, cols], refs[2][0, :, cols], refs[3][0, :, cols]], axis=0
+    )
+    together = max(1, min(frames, ROOM // (2 * (2 * rows) * (2 * places) * 6)))
+    for start in range(0, frames, together):
+        now = range(start, min(start + together, frames))
+        items = [(f, slice(p * half, (p + 1) * half)) for f in now for p in range(2)]
         scores = []
-        for (_, q_ref, k_ref, _), f, cols in items:
+        for f, cols in items:
             q = q_ref[f, turn * rows : (turn + 1) * rows, cols]
             zero = jnp.zeros_like(q)
             q = jnp.concatenate([jnp.where(low, q, zero), jnp.where(low, zero, q)], axis=0)
-            scores.append(dot_t(q, jnp.concatenate([k_ref[f, :, cols], k0[last, :, cols]], axis=0)))
+            scores.append(dot_t(q, both(k_refs, f, cols)))
         weights = [
             jnp.exp2(s - jnp.max(s, axis=-1, keepdims=True)).astype(jnp.bfloat16) for s in scores
         ]
         sums = []
-        for w, ((_, _, _, v_ref), f, cols) in zip(weights, items):
-            vals = jnp.concatenate([v_ref[f, :, cols], v0[last, :, cols]], axis=0)
-            r = dot(w, jnp.concatenate([vals, ones], axis=1))
+        for w, (f, cols) in zip(weights, items):
+            r = dot(w, jnp.concatenate([both(v_refs, f, cols), ones], axis=1))
             top = jnp.where(low, r[:rows, :half], r[rows:, :half])
             bottom = jnp.where(low, r[:rows, half:], r[rows:, half:])
             sums.append(top / bottom)
-        for u, ((pieces, *_), f) in enumerate(now):
+        for u, f in enumerate(now):
             a = jnp.concatenate(sums[2 * u : 2 * u + 2], axis=1).astype(jnp.bfloat16)
             x = jnp.concatenate([r[f].astype(jnp.float32) for r in pieces], axis=0)
-            mid_s[start + u] = pick(x, chips, turns, turn) + dot(a, wo_ref[...])
-    for f in range(len(frames)):
+            mid_s[f] = pick(x, chips, turns, turn) + dot(a, wo_ref[...])
+    for f in range(frames):
         for t in range(shards):
             for s in range(chips):
                 at = pl.multiple_of((s * shards + (t ^ zf)) * step, step)
-                piece = mid_s[f, pl.ds(at, step), :].astype(jnp.bfloat16)
-                if by_shard:
-                    outs[t][s, f] = piece
-                else:
-                    outs[s][t, f] = piece
-
-
-def early_kernel(chips, turns, *refs):
-    mine, (other, gain, wq, wk, wv, q, k, v) = refs[:chips], refs[chips:]
-    project(mine, other, gain, wq, wk, wv, q, k, v, turns)
+                outs[t][s, f] = mid_s[f, pl.ds(at, step), :].astype(jnp.bfloat16)
+
+
+def ready_kernel(chips, turns, *refs):
+    mine, (gain, wq, wk, wv, q_ref, k_ref, v_ref) = refs[:chips], refs[chips:]
+    normal = project([r[...] for r in mine], gain, wk, wv, k_ref, v_ref)
+    scale = (wq.shape[0] // HEADS) ** -0.5 * LOG2E
+    for f in range(q_ref.shape[0]):
+        n = jnp.concatenate([w[f] for w in normal], axis=0)
+        n = jnp.concatenate([pick(n, chips, turns, j) for j in range(turns)], axis=0)
+        q_ref[f] = (dot(n.astype(jnp.bfloat16), wq[...]) * scale).astype(jnp.bfloat16)
+
+
+def rest_kernel(chips, other, gain, wk, wv, k_ref, v_ref):
+    project([other[s] for s in range(chips)], gain, wk, wv, k_ref, v_ref)
 
 
 def first_kernel(chips, shards, turns, ids_ref, *refs):
-    early, refs = refs[:chips], refs[chips:]
-    late, refs = refs[:chips], refs[chips:]
-    other, gain, wq, wk, wv, wo, q1, k1, v1 = refs[:9]
-    outs, (q2, k2, v2, mid_s) = refs[9 : 9 + shards], refs[9 + shards :]
-    project(late, other, gain, wq, wk, wv, q2, k2, v2, turns)
-    attend(turns, 0, ids_ref[0], [(early, q1, k1, v1), (late, q2, k2, v2)], wo, outs, mid_s, True)
-
-
-def later_kernel(chips, shards, turns, turn, ids_ref, *refs):
-    early, refs = refs[:chips], refs[chips:]
-    late, refs = refs[:chips], refs[chips:]
-    q1, k1, v1, q2, k2, v2, wo = refs[:7]
-    outs, mid_s = refs[7:-1], refs[-1]
-    attend(turns, turn, ids_ref[0], [(early, q1, k1, v1), (late, q2, k2, v2)], wo, outs, mid_s, False)
+    mine, (near, far, gain, wk, wv, wo, q, k, v, ko, vo) = refs[:chips], refs[chips : chips + 11]
+    outs, saved = refs[chips + 11 : chips + 11 + shards], refs[chips + 11 + shards :]
+    kn, vn, kf, vf, mid_s = saved
+    project([near[s : s + 1] for s in range(chips)], gain, wk, wv, kn, vn)
+    project([far[s : s + 1] for s in range(chips)], gain, wk, wv, kf, vf)
+    attend(turns, 0, ids_ref[0], mine, q, (k, ko, kn, kf), (v, vo, vn, vf), wo, outs, mid_s)
+
+
+def later_kernel(chips, turns, turn, ids_ref, *refs):
+    mine, (q, k, v, ko, vo, kn, vn, kf, vf, wo) = refs[:chips], refs[chips : chips + 10]
+    keys, values, outs = (k, ko, kn, kf), (v, vo, vn, vf), refs[chips + 10 : -1]
+    attend(turns, turn, ids_ref[0], mine, q, keys, values, wo, outs, refs[-1])
 
 
 def vmem(count):
@@ -148,63 +142,66 @@
     return jax.ShapeDtypeStruct(sizes, jnp.bfloat16)
 
 
-def saved_shapes(frames, asked, local, chips, width):
-    return [
-        shape(asked, chips * local, width),
-        shape(frames, 2 * chips * local, width),
-        shape(frames, 2 * chips * local, width),
-    ]
-
-
-def spatial_early(mine, other, gain, wq, wk, wv, shards, turns):
+def spatial_ready(mine, gain, wq, wk, wv, turns):
     chips = len(mine)
-    frames, local, width = other.shape[1:]
-    args = (*mine, other, gain, wq, wk, wv)
-    return pl.pallas_call(
-        functools.partial(early_kernel, chips, turns),
+    frames, local, width = mine[0].shape
+    args = (*mine, gain, wq, wk, wv)
+    keys = shape(frames, chips * local, width)
+    return pl.pallas_call(
+        functools.partial(ready_kernel, chips, turns),
         in_specs=vmem(len(args)),
         out_specs=vmem(3),
-        out_shape=saved_shapes(frames, frames, local, chips, width),
+        out_shape=[shape(frames, chips * local, width), keys, keys],
         compiler_params=params(),
-        cost_estimate=cost(EARLY),
-        name="spatial_early",
+        cost_estimate=cost(READY),
+        name="spatial_ready",
     )(*args)
 
 
-def spatial_first(ids, early, late, other, gain, wq, wk, wv, wo, saved, shards, turns):
-    chips = len(early)
-    local, width = early[0].shape[1:]
-    frames, extra = saved[0].shape[0], late[0].shape[0]
+def spatial_rest(other, gain, wk, wv):
+    chips, frames, local, width = other.shape
+    args = (other, gain, wk, wv)
+    return pl.pallas_call(
+        functools.partial(rest_kernel, chips),
+        in_specs=vmem(len(args)),
+        out_specs=vmem(2),
+        out_shape=[shape(frames, chips * local, width)] * 2,
+        compiler_params=params(),
+        cost_estimate=cost(1),
+        name="spatial_rest",
+    )(*args)
+
+
+def spatial_first(ids, mine, near, far, gain, wk, wv, wo, saved, shards, turns):
+    chips = len(mine)
+    frames, local, width = mine[0].shape
     step = local // shards // turns
-    total = frames + extra - 1
-    args = (*early, *late, other, gain, wq, wk, wv, wo, *saved)
-    out = [shape(chips, total, step, width)] * shards
-    out = out + saved_shapes(extra, extra - 1, local, chips, width)
+    args = (*mine, near, far, gain, wk, wv, wo, *saved)
+    out = [shape(chips, frames, step, width)] * shards + [shape(1, chips * local, width)] * 4
     got = pl.pallas_call(
         functools.partial(first_kernel, chips, shards, turns),
         in_specs=[pl.BlockSpec(memory_space=pltpu.SMEM)] + vmem(len(args)),
         out_specs=vmem(len(out)),
         out_shape=out,
-        scratch_shapes=[pltpu.VMEM((total, chips * shards * step, width), jnp.float32)],
+        scratch_shapes=[pltpu.VMEM((frames, chips * shards * step, width), jnp.float32)],
         compiler_params=params(),
-        cost_estimate=cost(7.5),
+        cost_estimate=cost(6.5),
         name="spatial_first",
     )(ids, *args)
     return got[:shards], got[shards:]
 
 
-def spatial_later(ids, early, late, saved, wo, shards, turns, turn):
-    chips = len(early)
-    local, width = early[0].shape[1:]
-    total = saved[0].shape[0] + saved[3].shape[0]
+def spatial_later(ids, mine, saved, wo, shards, turns, turn):
+    chips = len(mine)
+    frames, local, width = mine[0].shape
     step = local // shards // turns
-    args = (*early, *late, *saved, wo)
-    return pl.pallas_call(
-        functools.partial(later_kernel, chips, shards, turns, turn),
+    args = (*mine, *saved, wo)
+    return pl.pallas_call(
+        functools.partial(later_kernel, chips, turns, turn),
         in_specs=[pl.BlockSpec(memory_space=pltpu.SMEM)] + vmem(len(args)),
-        out_specs=vmem(chips),
-        out_shape=[shape(shards, total, step, width)] * chips,
-        scratch_shapes=[pltpu.VMEM((total, chips * shards * step, width), jnp.float32)],
+        out_specs=vmem(shards),
+        out_shape=[shape(chips, frames, step, width)] * shards,
+        scratch_shapes=[pltpu.VMEM((frames, chips * shards * step, width), jnp.float32)],
         compiler_params=params(),
         cost_estimate=cost(LATER),
         name="spatial_later",
@@ -397,38 +394,42 @@
         sent = lax.ppermute(found, "frame", [(i, i + hop) for i in range(0, shards, 2 * hop)])
         found = jnp.where(zf % (2 * hop) == hop, sent, found)
         hop //= 2
-    early_other = swap(jnp.stack([e[:half] for e in early]), "pos", spots, 1)
-    saved = spatial_early(
-        early, early_other, row(gain_one), query_one, key_one, value_one, shards, turns
-    )
-    late = [jnp.concatenate([l, found[s : s + 1]], axis=0) for s, l in enumerate(late)]
-    late_other = swap(jnp.stack(late), "pos", spots, 1)
-    mid, rest = spatial_first(
-        ids, early, late, late_other, row(gain_one), query_one, key_one, value_one, out_one, saved,
-        shards, turns,
+    mine = [jnp.concatenate([e[:half], l], axis=0) for e, l in zip(early, late)]
+    saved = spatial_ready(mine, row(gain_one), query_one, key_one, value_one, turns)
+    rest = spatial_rest(
+        swap(jnp.stack(mine), "pos", spots, 1), row(gain_one), key_one, value_one
     )
     saved = (*saved, *rest)
+    far = swap(found, "pos", spots, 1)
+    mid, ends = spatial_first(
+        ids, mine, found, far, row(gain_one), key_one, value_one, out_one, saved, shards, turns
+    )
+    saved = (*saved, *ends)
     step = share // turns
     flat = lambda v: [m.reshape(m.shape[0], each * step, width) for m in v]
     heads = lambda v: [m[0] for m in v]
     across = lambda v, n: [None] + [jnp.stack([m[i] for m in v]) for i in range(1, n)]
     whole = blank(latents.shape)
     weights = (row(gain_two), query_two, key_two, value_two, out_two)
+    mids = [mid]
+    for turn in range(1, turns):
+        mids.append(spatial_later(ids, mine, saved, out_one, shards, turns, turn))
+    pass
+    got = [over_shards(mid) for mid in mids]
+    done = None
     for turn in range(turns):
-        if turn == 0:
-            got = over_shards(mid)
-            gate = got[1:]
-            got = flat(got)
-            came = over_chips([None] + across(got, chips)[1:])
-        else:
-            mid = spatial_later(ids, early, late, saved, out_one, shards, turns, turn)
-            mid, _ = lax.optimization_barrier((mid, gate[0]))
-            got = flat(over_chips(mid))
-            came = over_shards([None] + across(got, shards)[1:])
+        now = got[turn]
+        if turn + 1 < turns:
+            more = got[turn + 1]
+            now, mids[1] = lax.optimization_barrier((now, mids[1]))
         if turn:
-            came, done = lax.optimization_barrier((came[1:], done))
-            came = [None] + list(came)
-        done = temporal(heads(got), came[1:], *weights, step, turn == 0)
+            now, _ = lax.optimization_barrier((now, done))
+        came = over_chips([None] + across(flat(now), chips)[1:])[1:]
+        if turn + 1 < turns:
+            came, _ = lax.optimization_barrier((came, more[1:3]))
+        if turn:
+            came, done = lax.optimization_barrier((came, done))
+        done = temporal(heads(flat(now)), came, *weights, step, True)
         back = over_shards(done)
         whole = assemble(ids, [d.reshape(chips, each, step, width) for d in back], whole, turn)
     return whole

time: 93.6 us -> 90.2 us (0.964)
  waiting for transfers between devices: 24.6 us -> 18.5 us
  local copies, waits for them, and re-layouts: 1.19 us -> 3.61 us
    ppermute x26, waiting for transfers between devices: 22.3 us -> 13 us  [swap(): return lax.ppermute(value, axis, [(i, i ^ mask) for i in range(size)])]
    ppermute x2, waiting for transfers between devices: 2.32 us -> 5.46 us  [shards_fn(): lax.ppermute(found, 'frame', [(i, i + hop) for i in range(0, shards, 2 *...]
    pallas_call x2 -> x3, Pallas kernels: 7.02 us -> 8.4 us  [the longest x1 6.28 us: spatial_later(): pl.pallas_call(functools.partial(later_kernel, chips, turns, turn), in_sp...]
    pallas_call x1, Pallas kernels: 7.93 us -> 6.58 us  [spatial_first(): pl.pallas_call(functools.partial(first_kernel, chips, shards, turns), in_...]
    unnamed x22 -> x20, local copies, waits for them, and re-layouts: 0.06 us -> 1.32 us
    dynamic_slice x2, local copies, waits for them, and re-layouts: 1.02 us -> 2.18 us  [shards_fn(): lax.dynamic_slice_in_dim(latents, (chip ^ s) * each + part * half, each -...]
  transfers between devices with their start and end apart: 28 -> 28, of which waited for: 11 -> 6; matrix products, arithmetic and copies ran while one was open for 1% -> 2% of each run, Pallas kernels for 13% -> 15%
where the time goes in v3:
time: 90.2 us; the launch traced here: 89.9 us
  starting transfers between devices  45.2 us (50%)
  Pallas kernels  21.5 us (24%)
  waiting for transfers between devices  18.5 us (21%)
  local copies, waits for them, and re-layouts  3.61 us (4%)
    ppermute x26, starting transfers between devices, swap(): return lax.ppermute(value, axis, [(i, i ^ mask) for i in range(size)])  39.2 us
    ppermute x26, waiting for transfers between devices, swap(): return lax.ppermute(value, axis, [(i, i ^ mask) for i in range(size)])  13 us
    pallas_call x1, Pallas kernels, spatial_first(): pl.pallas_call(functools.partial(first_kernel, chips, shards, turns), in_...  6.58 us
    pallas_call x1, Pallas kernels, spatial_later(): pl.pallas_call(functools.partial(later_kernel, chips, turns, turn), in_sp...  6.28 us
    ppermute x2, starting transfers between devices, shards_fn(): lax.ppermute(found, 'frame', [(i, i + hop) for i in range(0, shards, 2 *...  5.95 us
    ppermute x2, waiting for transfers between devices, shards_fn(): lax.ppermute(found, 'frame', [(i, i + hop) for i in range(0, shards, 2 *...  5.46 us
    pallas_call x2, Pallas kernels, temporal(): pl.pallas_call(functools.partial(temporal_kernel, chips, shards, share, b...  3.73 us
    pallas_call x2, Pallas kernels, assemble(): pl.pallas_call(functools.partial(assemble_kernel, turn), in_specs=[pl.Blo...  2.82 us
  transfers between devices with their start and end apart: 28, of which 6 were waited for; matrix products, arithmetic and copies ran while one was open for 2% of the time, Pallas kernels for 15%

profile of v3, /device:TPU:0, one launch (start us, length us, event | category | flops | bytes accessed | tf_op | source)
XLA Modules:
  0.0 89.9 jit_solution(360399570806761059)
XLA Ops:
  0.0 0.8 constant_dynamic-slice_fusion.1
  0.9 3.0 %collective-permute-start = (bf16[2,64,256]{2,1,0:T(8,128)(2,1)S(1)}, bf16[2,64,256]{2,1,0:T(8,128)(2,1)S(1)}, u32[]{:S(2)}, u32[]{:S(2)}) collective-permute-start(bf16[2,64,256]{2,1,0:T(8,128)(2,1)S(1)} %get-tuple-element.140), channel_id=1, source_target_pairs={{0,2},{1,3},{2,0},{3,1},{4,6},{5,7},{6,4},{7,5},{8,10},{9,11},{10,... | collective-permute-start | bytes 196616 | tf_op jit(solution)/shard_map/ppermute | solution.py:354
  3.9 1.5 %collective-permute-start.2 = (bf16[2,64,256]{2,1,0:T(8,128)(2,1)S(1)}, bf16[2,64,256]{2,1,0:T(8,128)(2,1)S(1)}, u32[]{:S(2)}, u32[]{:S(2)}) collective-permute-start(bf16[2,64,256]{2,1,0:T(8,128)(2,1)S(1)} %get-tuple-element.139), channel_id=1, source_target_pairs={{0,4},{1,5},{2,6},{3,7},{4,0},{5,1},{6,2},{7,3},{8,12},{9,13},{10,... | collective-permute-start | bytes 196616 | tf_op jit(solution)/shard_map/ppermute | solution.py:354
  5.4 0.0 collective-permute-start.4
  5.4 1.3 %constant_dynamic-slice_fusion = (bf16[7,64,256]{2,1,0:T(8,128)(2,1)S(1)}, bf16[7,64,256]{2,1,0:T(8,128)(2,1)S(1)}, bf16[7,64,256]{2,1,0:T(8,128)(2,1)S(1)}, bf16[7,64,256]{2,1,0:T(8,128)(2,1)S(1)}) fusion(bf16[32,64,256]{2,1,0:T(8,128)(2,1)} %param.11, s32[]{:T(128)S(6)} %select_n.61, s32[]{:T(128)S(6)} %select_n.59, s32[]{:T(128)S(6)} %select_n.57, ...), kind=kLoop, calls=%fused_computation.49 | loop fusion | bytes 1835024 | tf_op jit(solution)/shard_map/dynamic_slice | solution.py:385
  6.8 2.0 %collective-permute-start.3 = (bf16[7,64,256]{2,1,0:T(8,128)(2,1)S(1)}, bf16[7,64,256]{2,1,0:T(8,128)(2,1)S(1)}, u32[]{:S(2)}, u32[]{:S(2)}) collective-permute-start(bf16[7,64,256]{2,1,0:T(8,128)(2,1)S(1)} %get-tuple-element.89), channel_id=1, source_target_pairs={{0,4},{1,5},{2,6},{3,7},{4,0},{5,1},{6,2},{7,3},{8,12},{9,13},{10,... | collective-permute-start | bytes 688136 | tf_op jit(solution)/shard_map/ppermute | solution.py:354
  8.8 1.4 %collective-permute-start.5 = (bf16[7,64,256]{2,1,0:T(8,128)(2,1)S(1)}, bf16[7,64,256]{2,1,0:T(8,128)(2,1)S(1)}, u32[]{:S(2)}, u32[]{:S(2)}) collective-permute-start(bf16[7,64,256]{2,1,0:T(8,128)(2,1)S(1)} %get-tuple-element.88), channel_id=1, source_target_pairs={{0,6},{1,7},{2,4},{3,5},{4,2},{5,3},{6,0},{7,1},{8,14},{9,15},{10,... | collective-permute-start | bytes 688136 | tf_op jit(solution)/shard_map/ppermute | solution.py:354
  10.2 0.1 collective-permute-start.1
  10.4 0.3 collective-permute-done.4
  10.7 4.7 %collective-permute-start.7 = (bf16[4,64,256]{2,1,0:T(8,128)(2,1)S(1)}, bf16[4,64,256]{2,1,0:T(8,128)(2,1)S(1)}, u32[]{:S(2)}, u32[]{:S(2)}) collective-permute-start(bf16[4,64,256]{2,1,0:T(8,128)(2,1)S(1)} %pad_maximum_fusion.5), channel_id=1, source_target_pairs={{0,16},{1,17},{2,18},{3,19},{4,20},{5,21},{6,22},{7,23}} | collective-permute-start | bytes 393224 | tf_op jit(solution)/shard_map/ppermute | solution.py:394
  15.4 0.1 pad_add_fusion.ids_ref
  15.5 3.4 %collective-permute-done.7 = bf16[4,64,256]{2,1,0:T(8,128)(2,1)S(1)} collective-permute-done((bf16[4,64,256]{2,1,0:T(8,128)(2,1)S(1)}, bf16[4,64,256]{2,1,0:T(8,128)(2,1)S(1)}, u32[]{:S(2)}, u32[]{:S(2)}) %collective-permute-start.7) | collective-permute-done | bytes 131104 | tf_op jit(solution)/shard_map/ppermute | solution.py:394
  18.9 1.3 %collective-permute-start.8 = (bf16[4,64,256]{2,1,0:T(8,128)(2,1)S(1)}, bf16[4,64,256]{2,1,0:T(8,128)(2,1)S(1)}, u32[]{:S(2)}, u32[]{:S(2)}) collective-permute-start(bf16[4,64,256]{2,1,0:T(8,128)(2,1)S(1)} %broadcast_select_fusion), channel_id=1, source_target_pairs={{0,8},{16,24},{1,9},{17,25},{2,10},{18,26},{3,11},{19,27},{4,12},{... | collective-permute-start | bytes 393224 | tf_op jit(solution)/shard_map/ppermute | solution.py:394
  20.4 0.1 pad_maximum_fusion
  20.5 0.0 copy-start
  20.5 0.1 collective-permute-start.6
  20.6 2.1 %collective-permute-done.8 = bf16[4,64,256]{2,1,0:T(8,128)(2,1)S(1)} collective-permute-done((bf16[4,64,256]{2,1,0:T(8,128)(2,1)S(1)}, bf16[4,64,256]{2,1,0:T(8,128)(2,1)S(1)}, u32[]{:S(2)}, u32[]{:S(2)}) %collective-permute-start.8) | collective-permute-done | bytes 131104 | tf_op jit(solution)/shard_map/ppermute | solution.py:394
  22.7 0.1 collective-permute-start.9
  22.9 0.6 copy-done.8
  23.5 1.2 %spatial_ready.1 = (bf16[8,256,256]{2,1,0:T(8,128)(2,1)S(1)}, bf16[8,256,256]{2,1,0:T(8,128)(2,1)S(1)}, bf16[8,256,256]{2,1,0:T(8,128)(2,1)S(1)}) custom-call(bf16[8,64,256]{2,1,0:T(8,128)(2,1)S(1)} %get-tuple-element.93.refs_0_, bf16[8,64,256]{2,1,0:T(8,128)(2,1)S(1)} %get-tuple-element.95.refs_1_, bf16[8,64,256]{2,1,0:T(8,128)(2,1)S(1)} %get-tuple-element.97.refs_2_, ...), custom_call_target="tpu_custom_call" | custom-call | flops 40000000000 | bytes 144000000 | tf_op jit(solution)/shard_map/spatial_ready/pallas_call | solution.py:150
  24.7 0.9 %spatial_rest.1 = (bf16[8,256,256]{2,1,0:T(8,128)(2,1)S(1)}, bf16[8,256,256]{2,1,0:T(8,128)(2,1)S(1)}) custom-call(bf16[4,8,64,256]{3,2,1,0:T(8,128)(2,1)S(1)} %collective-permute-done.6.other, f32[1,256]{1,0:T(1,128)S(1)} %bitcast.91, bf16[256,256]{1,0:T(8,128)(2,1)S(1)} %copy-done.1, bf16[256,256]{1,0:T(8,128)(2,1)S(1)} %copy-done.2), custom_call_target="tpu_custom_call" | custom-call | flops 1000000000 | bytes 3600000 | tf_op jit(solution)/shard_map/spatial_rest/pallas_call | solution.py:164
  25.7 6.6 %spatial_first.1 = (bf16[4,8,8,256]{3,2,1,0:T(8,128)(2,1)S(1)}, bf16[4,8,8,256]{3,2,1,0:T(8,128)(2,1)S(1)}, bf16[4,8,8,256]{3,2,1,0:T(8,128)(2,1)S(1)}, bf16[4,8...) custom-call(s32[2]{0:T(128)S(1)} %pad_add_fusion.ids_ref, ...), custom_call_target="tpu_custom_call" | custom-call | flops 6499999744 | bytes 23400000 | tf_op jit(solution)/shard_map/spatial_first/pallas_call | solution.py:181
  32.3 2.5 %collective-permute-start.13 = (bf16[4,8,8,256]{3,2,1,0:T(8,128)(2,1)S(1)}, bf16[4,8,8,256]{3,2,1,0:T(8,128)(2,1)S(1)}, u32[]{:S(2)}, u32[]{:S(2)}) collective-permute-start(bf16[4,8,8,256]{3,2,1,0:T(8,128)(2,1)S(1)} %get-tuple-element.58), channel_id=1, source_target_pairs={{0,8},{8,0},{16,24},{24,16},{1,9},{9,1},{17,25},{25,17},{2,10},{10... | collective-permute-start | bytes 393224 | tf_op jit(solution)/shard_map/ppermute | solution.py:354
  34.8 3.4 %collective-permute-start.14 = (bf16[4,8,8,256]{3,2,1,0:T(8,128)(2,1)S(1)}, bf16[4,8,8,256]{3,2,1,0:T(8,128)(2,1)S(1)}, u32[]{:S(2)}, u32[]{:S(2)}) collective-permute-start(bf16[4,8,8,256]{3,2,1,0:T(8,128)(2,1)S(1)} %get-tuple-element.59), channel_id=1, source_target_pairs={{0,16},{8,24},{16,0},{24,8},{1,17},{9,25},{17,1},{25,9},{2,18},{10... | collective-permute-start | bytes 393224 | tf_op jit(solution)/shard_map/ppermute | solution.py:354
  38.2 6.3 %spatial_later.1 = (bf16[4,8,8,256]{3,2,1,0:T(8,128)(2,1)S(1)}, bf16[4,8,8,256]{3,2,1,0:T(8,128)(2,1)S(1)}, bf16[4,8,8,256]{3,2,1,0:T(8,128)(2,1)S(1)}, bf16[4,8,8,256]{3,2,1,0:T(8,128)(2,1)S(1)}) custom-call(s32[2]{0:T(128)S(1)} %pad_add_fusion.ids_ref, bf16[8,64,256]{2,1,0:T(8,128)(2,1)S(1)} %get-tuple-element.93.refs_0_, ...), custom_call_target="tpu_custom_call" | custom-call | flops 6400000000 | bytes 23040000 | tf_op jit(solution)/shard_map/spatial_later/pallas_call | solution.py:199
  44.4 0.6 collective-permute-start.10
  45.1 3.8 %collective-permute-start.11 = (bf16[4,8,8,256]{3,2,1,0:T(8,128)(2,1)S(1)}, bf16[4,8,8,256]{3,2,1,0:T(8,128)(2,1)S(1)}, u32[]{:S(2)}, u32[]{:S(2)}) collective-permute-start(bf16[4,8,8,256]{3,2,1,0:T(8,128)(2,1)S(1)} %get-tuple-element.55), channel_id=1, source_target_pairs={{0,16},{8,24},{16,0},{24,8},{1,17},{9,25},{17,1},{25,9},{2,18},{10... | collective-permute-start | bytes 393224 | tf_op jit(solution)/shard_map/ppermute | solution.py:354
  49.0 2.5 %collective-permute-start.18 = (bf16[4,64,256]{2,1,0:T(8,128)(2,1)S(1)}, bf16[4,64,256]{2,1,0:T(8,128)(2,1)S(1)}, u32[]{:S(2)}, u32[]{:S(2)}) collective-permute-start(bf16[4,64,256]{2,1,0:T(8,128)(2,1)S(1)} %pad_maximum_fusion.8), channel_id=1, source_target_pairs={{0,6},{1,7},{2,4},{3,5},{4,2},{5,3},{6,0},{7,1},{8,14},{9,15},{10,... | collective-permute-start | bytes 393224 | tf_op jit(solution)/shard_map/ppermute | solution.py:354
  51.5 0.6 collective-permute-start.17
  52.1 0.6 collective-permute-start.16
  52.7 1.6 %collective-permute-start.12 = (bf16[4,8,8,256]{3,2,1,0:T(8,128)(2,1)S(1)}, bf16[4,8,8,256]{3,2,1,0:T(8,128)(2,1)S(1)}, u32[]{:S(2)}, u32[]{:S(2)}) collective-permute-start(bf16[4,8,8,256]{3,2,1,0:T(8,128)(2,1)S(1)} %get-tuple-element.56), channel_id=1, source_target_pairs={{0,24},{8,16},{16,8},{24,0},{1,25},{9,17},{17,9},{25,1},{2,26},{10... | collective-permute-start | bytes 393224 | tf_op jit(solution)/shard_map/ppermute | solution.py:354
  54.3 3.5 %collective-permute-done.11 = bf16[4,8,8,256]{3,2,1,0:T(8,128)(2,1)S(1)} collective-permute-done((bf16[4,8,8,256]{3,2,1,0:T(8,128)(2,1)S(1)}, bf16[4,8,8,256]{3,2,1,0:T(8,128)(2,1)S(1)}, u32[]{:S(2)}, u32[]{:S(2)}) %collective-permute-start.11) | collective-permute-done | bytes 131104 | tf_op jit(solution)/shard_map/ppermute | solution.py:354
  57.9 0.6 copy-done.9
  58.6 1.9 %temporal.2 = (bf16[4,64,256]{2,1,0:T(8,128)(2,1)S(1)}, bf16[4,64,256]{2,1,0:T(8,128)(2,1)S(1)}, bf16[4,64,256]{2,1,0:T(8,128)(2,1)S(1)}, bf16[4,64,256]{2,1,0:T(8,128)(2,1)S(1)}) custom-call(bf16[64,256]{1,0:T(8,128)(2,1)S(1)} %get-tuple-element.145.refs_0_, bf16[64,256]{1,0:T(8,128)(2,1)S(1)} %get-tuple-element.123.refs_1_, ...), custom_call_target="tpu_custom_call" | custom-call | flops 1900000000 | bytes 6840000 | tf_op jit(solution)/shard_map/temporal/pallas_call | solution.py:287
  60.6 2.5 %collective-permute-start.21 = (bf16[4,64,256]{2,1,0:T(8,128)(2,1)S(1)}, bf16[4,64,256]{2,1,0:T(8,128)(2,1)S(1)}, u32[]{:S(2)}, u32[]{:S(2)}) collective-permute-start(bf16[4,64,256]{2,1,0:T(8,128)(2,1)S(1)} %pad_maximum_fusion.11), channel_id=1, source_target_pairs={{0,6},{1,7},{2,4},{3,5},{4,2},{5,3},{6,0},{7,1},{8,14},{9,15},{10,... | collective-permute-start | bytes 393224 | tf_op jit(solution)/shard_map/ppermute | solution.py:354
  63.1 0.6 collective-permute-start.20
  63.7 0.6 collective-permute-start.19
  64.3 3.5 %collective-permute-start.25 = (bf16[4,64,256]{2,1,0:T(8,128)(2,1)S(1)}, bf16[4,64,256]{2,1,0:T(8,128)(2,1)S(1)}, u32[]{:S(2)}, u32[]{:S(2)}) collective-permute-start(bf16[4,64,256]{2,1,0:T(8,128)(2,1)S(1)} %get-tuple-element.69), channel_id=1, source_target_pairs={{0,8},{8,0},{16,24},{24,16},{1,9},{9,1},{17,25},{25,17},{2,10},{10... | collective-permute-start | bytes 393224 | tf_op jit(solution)/shard_map/ppermute | solution.py:354
  67.8 2.1 %collective-permute-start.26 = (bf16[4,64,256]{2,1,0:T(8,128)(2,1)S(1)}, bf16[4,64,256]{2,1,0:T(8,128)(2,1)S(1)}, u32[]{:S(2)}, u32[]{:S(2)}) collective-permute-start(bf16[4,64,256]{2,1,0:T(8,128)(2,1)S(1)} %get-tuple-element.70), channel_id=1, source_target_pairs={{0,16},{8,24},{16,0},{24,8},{1,17},{9,25},{17,1},{25,9},{2,18},{10... | collective-permute-start | bytes 393224 | tf_op jit(solution)/shard_map/ppermute | solution.py:354
  69.9 1.6 %collective-permute-start.27 = (bf16[4,64,256]{2,1,0:T(8,128)(2,1)S(1)}, bf16[4,64,256]{2,1,0:T(8,128)(2,1)S(1)}, u32[]{:S(2)}, u32[]{:S(2)}) collective-permute-start(bf16[4,64,256]{2,1,0:T(8,128)(2,1)S(1)} %get-tuple-element.71), channel_id=1, source_target_pairs={{0,24},{8,16},{16,8},{24,0},{1,25},{9,17},{17,9},{25,1},{2,26},{10... | collective-permute-start | bytes 393224 | tf_op jit(solution)/shard_map/ppermute | solution.py:354
  71.5 1.9 %temporal.3 = (bf16[4,64,256]{2,1,0:T(8,128)(2,1)S(1)}, bf16[4,64,256]{2,1,0:T(8,128)(2,1)S(1)}, bf16[4,64,256]{2,1,0:T(8,128)(2,1)S(1)}, bf16[4,64,256]{2,1,0:T(8,128)(2,1)S(1)}) custom-call(bf16[64,256]{1,0:T(8,128)(2,1)S(1)} %get-tuple-element.103.refs_0_, bf16[64,256]{1,0:T(8,128)(2,1)S(1)} %get-tuple-element.107.refs_1_, ...), custom_call_target="tpu_custom_call" | custom-call | flops 1900000000 | bytes 6840000 | tf_op jit(solution)/shard_map/temporal/pallas_call | solution.py:287
  73.3 1.3 %collective-permute-start.22 = (bf16[4,64,256]{2,1,0:T(8,128)(2,1)S(1)}, bf16[4,64,256]{2,1,0:T(8,128)(2,1)S(1)}, u32[]{:S(2)}, u32[]{:S(2)}) collective-permute-start(bf16[4,64,256]{2,1,0:T(8,128)(2,1)S(1)} %get-tuple-element.80), channel_id=1, source_target_pairs={{0,8},{8,0},{16,24},{24,16},{1,9},{9,1},{17,25},{25,17},{2,10},{10... | collective-permute-start | bytes 393224 | tf_op jit(solution)/shard_map/ppermute | solution.py:354
  74.7 1.6 %collective-permute-start.23 = (bf16[4,64,256]{2,1,0:T(8,128)(2,1)S(1)}, bf16[4,64,256]{2,1,0:T(8,128)(2,1)S(1)}, u32[]{:S(2)}, u32[]{:S(2)}) collective-permute-start(bf16[4,64,256]{2,1,0:T(8,128)(2,1)S(1)} %get-tuple-element.81), channel_id=1, source_target_pairs={{0,16},{8,24},{16,0},{24,8},{1,17},{9,25},{17,1},{25,9},{2,18},{10... | collective-permute-start | bytes 393224 | tf_op jit(solution)/shard_map/ppermute | solution.py:354
  76.2 1.6 %collective-permute-start.24 = (bf16[4,64,256]{2,1,0:T(8,128)(2,1)S(1)}, bf16[4,64,256]{2,1,0:T(8,128)(2,1)S(1)}, u32[]{:S(2)}, u32[]{:S(2)}) collective-permute-start(bf16[4,64,256]{2,1,0:T(8,128)(2,1)S(1)} %get-tuple-element.82), channel_id=1, source_target_pairs={{0,24},{8,16},{16,8},{24,0},{1,25},{9,17},{17,9},{25,1},{2,26},{10... | collective-permute-start | bytes 393224 | tf_op jit(solution)/shard_map/ppermute | solution.py:354
  77.8 3.3 %collective-permute-done.27 = bf16[4,64,256]{2,1,0:T(8,128)(2,1)S(1)} collective-permute-done((bf16[4,64,256]{2,1,0:T(8,128)(2,1)S(1)}, bf16[4,64,256]{2,1,0:T(8,128)(2,1)S(1)}, u32[]{:S(2)}, u32[]{:S(2)}) %collective-permute-start.27) | collective-permute-done | bytes 131104 | tf_op jit(solution)/shard_map/ppermute | solution.py:354
  81.1 1.4 %assemble.2.refs_4_ = bf16[32,64,256]{2,1,0:T(8,128)(2,1)} custom-call(s32[2]{0:T(128)S(1)} %pad_add_fusion.ids_ref, bf16[4,8,8,256]{3,2,1,0:T(8,128)(2,1)S(1)} %bitcast.95, bf16[4,8,8,256]{3,2,1,0:T(8,128)(2,1)S(1)} %bitcast.84, bf16[4,8,8,256]{3,2,1,0:T(8,128)(2,1)S(1)} %bitcast.85, ...), custom_call_target="tpu_custom_call", output_to_operand_aliasing={{}: (5, {})} | custom-call | flops 60000002048 | bytes 216000000 | tf_op jit(solution)/shard_map/assemble/pallas_call | solution.py:326
  82.5 5.8 %collective-permute-done.23 = bf16[4,64,256]{2,1,0:T(8,128)(2,1)S(1)} collective-permute-done((bf16[4,64,256]{2,1,0:T(8,128)(2,1)S(1)}, bf16[4,64,256]{2,1,0:T(8,128)(2,1)S(1)}, u32[]{:S(2)}, u32[]{:S(2)}) %collective-permute-start.23) | collective-permute-done | bytes 131104 | tf_op jit(solution)/shard_map/ppermute | solution.py:354
  88.4 1.4 %assemble.3 = bf16[32,64,256]{2,1,0:T(8,128)(2,1)} custom-call(s32[2]{0:T(128)S(1)} %pad_add_fusion.ids_ref, bf16[4,8,8,256]{3,2,1,0:T(8,128)(2,1)S(1)} %bitcast.96, bf16[4,8,8,256]{3,2,1,0:T(8,128)(2,1)S(1)} %bitcast.87, bf16[4,8,8,256]{3,2,1,0:T(8,128)(2,1)S(1)} %bitcast.88, bf16[4,8,8,256]{3,2,1,0:T(8,128)(2,1)S(1)} %bitcast.89, ...), custom_call_target="tpu_custom_call", output_to_operand_aliasing={{}: (5, {})} | custom-call | flops 1000000000 | bytes 3600000 | tf_op jit(solution)/shard_map/assemble/pallas_call | solution.py:326
  (64 shorter events, 0.6 us)
Async XLA Ops:
  0.9 9.4 %collective-permute-start = (bf16[2,64,256]{2,1,0:T(8,128)(2,1)S(1)}, bf16[2,64,256]{2,1,0:T(8,128)(2,1)S(1)}, u32[]{:S(2)}, u32[]{:S(2)}) collective-permute-start(bf16[2,64,256]{2,1,0:T(8,128)(2,1)S(1)} %get-tuple-element.140), channel_id=1, source_target_pairs={{0,2},{1,3},{2,0},{3,1},{4,6},{5,7},{6,4},{7,5},{8,10},{9,11},{10,... | collective-permute-start | bytes 196616 | tf_op jit(solution)/shard_map/ppermute | solution.py:354
  3.9 6.5 %collective-permute-start.2 = (bf16[2,64,256]{2,1,0:T(8,128)(2,1)S(1)}, bf16[2,64,256]{2,1,0:T(8,128)(2,1)S(1)}, u32[]{:S(2)}, u32[]{:S(2)}) collective-permute-start(bf16[2,64,256]{2,1,0:T(8,128)(2,1)S(1)} %get-tuple-element.139), channel_id=1, source_target_pairs={{0,4},{1,5},{2,6},{3,7},{4,0},{5,1},{6,2},{7,3},{8,12},{9,13},{10,... | collective-permute-start | bytes 196616 | tf_op jit(solution)/shard_map/ppermute | solution.py:354
  5.4 5.3 %collective-permute-start.4 = (bf16[2,64,256]{2,1,0:T(8,128)(2,1)S(1)}, bf16[2,64,256]{2,1,0:T(8,128)(2,1)S(1)}, u32[]{:S(2)}, u32[]{:S(2)}) collective-permute-start(bf16[2,64,256]{2,1,0:T(8,128)(2,1)S(1)} %get-tuple-element.138), channel_id=1, source_target_pairs={{0,6},{1,7},{2,4},{3,5},{4,2},{5,3},{6,0},{7,1},{8,14},{9,15},{10,... | collective-permute-start | bytes 196616 | tf_op jit(solution)/shard_map/ppermute | solution.py:354
  6.8 13.4 %collective-permute-start.3 = (bf16[7,64,256]{2,1,0:T(8,128)(2,1)S(1)}, bf16[7,64,256]{2,1,0:T(8,128)(2,1)S(1)}, u32[]{:S(2)}, u32[]{:S(2)}) collective-permute-start(bf16[7,64,256]{2,1,0:T(8,128)(2,1)S(1)} %get-tuple-element.89), channel_id=1, source_target_pairs={{0,4},{1,5},{2,6},{3,7},{4,0},{5,1},{6,2},{7,3},{8,12},{9,13},{10,... | collective-permute-start | bytes 688136 | tf_op jit(solution)/shard_map/ppermute | solution.py:354
  8.8 11.5 %collective-permute-start.5 = (bf16[7,64,256]{2,1,0:T(8,128)(2,1)S(1)}, bf16[7,64,256]{2,1,0:T(8,128)(2,1)S(1)}, u32[]{:S(2)}, u32[]{:S(2)}) collective-permute-start(bf16[7,64,256]{2,1,0:T(8,128)(2,1)S(1)} %get-tuple-element.88), channel_id=1, source_target_pairs={{0,6},{1,7},{2,4},{3,5},{4,2},{5,3},{6,0},{7,1},{8,14},{9,15},{10,... | collective-permute-start | bytes 688136 | tf_op jit(solution)/shard_map/ppermute | solution.py:354
  10.2 10.1 %collective-permute-start.1 = (bf16[7,64,256]{2,1,0:T(8,128)(2,1)S(1)}, bf16[7,64,256]{2,1,0:T(8,128)(2,1)S(1)}, u32[]{:S(2)}, u32[]{:S(2)}) collective-permute-start(bf16[7,64,256]{2,1,0:T(8,128)(2,1)S(1)} %get-tuple-element.90), channel_id=1, source_target_pairs={{0,2},{1,3},{2,0},{3,1},{4,6},{5,7},{6,4},{7,5},{8,10},{9,11},{10,... | collective-permute-start | bytes 688136 | tf_op jit(solution)/shard_map/ppermute | solution.py:354
  10.7 8.2 %collective-permute-start.7 = (bf16[4,64,256]{2,1,0:T(8,128)(2,1)S(1)}, bf16[4,64,256]{2,1,0:T(8,128)(2,1)S(1)}, u32[]{:S(2)}, u32[]{:S(2)}) collective-permute-start(bf16[4,64,256]{2,1,0:T(8,128)(2,1)S(1)} %pad_maximum_fusion.5), channel_id=1, source_target_pairs={{0,16},{1,17},{2,18},{3,19},{4,20},{5,21},{6,22},{7,23}} | collective-permute-start | bytes 393224 | tf_op jit(solution)/shard_map/ppermute | solution.py:394
  18.9 3.8 %collective-permute-start.8 = (bf16[4,64,256]{2,1,0:T(8,128)(2,1)S(1)}, bf16[4,64,256]{2,1,0:T(8,128)(2,1)S(1)}, u32[]{:S(2)}, u32[]{:S(2)}) collective-permute-start(bf16[4,64,256]{2,1,0:T(8,128)(2,1)S(1)} %broadcast_select_fusion), channel_id=1, source_target_pairs={{0,8},{16,24},{1,9},{17,25},{2,10},{18,26},{3,11},{19,27},{4,12},{... | collective-permute-start | bytes 393224 | tf_op jit(solution)/shard_map/ppermute | solution.py:394
  20.5 2.3 %copy-start = (bf16[256,256]{1,0:T(8,128)(2,1)S(1)}, bf16[256,256]{1,0:T(8,128)(2,1)}, u32[]{:S(2)}) copy-start(bf16[256,256]{1,0:T(8,128)(2,1)} %refs_5_.1) | copy-start | bytes 393220
  20.5 2.3 %copy-start.1 = (bf16[256,256]{1,0:T(8,128)(2,1)S(1)}, bf16[256,256]{1,0:T(8,128)(2,1)}, u32[]{:S(2)}) copy-start(bf16[256,256]{1,0:T(8,128)(2,1)} %refs_7_.3) | copy-start | bytes 393220
  20.5 2.3 %copy-start.2 = (bf16[256,256]{1,0:T(8,128)(2,1)S(1)}, bf16[256,256]{1,0:T(8,128)(2,1)}, u32[]{:S(2)}) copy-start(bf16[256,256]{1,0:T(8,128)(2,1)} %refs_8_.3) | copy-start | bytes 393220
  20.5 4.2 %collective-permute-start.6 = (bf16[4,8,64,256]{3,2,1,0:T(8,128)(2,1)S(1)}, bf16[4,8,64,256]{3,2,1,0:T(8,128)(2,1)S(1)}, u32[]{:S(2)}, u32[]{:S(2)}) collective-permute-start(bf16[4,8,64,256]{3,2,1,0:T(8,128)(2,1)S(1)} %pad_maximum_fusion), channel_id=1, source_target_pairs={{0,1},{1,0},{2,3},{3,2},{4,5},{5,4},{6,7},{7,6},{8,9},{9,8},{10,11... | collective-permute-start | bytes 3145736 | tf_op jit(solution)/shard_map/ppermute | solution.py:354
  22.7 2.9 %collective-permute-start.9 = (bf16[4,64,256]{2,1,0:T(8,128)(2,1)S(1)}, bf16[4,64,256]{2,1,0:T(8,128)(2,1)S(1)}, u32[]{:S(2)}, u32[]{:S(2)}) collective-permute-start(bf16[4,64,256]{2,1,0:T(8,128)(2,1)S(1)} %broadcast_select_fusion.1.refs_4_), channel_id=1, source_target_pairs={{0,1},{1,0},{2,3},{3,2},{4,5},{5,4},{6,7},{7,6},{8,9},{9,8},{10,11... | collective-permute-start | bytes 393224 | tf_op jit(solution)/shard_map/ppermute | solution.py:354
  22.8 0.7 copy-start.8
  24.7 1.0 %copy-start.3 = (bf16[256,256]{1,0:T(8,128)(2,1)S(1)}, bf16[256,256]{1,0:T(8,128)(2,1)}, u32[]{:S(2)}) copy-start(bf16[256,256]{1,0:T(8,128)(2,1)} %refs_13_.1) | copy-start | bytes 393220
  32.3 16.6 %collective-permute-start.13 = (bf16[4,8,8,256]{3,2,1,0:T(8,128)(2,1)S(1)}, bf16[4,8,8,256]{3,2,1,0:T(8,128)(2,1)S(1)}, u32[]{:S(2)}, u32[]{:S(2)}) collective-permute-start(bf16[4,8,8,256]{3,2,1,0:T(8,128)(2,1)S(1)} %get-tuple-element.58), channel_id=1, source_target_pairs={{0,8},{8,0},{16,24},{24,16},{1,9},{9,1},{17,25},{25,17},{2,10},{10... | collective-permute-start | bytes 393224 | tf_op jit(solution)/shard_map/ppermute | solution.py:354
  34.8 14.2 %collective-permute-start.14 = (bf16[4,8,8,256]{3,2,1,0:T(8,128)(2,1)S(1)}, bf16[4,8,8,256]{3,2,1,0:T(8,128)(2,1)S(1)}, u32[]{:S(2)}, u32[]{:S(2)}) collective-permute-start(bf16[4,8,8,256]{3,2,1,0:T(8,128)(2,1)S(1)} %get-tuple-element.59), channel_id=1, source_target_pairs={{0,16},{8,24},{16,0},{24,8},{1,17},{9,25},{17,1},{25,9},{2,18},{10... | collective-permute-start | bytes 393224 | tf_op jit(solution)/shard_map/ppermute | solution.py:354
  38.2 10.8 %collective-permute-start.15 = (bf16[4,8,8,256]{3,2,1,0:T(8,128)(2,1)S(1)}, bf16[4,8,8,256]{3,2,1,0:T(8,128)(2,1)S(1)}, u32[]{:S(2)}, u32[]{:S(2)}) collective-permute-start(bf16[4,8,8,256]{3,2,1,0:T(8,128)(2,1)S(1)} %get-tuple-element.60), channel_id=1, source_target_pairs={{0,24},{8,16},{16,8},{24,0},{1,25},{9,17},{17,9},{25,1},{2,26},{10... | collective-permute-start | bytes 393224 | tf_op jit(solution)/shard_map/ppermute | solution.py:354
  38.2 19.7 %copy-start.6 = (bf16[256,256]{1,0:T(8,128)(2,1)S(1)}, bf16[256,256]{1,0:T(8,128)(2,1)}, u32[]{:S(2)}) copy-start(bf16[256,256]{1,0:T(8,128)(2,1)} %refs_10_.3) | copy-start | bytes 393220
  38.2 19.7 %copy-start.7 = (bf16[256,256]{1,0:T(8,128)(2,1)S(1)}, bf16[256,256]{1,0:T(8,128)(2,1)}, u32[]{:S(2)}) copy-start(bf16[256,256]{1,0:T(8,128)(2,1)} %refs_11_.3) | copy-start | bytes 393220
  44.4 8.3 %collective-permute-start.10 = (bf16[4,8,8,256]{3,2,1,0:T(8,128)(2,1)S(1)}, bf16[4,8,8,256]{3,2,1,0:T(8,128)(2,1)S(1)}, u32[]{:S(2)}, u32[]{:S(2)}) collective-permute-start(bf16[4,8,8,256]{3,2,1,0:T(8,128)(2,1)S(1)} %get-tuple-element.54), channel_id=1, source_target_pairs={{0,8},{8,0},{16,24},{24,16},{1,9},{9,1},{17,25},{25,17},{2,10},{10... | collective-permute-start | bytes 393224 | tf_op jit(solution)/shard_map/ppermute | solution.py:354
  45.1 12.8 %collective-permute-start.11 = (bf16[4,8,8,256]{3,2,1,0:T(8,128)(2,1)S(1)}, bf16[4,8,8,256]{3,2,1,0:T(8,128)(2,1)S(1)}, u32[]{:S(2)}, u32[]{:S(2)}) collective-permute-start(bf16[4,8,8,256]{3,2,1,0:T(8,128)(2,1)S(1)} %get-tuple-element.55), channel_id=1, source_target_pairs={{0,16},{8,24},{16,0},{24,8},{1,17},{9,25},{17,1},{25,9},{2,18},{10... | collective-permute-start | bytes 393224 | tf_op jit(solution)/shard_map/ppermute | solution.py:354
  49.0 8.9 %collective-permute-start.18 = (bf16[4,64,256]{2,1,0:T(8,128)(2,1)S(1)}, bf16[4,64,256]{2,1,0:T(8,128)(2,1)S(1)}, u32[]{:S(2)}, u32[]{:S(2)}) collective-permute-start(bf16[4,64,256]{2,1,0:T(8,128)(2,1)S(1)} %pad_maximum_fusion.8), channel_id=1, source_target_pairs={{0,6},{1,7},{2,4},{3,5},{4,2},{5,3},{6,0},{7,1},{8,14},{9,15},{10,... | collective-permute-start | bytes 393224 | tf_op jit(solution)/shard_map/ppermute | solution.py:354
  51.5 6.4 %collective-permute-start.17 = (bf16[4,64,256]{2,1,0:T(8,128)(2,1)S(1)}, bf16[4,64,256]{2,1,0:T(8,128)(2,1)S(1)}, u32[]{:S(2)}, u32[]{:S(2)}) collective-permute-start(bf16[4,64,256]{2,1,0:T(8,128)(2,1)S(1)} %pad_maximum_fusion.7), channel_id=1, source_target_pairs={{0,4},{1,5},{2,6},{3,7},{4,0},{5,1},{6,2},{7,3},{8,12},{9,13},{10,... | collective-permute-start | bytes 393224 | tf_op jit(solution)/shard_map/ppermute | solution.py:354
  52.1 5.8 %copy-start.4 = (bf16[256,256]{1,0:T(8,128)(2,1)S(1)}, bf16[256,256]{1,0:T(8,128)(2,1)}, u32[]{:S(2)}) copy-start(bf16[256,256]{1,0:T(8,128)(2,1)} %refs_8_.5) | copy-start | bytes 393220
  52.1 5.8 %copy-start.5 = (bf16[256,256]{1,0:T(8,128)(2,1)S(1)}, bf16[256,256]{1,0:T(8,128)(2,1)}, u32[]{:S(2)}) copy-start(bf16[256,256]{1,0:T(8,128)(2,1)} %refs_9_.5) | copy-start | bytes 393220
  52.1 5.8 %collective-permute-start.16 = (bf16[4,64,256]{2,1,0:T(8,128)(2,1)S(1)}, bf16[4,64,256]{2,1,0:T(8,128)(2,1)S(1)}, u32[]{:S(2)}, u32[]{:S(2)}) collective-permute-start(bf16[4,64,256]{2,1,0:T(8,128)(2,1)S(1)} %pad_maximum_fusion.6), channel_id=1, source_target_pairs={{0,2},{1,3},{2,0},{3,1},{4,6},{5,7},{6,4},{7,5},{8,10},{9,11},{10,... | collective-permute-start | bytes 393224 | tf_op jit(solution)/shard_map/ppermute | solution.py:354
  52.7 7.7 %collective-permute-start.12 = (bf16[4,8,8,256]{3,2,1,0:T(8,128)(2,1)S(1)}, bf16[4,8,8,256]{3,2,1,0:T(8,128)(2,1)S(1)}, u32[]{:S(2)}, u32[]{:S(2)}) collective-permute-start(bf16[4,8,8,256]{3,2,1,0:T(8,128)(2,1)S(1)} %get-tuple-element.56), channel_id=1, source_target_pairs={{0,24},{8,16},{16,8},{24,0},{1,25},{9,17},{17,9},{25,1},{2,26},{10... | collective-permute-start | bytes 393224 | tf_op jit(solution)/shard_map/ppermute | solution.py:354
  57.9 0.7 copy-start.9
  60.6 9.3 %collective-permute-start.21 = (bf16[4,64,256]{2,1,0:T(8,128)(2,1)S(1)}, bf16[4,64,256]{2,1,0:T(8,128)(2,1)S(1)}, u32[]{:S(2)}, u32[]{:S(2)}) collective-permute-start(bf16[4,64,256]{2,1,0:T(8,128)(2,1)S(1)} %pad_maximum_fusion.11), channel_id=1, source_target_pairs={{0,6},{1,7},{2,4},{3,5},{4,2},{5,3},{6,0},{7,1},{8,14},{9,15},{10,... | collective-permute-start | bytes 393224 | tf_op jit(solution)/shard_map/ppermute | solution.py:354
  63.1 8.4 %collective-permute-start.20 = (bf16[4,64,256]{2,1,0:T(8,128)(2,1)S(1)}, bf16[4,64,256]{2,1,0:T(8,128)(2,1)S(1)}, u32[]{:S(2)}, u32[]{:S(2)}) collective-permute-start(bf16[4,64,256]{2,1,0:T(8,128)(2,1)S(1)} %pad_maximum_fusion.10), channel_id=1, source_target_pairs={{0,4},{1,5},{2,6},{3,7},{4,0},{5,1},{6,2},{7,3},{8,12},{9,13},{10,... | collective-permute-start | bytes 393224 | tf_op jit(solution)/shard_map/ppermute | solution.py:354
  63.7 7.8 %collective-permute-start.19 = (bf16[4,64,256]{2,1,0:T(8,128)(2,1)S(1)}, bf16[4,64,256]{2,1,0:T(8,128)(2,1)S(1)}, u32[]{:S(2)}, u32[]{:S(2)}) collective-permute-start(bf16[4,64,256]{2,1,0:T(8,128)(2,1)S(1)} %pad_maximum_fusion.9), channel_id=1, source_target_pairs={{0,2},{1,3},{2,0},{3,1},{4,6},{5,7},{6,4},{7,5},{8,10},{9,11},{10,... | collective-permute-start | bytes 393224 | tf_op jit(solution)/shard_map/ppermute | solution.py:354
  64.3 11.9 %collective-permute-start.25 = (bf16[4,64,256]{2,1,0:T(8,128)(2,1)S(1)}, bf16[4,64,256]{2,1,0:T(8,128)(2,1)S(1)}, u32[]{:S(2)}, u32[]{:S(2)}) collective-permute-start(bf16[4,64,256]{2,1,0:T(8,128)(2,1)S(1)} %get-tuple-element.69), channel_id=1, source_target_pairs={{0,8},{8,0},{16,24},{24,16},{1,9},{9,1},{17,25},{25,17},{2,10},{10... | collective-permute-start | bytes 393224 | tf_op jit(solution)/shard_map/ppermute | solution.py:354
  67.8 10.0 %collective-permute-start.26 = (bf16[4,64,256]{2,1,0:T(8,128)(2,1)S(1)}, bf16[4,64,256]{2,1,0:T(8,128)(2,1)S(1)}, u32[]{:S(2)}, u32[]{:S(2)}) collective-permute-start(bf16[4,64,256]{2,1,0:T(8,128)(2,1)S(1)} %get-tuple-element.70), channel_id=1, source_target_pairs={{0,16},{8,24},{16,0},{24,8},{1,17},{9,25},{17,1},{25,9},{2,18},{10... | collective-permute-start | bytes 393224 | tf_op jit(solution)/shard_map/ppermute | solution.py:354
  69.9 11.2 %collective-permute-start.27 = (bf16[4,64,256]{2,1,0:T(8,128)(2,1)S(1)}, bf16[4,64,256]{2,1,0:T(8,128)(2,1)S(1)}, u32[]{:S(2)}, u32[]{:S(2)}) collective-permute-start(bf16[4,64,256]{2,1,0:T(8,128)(2,1)S(1)} %get-tuple-element.71), channel_id=1, source_target_pairs={{0,24},{8,16},{16,8},{24,0},{1,25},{9,17},{17,9},{25,1},{2,26},{10... | collective-permute-start | bytes 393224 | tf_op jit(solution)/shard_map/ppermute | solution.py:354
  73.3 9.2 %collective-permute-start.22 = (bf16[4,64,256]{2,1,0:T(8,128)(2,1)S(1)}, bf16[4,64,256]{2,1,0:T(8,128)(2,1)S(1)}, u32[]{:S(2)}, u32[]{:S(2)}) collective-permute-start(bf16[4,64,256]{2,1,0:T(8,128)(2,1)S(1)} %get-tuple-element.80), channel_id=1, source_target_pairs={{0,8},{8,0},{16,24},{24,16},{1,9},{9,1},{17,25},{25,17},{2,10},{10... | collective-permute-start | bytes 393224 | tf_op jit(solution)/shard_map/ppermute | solution.py:354
  74.7 13.7 %collective-permute-start.23 = (bf16[4,64,256]{2,1,0:T(8,128)(2,1)S(1)}, bf16[4,64,256]{2,1,0:T(8,128)(2,1)S(1)}, u32[]{:S(2)}, u32[]{:S(2)}) collective-permute-start(bf16[4,64,256]{2,1,0:T(8,128)(2,1)S(1)} %get-tuple-element.81), channel_id=1, source_target_pairs={{0,16},{8,24},{16,0},{24,8},{1,17},{9,25},{17,1},{25,9},{2,18},{10... | collective-permute-start | bytes 393224 | tf_op jit(solution)/shard_map/ppermute | solution.py:354
  76.2 12.2 %collective-permute-start.24 = (bf16[4,64,256]{2,1,0:T(8,128)(2,1)S(1)}, bf16[4,64,256]{2,1,0:T(8,128)(2,1)S(1)}, u32[]{:S(2)}, u32[]{:S(2)}) collective-permute-start(bf16[4,64,256]{2,1,0:T(8,128)(2,1)S(1)} %get-tuple-element.82), channel_id=1, source_target_pairs={{0,24},{8,16},{16,8},{24,0},{1,25},{9,17},{17,9},{25,1},{2,26},{10... | collective-permute-start | bytes 393224 | tf_op jit(solution)/shard_map/ppermute | solution.py:354

commit v4 on v3

--- a/solution.py
+++ b/solution.py
@@ -42,6 +42,10 @@
             got = dot(n, weight[...]).astype(jnp.bfloat16)
             out[:, s * local : (s + 1) * local, :] = got.reshape(frames, local, width)
     return [n.reshape(frames, local, width) for n in normal]
+
+
+def mask(place, shards):
+    return (shards - place) % shards
 
 
 def pick(rows, chips, turns, turn):
@@ -91,7 +95,7 @@
     for f in range(frames):
         for t in range(shards):
             for s in range(chips):
-                at = pl.multiple_of((s * shards + (t ^ zf)) * step, step)
+                at = pl.multiple_of((s * shards + (mask(t, shards) ^ zf)) * step, step)
                 outs[t][s, f] = mid_s[f, pl.ds(at, step), :].astype(jnp.bfloat16)
 
 
@@ -167,7 +171,7 @@
         out_specs=vmem(2),
         out_shape=[shape(frames, chips * local, width)] * 2,
         compiler_params=params(),
-        cost_estimate=cost(1),
+        cost_estimate=cost(40),
         name="spatial_rest",
     )(*args)
 
@@ -310,7 +314,7 @@
         @pl.when(ids_ref[0] == z)
         def _():
             for s in range(chips):
-                got = [pieces[g ^ z][s].astype(jnp.float32) for g in range(shards)]
+                got = [pieces[mask(g ^ z, shards)][s].astype(jnp.float32) for g in range(shards)]
                 held[pl.ds((s ^ ids_ref[1]) * frames, frames)] = jnp.concatenate(got, axis=1).astype(
                     jnp.bfloat16
                 )
@@ -379,7 +383,7 @@
     ids = jnp.stack([zf, chip]).astype(jnp.int32)
     row = lambda g: g.reshape(1, -1)
 
-    over_shards = lambda v: [v[0]] + [swap(v[t], "frame", shards, t) for t in range(1, shards)]
+    over_shards = lambda v: [v[0]] + [swap(v[t], "frame", shards, mask(t, shards)) for t in range(1, shards)]
     over_chips = lambda v: [v[0]] + [swap(v[s], "pos", spots, 2 * s) for s in range(1, chips)]
     half = max(1, each // SPLIT)
     cut = lambda s, part: lax.dynamic_slice_in_dim(
@@ -399,6 +403,7 @@
     rest = spatial_rest(
         swap(jnp.stack(mine), "pos", spots, 1), row(gain_one), key_one, value_one
     )
+    found, ready = lax.optimization_barrier((found, saved))
     saved = (*saved, *rest)
     far = swap(found, "pos", spots, 1)
     mid, ends = spatial_first(
@@ -426,7 +431,7 @@
             now, _ = lax.optimization_barrier((now, done))
         came = over_chips([None] + across(flat(now), chips)[1:])[1:]
         if turn + 1 < turns:
-            came, _ = lax.optimization_barrier((came, more[1:3]))
+            came, _ = lax.optimization_barrier((came, more[1::2]))
         if turn:
             came, done = lax.optimization_barrier((came, done))
         done = temporal(heads(flat(now)), came, *weights, step, True)

time: 90.2 us -> 87.9 us (0.975)
  waiting for transfers between devices: 18.5 us -> 16.7 us
    ppermute x2, waiting for transfers between devices: 5.46 us -> 3.83 us  [shards_fn(): lax.ppermute(found, 'frame', [(i, i + hop) for i in range(0, shards, 2 *...]
  transfers between devices with their start and end apart: 28 -> 28, of which waited for: 6 -> 11; matrix products, arithmetic and copies ran while one was open for 2% -> 2% of each run, Pallas kernels for 15% -> 15%
where the time goes in v4:
time: 87.9 us; the launch traced here: 87.7 us
  starting transfers between devices  44.5 us (51%)
  Pallas kernels  21.6 us (25%)
  waiting for transfers between devices  16.7 us (19%)
  local copies, waits for them, and re-layouts  3.74 us (4%)
    ppermute x26, starting transfers between devices, swap(): return lax.ppermute(value, axis, [(i, i ^ mask) for i in range(size)])  38.7 us
    ppermute x26, waiting for transfers between devices, swap(): return lax.ppermute(value, axis, [(i, i ^ mask) for i in range(size)])  12.9 us
    pallas_call x1, Pallas kernels, spatial_first(): pl.pallas_call(functools.partial(first_kernel, chips, shards, turns), in_...  6.63 us
    pallas_call x1, Pallas kernels, spatial_later(): pl.pallas_call(functools.partial(later_kernel, chips, turns, turn), in_sp...  6.32 us
    ppermute x2, starting transfers between devices, shards_fn(): lax.ppermute(found, 'frame', [(i, i + hop) for i in range(0, shards, 2 *...  5.8 us
    ppermute x2, waiting for transfers between devices, shards_fn(): lax.ppermute(found, 'frame', [(i, i + hop) for i in range(0, shards, 2 *...  3.83 us
    pallas_call x2, Pallas kernels, temporal(): pl.pallas_call(functools.partial(temporal_kernel, chips, shards, share, b...  3.72 us
    pallas_call x2, Pallas kernels, assemble(): pl.pallas_call(functools.partial(assemble_kernel, turn), in_specs=[pl.Blo...  2.82 us
  transfers between devices with their start and end apart: 28, of which 11 were waited for; matrix products, arithmetic and copies ran while one was open for 2% of the time, Pallas kernels for 15%

profile of v4, /device:TPU:0, one launch (start us, length us, event | category | flops | bytes accessed | tf_op | source)
XLA Modules:
  0.0 87.7 jit_solution(3222810435837113578)
XLA Ops:
  0.0 0.8 constant_dynamic-slice_fusion.1
  0.9 3.0 %collective-permute-start = (bf16[2,64,256]{2,1,0:T(8,128)(2,1)S(1)}, bf16[2,64,256]{2,1,0:T(8,128)(2,1)S(1)}, u32[]{:S(2)}, u32[]{:S(2)}) collective-permute-start(bf16[2,64,256]{2,1,0:T(8,128)(2,1)S(1)} %get-tuple-element.142), channel_id=1, source_target_pairs={{0,2},{1,3},{2,0},{3,1},{4,6},{5,7},{6,4},{7,5},{8,10},{9,11},{10,... | collective-permute-start | bytes 196616 | tf_op jit(solution)/shard_map/ppermute | solution.py:358
  3.9 1.5 %collective-permute-start.2 = (bf16[2,64,256]{2,1,0:T(8,128)(2,1)S(1)}, bf16[2,64,256]{2,1,0:T(8,128)(2,1)S(1)}, u32[]{:S(2)}, u32[]{:S(2)}) collective-permute-start(bf16[2,64,256]{2,1,0:T(8,128)(2,1)S(1)} %get-tuple-element.141), channel_id=1, source_target_pairs={{0,4},{1,5},{2,6},{3,7},{4,0},{5,1},{6,2},{7,3},{8,12},{9,13},{10,... | collective-permute-start | bytes 196616 | tf_op jit(solution)/shard_map/ppermute | solution.py:358
  5.4 1.3 %constant_dynamic-slice_fusion = (bf16[7,64,256]{2,1,0:T(8,128)(2,1)S(1)}, bf16[7,64,256]{2,1,0:T(8,128)(2,1)S(1)}, bf16[7,64,256]{2,1,0:T(8,128)(2,1)S(1)}, bf16[7,64,256]{2,1,0:T(8,128)(2,1)S(1)}) fusion(bf16[32,64,256]{2,1,0:T(8,128)(2,1)} %param.11, s32[]{:T(128)S(6)} %select_n.61, s32[]{:T(128)S(6)} %select_n.59, s32[]{:T(128)S(6)} %select_n.57, ...), kind=kLoop, calls=%fused_computation.49 | loop fusion | bytes 1835024 | tf_op jit(solution)/shard_map/dynamic_slice | solution.py:389
  6.8 3.0 %collective-permute-start.5 = (bf16[7,64,256]{2,1,0:T(8,128)(2,1)S(1)}, bf16[7,64,256]{2,1,0:T(8,128)(2,1)S(1)}, u32[]{:S(2)}, u32[]{:S(2)}) collective-permute-start(bf16[7,64,256]{2,1,0:T(8,128)(2,1)S(1)} %get-tuple-element.90), channel_id=1, source_target_pairs={{0,6},{1,7},{2,4},{3,5},{4,2},{5,3},{6,0},{7,1},{8,14},{9,15},{10,... | collective-permute-start | bytes 688136 | tf_op jit(solution)/shard_map/ppermute | solution.py:358
  9.7 0.5 collective-permute-start.3
  10.2 0.1 collective-permute-start.1
  10.4 0.9 %collective-permute-done.4 = bf16[2,64,256]{2,1,0:T(8,128)(2,1)S(1)} collective-permute-done((bf16[2,64,256]{2,1,0:T(8,128)(2,1)S(1)}, bf16[2,64,256]{2,1,0:T(8,128)(2,1)S(1)}, u32[]{:S(2)}, u32[]{:S(2)}) %collective-permute-start.4) | collective-permute-done | bytes 65568 | tf_op jit(solution)/shard_map/ppermute | solution.py:358
  11.3 4.5 %collective-permute-start.7 = (bf16[4,64,256]{2,1,0:T(8,128)(2,1)S(1)}, bf16[4,64,256]{2,1,0:T(8,128)(2,1)S(1)}, u32[]{:S(2)}, u32[]{:S(2)}) collective-permute-start(bf16[4,64,256]{2,1,0:T(8,128)(2,1)S(1)} %pad_maximum_fusion.5), channel_id=1, source_target_pairs={{0,16},{1,17},{2,18},{3,19},{4,20},{5,21},{6,22},{7,23}} | collective-permute-start | bytes 393224 | tf_op jit(solution)/shard_map/ppermute | solution.py:398
  15.8 0.1 pad_add_fusion.ids_ref
  15.9 3.7 %collective-permute-done.7 = bf16[4,64,256]{2,1,0:T(8,128)(2,1)S(1)} collective-permute-done((bf16[4,64,256]{2,1,0:T(8,128)(2,1)S(1)}, bf16[4,64,256]{2,1,0:T(8,128)(2,1)S(1)}, u32[]{:S(2)}, u32[]{:S(2)}) %collective-permute-start.7) | collective-permute-done | bytes 131104 | tf_op jit(solution)/shard_map/ppermute | solution.py:398
  19.7 1.3 %collective-permute-start.8 = (bf16[4,64,256]{2,1,0:T(8,128)(2,1)S(1)}, bf16[4,64,256]{2,1,0:T(8,128)(2,1)S(1)}, u32[]{:S(2)}, u32[]{:S(2)}) collective-permute-start(bf16[4,64,256]{2,1,0:T(8,128)(2,1)S(1)} %broadcast_select_fusion), channel_id=1, source_target_pairs={{0,8},{16,24},{1,9},{17,25},{2,10},{18,26},{3,11},{19,27},{4,12},{... | collective-permute-start | bytes 393224 | tf_op jit(solution)/shard_map/ppermute | solution.py:398
  21.2 0.1 pad_maximum_fusion
  21.4 0.1 collective-permute-start.6
  21.5 0.6 copy-done
  22.2 1.2 %spatial_ready.1 = (bf16[8,256,256]{2,1,0:T(8,128)(2,1)S(1)}, bf16[8,256,256]{2,1,0:T(8,128)(2,1)S(1)}, bf16[8,256,256]{2,1,0:T(8,128)(2,1)S(1)}) custom-call(bf16[8,64,256]{2,1,0:T(8,128)(2,1)S(1)} %get-tuple-element.95.refs_0_, bf16[8,64,256]{2,1,0:T(8,128)(2,1)S(1)} %get-tuple-element.97.refs_1_, bf16[8,64,256]{2,1,0:T(8,128)(2,1)S(1)} %get-tuple-element.99.refs_2_, ...), custom_call_target="tpu_custom_call" | custom-call | flops 40000000000 | bytes 144000000 | tf_op jit(solution)/shard_map/spatial_ready/pallas_call | solution.py:154
  23.4 0.1 collective-permute-done.8
  23.6 0.4 collective-permute-start.9
  23.9 0.1 collective-permute-done.6.other
  24.1 0.9 %spatial_rest.1 = (bf16[8,256,256]{2,1,0:T(8,128)(2,1)S(1)}, bf16[8,256,256]{2,1,0:T(8,128)(2,1)S(1)}) custom-call(bf16[4,8,64,256]{3,2,1,0:T(8,128)(2,1)S(1)} %collective-permute-done.6.other, f32[1,256]{1,0:T(1,128)S(1)} %bitcast.91, bf16[256,256]{1,0:T(8,128)(2,1)S(1)} %copy-done.1, bf16[256,256]{1,0:T(8,128)(2,1)S(1)} %copy-done.2), custom_call_target="tpu_custom_call" | custom-call | flops 40000000000 | bytes 144000000 | tf_op jit(solution)/shard_map/spatial_rest/pallas_call | solution.py:168
  25.1 6.6 %spatial_first.1 = (bf16[4,8,8,256]{3,2,1,0:T(8,128)(2,1)S(1)}, bf16[4,8,8,256]{3,2,1,0:T(8,128)(2,1)S(1)}, bf16[4,8,8,256]{3,2,1,0:T(8,128)(2,1)S(1)}, bf16[4,8...) custom-call(s32[2]{0:T(128)S(1)} %pad_add_fusion.ids_ref, ...), custom_call_target="tpu_custom_call" | custom-call | flops 6499999744 | bytes 23400000 | tf_op jit(solution)/shard_map/spatial_first/pallas_call | solution.py:185
  31.7 5.2 %collective-permute-start.13 = (bf16[4,8,8,256]{3,2,1,0:T(8,128)(2,1)S(1)}, bf16[4,8,8,256]{3,2,1,0:T(8,128)(2,1)S(1)}, u32[]{:S(2)}, u32[]{:S(2)}) collective-permute-start(bf16[4,8,8,256]{3,2,1,0:T(8,128)(2,1)S(1)} %get-tuple-element.60), channel_id=1, source_target_pairs={{0,24},{8,16},{16,8},{24,0},{1,25},{9,17},{17,9},{25,1},{2,26},{10... | collective-permute-start | bytes 393224 | tf_op jit(solution)/shard_map/ppermute | solution.py:358
  36.9 0.6 collective-permute-start.15
  37.6 6.3 %spatial_later.1 = (bf16[4,8,8,256]{3,2,1,0:T(8,128)(2,1)S(1)}, bf16[4,8,8,256]{3,2,1,0:T(8,128)(2,1)S(1)}, bf16[4,8,8,256]{3,2,1,0:T(8,128)(2,1)S(1)}, bf16[4,8,8,256]{3,2,1,0:T(8,128)(2,1)S(1)}) custom-call(s32[2]{0:T(128)S(1)} %pad_add_fusion.ids_ref, bf16[8,64,256]{2,1,0:T(8,128)(2,1)S(1)} %get-tuple-element.95.refs_0_, ...), custom_call_target="tpu_custom_call" | custom-call | flops 6400000000 | bytes 23040000 | tf_op jit(solution)/shard_map/spatial_later/pallas_call | solution.py:203
  43.9 3.8 %collective-permute-start.10 = (bf16[4,8,8,256]{3,2,1,0:T(8,128)(2,1)S(1)}, bf16[4,8,8,256]{3,2,1,0:T(8,128)(2,1)S(1)}, u32[]{:S(2)}, u32[]{:S(2)}) collective-permute-start(bf16[4,8,8,256]{3,2,1,0:T(8,128)(2,1)S(1)} %get-tuple-element.56), channel_id=1, source_target_pairs={{0,24},{8,16},{16,8},{24,0},{1,25},{9,17},{17,9},{25,1},{2,26},{10... | collective-permute-start | bytes 393224 | tf_op jit(solution)/shard_map/ppermute | solution.py:358
  47.7 0.3 collective-permute-done.14
  48.1 1.7 %collective-permute-start.18 = (bf16[4,64,256]{2,1,0:T(8,128)(2,1)S(1)}, bf16[4,64,256]{2,1,0:T(8,128)(2,1)S(1)}, u32[]{:S(2)}, u32[]{:S(2)}) collective-permute-start(bf16[4,64,256]{2,1,0:T(8,128)(2,1)S(1)} %pad_maximum_fusion.8), channel_id=1, source_target_pairs={{0,6},{1,7},{2,4},{3,5},{4,2},{5,3},{6,0},{7,1},{8,14},{9,15},{10,... | collective-permute-start | bytes 393224 | tf_op jit(solution)/shard_map/ppermute | solution.py:358
  49.8 0.6 collective-permute-start.17
  50.4 1.4 %collective-permute-start.16 = (bf16[4,64,256]{2,1,0:T(8,128)(2,1)S(1)}, bf16[4,64,256]{2,1,0:T(8,128)(2,1)S(1)}, u32[]{:S(2)}, u32[]{:S(2)}) collective-permute-start(bf16[4,64,256]{2,1,0:T(8,128)(2,1)S(1)} %pad_maximum_fusion.6), channel_id=1, source_target_pairs={{0,2},{1,3},{2,0},{3,1},{4,6},{5,7},{6,4},{7,5},{8,10},{9,11},{10,... | collective-permute-start | bytes 393224 | tf_op jit(solution)/shard_map/ppermute | solution.py:358
  51.8 0.3 collective-permute-done.10
  52.2 2.7 %collective-permute-start.11 = (bf16[4,8,8,256]{3,2,1,0:T(8,128)(2,1)S(1)}, bf16[4,8,8,256]{3,2,1,0:T(8,128)(2,1)S(1)}, u32[]{:S(2)}, u32[]{:S(2)}) collective-permute-start(bf16[4,8,8,256]{3,2,1,0:T(8,128)(2,1)S(1)} %get-tuple-element.57), channel_id=1, source_target_pairs={{0,16},{8,24},{16,0},{24,8},{1,17},{9,25},{17,1},{25,9},{2,18},{10... | collective-permute-start | bytes 393224 | tf_op jit(solution)/shard_map/ppermute | solution.py:358
  54.8 0.3 collective-permute-done.18.refs_6_
  55.1 1.0 %collective-permute-done.17.refs_5_ = bf16[4,64,256]{2,1,0:T(8,128)(2,1)S(1)} collective-permute-done((bf16[4,64,256]{2,1,0:T(8,128)(2,1)S(1)}, bf16[4,64,256]{2,1,0:T(8,128)(2,1)S(1)}, u32[]{:S(2)}, u32[]{:S(2)}) %collective-permute-start.17) | collective-permute-done | bytes 131104 | tf_op jit(solution)/shard_map/ppermute | solution.py:358
  56.1 0.6 copy-done.9
  56.8 1.9 %temporal.2 = (bf16[4,64,256]{2,1,0:T(8,128)(2,1)S(1)}, bf16[4,64,256]{2,1,0:T(8,128)(2,1)S(1)}, bf16[4,64,256]{2,1,0:T(8,128)(2,1)S(1)}, bf16[4,64,256]{2,1,0:T(8,128)(2,1)S(1)}) custom-call(bf16[64,256]{1,0:T(8,128)(2,1)S(1)} %get-tuple-element.147.refs_0_, bf16[64,256]{1,0:T(8,128)(2,1)S(1)} %get-tuple-element.125.refs_1_, ...), custom_call_target="tpu_custom_call" | custom-call | flops 1900000000 | bytes 6840000 | tf_op jit(solution)/shard_map/temporal/pallas_call | solution.py:291
  58.6 1.7 %collective-permute-done.11 = bf16[4,8,8,256]{3,2,1,0:T(8,128)(2,1)S(1)} collective-permute-done((bf16[4,8,8,256]{3,2,1,0:T(8,128)(2,1)S(1)}, bf16[4,8,8,256]{3,2,1,0:T(8,128)(2,1)S(1)}, u32[]{:S(2)}, u32[]{:S(2)}) %collective-permute-start.11) | collective-permute-done | bytes 131104 | tf_op jit(solution)/shard_map/ppermute | solution.py:358
  60.5 1.7 %collective-permute-start.21 = (bf16[4,64,256]{2,1,0:T(8,128)(2,1)S(1)}, bf16[4,64,256]{2,1,0:T(8,128)(2,1)S(1)}, u32[]{:S(2)}, u32[]{:S(2)}) collective-permute-start(bf16[4,64,256]{2,1,0:T(8,128)(2,1)S(1)} %pad_maximum_fusion.11), channel_id=1, source_target_pairs={{0,6},{1,7},{2,4},{3,5},{4,2},{5,3},{6,0},{7,1},{8,14},{9,15},{10,... | collective-permute-start | bytes 393224 | tf_op jit(solution)/shard_map/ppermute | solution.py:358
  62.2 0.6 collective-permute-start.20
  62.8 1.4 %collective-permute-start.19 = (bf16[4,64,256]{2,1,0:T(8,128)(2,1)S(1)}, bf16[4,64,256]{2,1,0:T(8,128)(2,1)S(1)}, u32[]{:S(2)}, u32[]{:S(2)}) collective-permute-start(bf16[4,64,256]{2,1,0:T(8,128)(2,1)S(1)} %pad_maximum_fusion.9), channel_id=1, source_target_pairs={{0,2},{1,3},{2,0},{3,1},{4,6},{5,7},{6,4},{7,5},{8,10},{9,11},{10,... | collective-permute-start | bytes 393224 | tf_op jit(solution)/shard_map/ppermute | solution.py:358
  64.2 2.6 %collective-permute-start.25 = (bf16[4,64,256]{2,1,0:T(8,128)(2,1)S(1)}, bf16[4,64,256]{2,1,0:T(8,128)(2,1)S(1)}, u32[]{:S(2)}, u32[]{:S(2)}) collective-permute-start(bf16[4,64,256]{2,1,0:T(8,128)(2,1)S(1)} %get-tuple-element.71), channel_id=1, source_target_pairs={{0,24},{8,16},{16,8},{24,0},{1,25},{9,17},{17,9},{25,1},{2,26},{10... | collective-permute-start | bytes 393224 | tf_op jit(solution)/shard_map/ppermute | solution.py:358
  66.8 1.8 %collective-permute-start.27 = (bf16[4,64,256]{2,1,0:T(8,128)(2,1)S(1)}, bf16[4,64,256]{2,1,0:T(8,128)(2,1)S(1)}, u32[]{:S(2)}, u32[]{:S(2)}) collective-permute-start(bf16[4,64,256]{2,1,0:T(8,128)(2,1)S(1)} %get-tuple-element.73), channel_id=1, source_target_pairs={{0,8},{8,0},{16,24},{24,16},{1,9},{9,1},{17,25},{25,17},{2,10},{10... | collective-permute-start | bytes 393224 | tf_op jit(solution)/shard_map/ppermute | solution.py:358
  68.6 1.9 %temporal.3 = (bf16[4,64,256]{2,1,0:T(8,128)(2,1)S(1)}, bf16[4,64,256]{2,1,0:T(8,128)(2,1)S(1)}, bf16[4,64,256]{2,1,0:T(8,128)(2,1)S(1)}, bf16[4,64,256]{2,1,0:T(8,128)(2,1)S(1)}) custom-call(bf16[64,256]{1,0:T(8,128)(2,1)S(1)} %get-tuple-element.105.refs_0_, bf16[64,256]{1,0:T(8,128)(2,1)S(1)} %get-tuple-element.109.refs_1_, ...), custom_call_target="tpu_custom_call" | custom-call | flops 1900000000 | bytes 6840000 | tf_op jit(solution)/shard_map/temporal/pallas_call | solution.py:291
  70.5 2.6 %collective-permute-start.22 = (bf16[4,64,256]{2,1,0:T(8,128)(2,1)S(1)}, bf16[4,64,256]{2,1,0:T(8,128)(2,1)S(1)}, u32[]{:S(2)}, u32[]{:S(2)}) collective-permute-start(bf16[4,64,256]{2,1,0:T(8,128)(2,1)S(1)} %get-tuple-element.82), channel_id=1, source_target_pairs={{0,24},{8,16},{16,8},{24,0},{1,25},{9,17},{17,9},{25,1},{2,26},{10... | collective-permute-start | bytes 393224 | tf_op jit(solution)/shard_map/ppermute | solution.py:358
  73.1 3.4 %collective-permute-start.24 = (bf16[4,64,256]{2,1,0:T(8,128)(2,1)S(1)}, bf16[4,64,256]{2,1,0:T(8,128)(2,1)S(1)}, u32[]{:S(2)}, u32[]{:S(2)}) collective-permute-start(bf16[4,64,256]{2,1,0:T(8,128)(2,1)S(1)} %get-tuple-element.84), channel_id=1, source_target_pairs={{0,8},{8,0},{16,24},{24,16},{1,9},{9,1},{17,25},{25,17},{2,10},{10... | collective-permute-start | bytes 393224 | tf_op jit(solution)/shard_map/ppermute | solution.py:358
  76.5 5.1 %collective-permute-done.26 = bf16[4,64,256]{2,1,0:T(8,128)(2,1)S(1)} collective-permute-done((bf16[4,64,256]{2,1,0:T(8,128)(2,1)S(1)}, bf16[4,64,256]{2,1,0:T(8,128)(2,1)S(1)}, u32[]{:S(2)}, u32[]{:S(2)}) %collective-permute-start.26) | collective-permute-done | bytes 131104 | tf_op jit(solution)/shard_map/ppermute | solution.py:358
  81.6 1.4 %assemble.2.refs_4_ = bf16[32,64,256]{2,1,0:T(8,128)(2,1)} custom-call(s32[2]{0:T(128)S(1)} %pad_add_fusion.ids_ref, bf16[4,8,8,256]{3,2,1,0:T(8,128)(2,1)S(1)} %bitcast.95, bf16[4,8,8,256]{3,2,1,0:T(8,128)(2,1)S(1)} %bitcast.84, bf16[4,8,8,256]{3,2,1,0:T(8,128)(2,1)S(1)} %bitcast.85, ...), custom_call_target="tpu_custom_call", output_to_operand_aliasing={{}: (5, {})} | custom-call | flops 60000002048 | bytes 216000000 | tf_op jit(solution)/shard_map/assemble/pallas_call | solution.py:330
  83.0 3.1 %collective-permute-done.23 = bf16[4,64,256]{2,1,0:T(8,128)(2,1)S(1)} collective-permute-done((bf16[4,64,256]{2,1,0:T(8,128)(2,1)S(1)}, bf16[4,64,256]{2,1,0:T(8,128)(2,1)S(1)}, u32[]{:S(2)}, u32[]{:S(2)}) %collective-permute-start.23) | collective-permute-done | bytes 131104 | tf_op jit(solution)/shard_map/ppermute | solution.py:358
  86.1 1.4 %assemble.3 = bf16[32,64,256]{2,1,0:T(8,128)(2,1)} custom-call(s32[2]{0:T(128)S(1)} %pad_add_fusion.ids_ref, bf16[4,8,8,256]{3,2,1,0:T(8,128)(2,1)S(1)} %bitcast.96, bf16[4,8,8,256]{3,2,1,0:T(8,128)(2,1)S(1)} %bitcast.87, bf16[4,8,8,256]{3,2,1,0:T(8,128)(2,1)S(1)} %bitcast.88, bf16[4,8,8,256]{3,2,1,0:T(8,128)(2,1)S(1)} %bitcast.89, ...), custom_call_target="tpu_custom_call", output_to_operand_aliasing={{}: (5, {})} | custom-call | flops 1000000000 | bytes 3600000 | tf_op jit(solution)/shard_map/assemble/pallas_call | solution.py:330
  (64 shorter events, 0.7 us)
Async XLA Ops:
  0.9 9.4 %collective-permute-start = (bf16[2,64,256]{2,1,0:T(8,128)(2,1)S(1)}, bf16[2,64,256]{2,1,0:T(8,128)(2,1)S(1)}, u32[]{:S(2)}, u32[]{:S(2)}) collective-permute-start(bf16[2,64,256]{2,1,0:T(8,128)(2,1)S(1)} %get-tuple-element.142), channel_id=1, source_target_pairs={{0,2},{1,3},{2,0},{3,1},{4,6},{5,7},{6,4},{7,5},{8,10},{9,11},{10,... | collective-permute-start | bytes 196616 | tf_op jit(solution)/shard_map/ppermute | solution.py:358
  3.9 6.5 %collective-permute-start.2 = (bf16[2,64,256]{2,1,0:T(8,128)(2,1)S(1)}, bf16[2,64,256]{2,1,0:T(8,128)(2,1)S(1)}, u32[]{:S(2)}, u32[]{:S(2)}) collective-permute-start(bf16[2,64,256]{2,1,0:T(8,128)(2,1)S(1)} %get-tuple-element.141), channel_id=1, source_target_pairs={{0,4},{1,5},{2,6},{3,7},{4,0},{5,1},{6,2},{7,3},{8,12},{9,13},{10,... | collective-permute-start | bytes 196616 | tf_op jit(solution)/shard_map/ppermute | solution.py:358
  5.4 5.9 %collective-permute-start.4 = (bf16[2,64,256]{2,1,0:T(8,128)(2,1)S(1)}, bf16[2,64,256]{2,1,0:T(8,128)(2,1)S(1)}, u32[]{:S(2)}, u32[]{:S(2)}) collective-permute-start(bf16[2,64,256]{2,1,0:T(8,128)(2,1)S(1)} %get-tuple-element.140), channel_id=1, source_target_pairs={{0,6},{1,7},{2,4},{3,5},{4,2},{5,3},{6,0},{7,1},{8,14},{9,15},{10,... | collective-permute-start | bytes 196616 | tf_op jit(solution)/shard_map/ppermute | solution.py:358
  6.8 14.3 %collective-permute-start.5 = (bf16[7,64,256]{2,1,0:T(8,128)(2,1)S(1)}, bf16[7,64,256]{2,1,0:T(8,128)(2,1)S(1)}, u32[]{:S(2)}, u32[]{:S(2)}) collective-permute-start(bf16[7,64,256]{2,1,0:T(8,128)(2,1)S(1)} %get-tuple-element.90), channel_id=1, source_target_pairs={{0,6},{1,7},{2,4},{3,5},{4,2},{5,3},{6,0},{7,1},{8,14},{9,15},{10,... | collective-permute-start | bytes 688136 | tf_op jit(solution)/shard_map/ppermute | solution.py:358
  9.7 11.3 %collective-permute-start.3 = (bf16[7,64,256]{2,1,0:T(8,128)(2,1)S(1)}, bf16[7,64,256]{2,1,0:T(8,128)(2,1)S(1)}, u32[]{:S(2)}, u32[]{:S(2)}) collective-permute-start(bf16[7,64,256]{2,1,0:T(8,128)(2,1)S(1)} %get-tuple-element.91), channel_id=1, source_target_pairs={{0,4},{1,5},{2,6},{3,7},{4,0},{5,1},{6,2},{7,3},{8,12},{9,13},{10,... | collective-permute-start | bytes 688136 | tf_op jit(solution)/shard_map/ppermute | solution.py:358
  10.2 10.9 %collective-permute-start.1 = (bf16[7,64,256]{2,1,0:T(8,128)(2,1)S(1)}, bf16[7,64,256]{2,1,0:T(8,128)(2,1)S(1)}, u32[]{:S(2)}, u32[]{:S(2)}) collective-permute-start(bf16[7,64,256]{2,1,0:T(8,128)(2,1)S(1)} %get-tuple-element.92), channel_id=1, source_target_pairs={{0,2},{1,3},{2,0},{3,1},{4,6},{5,7},{6,4},{7,5},{8,10},{9,11},{10,... | collective-permute-start | bytes 688136 | tf_op jit(solution)/shard_map/ppermute | solution.py:358
  11.3 8.4 %collective-permute-start.7 = (bf16[4,64,256]{2,1,0:T(8,128)(2,1)S(1)}, bf16[4,64,256]{2,1,0:T(8,128)(2,1)S(1)}, u32[]{:S(2)}, u32[]{:S(2)}) collective-permute-start(bf16[4,64,256]{2,1,0:T(8,128)(2,1)S(1)} %pad_maximum_fusion.5), channel_id=1, source_target_pairs={{0,16},{1,17},{2,18},{3,19},{4,20},{5,21},{6,22},{7,23}} | collective-permute-start | bytes 393224 | tf_op jit(solution)/shard_map/ppermute | solution.py:398
  19.7 3.8 %collective-permute-start.8 = (bf16[4,64,256]{2,1,0:T(8,128)(2,1)S(1)}, bf16[4,64,256]{2,1,0:T(8,128)(2,1)S(1)}, u32[]{:S(2)}, u32[]{:S(2)}) collective-permute-start(bf16[4,64,256]{2,1,0:T(8,128)(2,1)S(1)} %broadcast_select_fusion), channel_id=1, source_target_pairs={{0,8},{16,24},{1,9},{17,25},{2,10},{18,26},{3,11},{19,27},{4,12},{... | collective-permute-start | bytes 393224 | tf_op jit(solution)/shard_map/ppermute | solution.py:398
  21.2 0.9 %copy-start = (bf16[256,256]{1,0:T(8,128)(2,1)S(1)}, bf16[256,256]{1,0:T(8,128)(2,1)}, u32[]{:S(2)}) copy-start(bf16[256,256]{1,0:T(8,128)(2,1)} %refs_5_.1) | copy-start | bytes 393220
  21.2 1.0 %copy-start.1 = (bf16[256,256]{1,0:T(8,128)(2,1)S(1)}, bf16[256,256]{1,0:T(8,128)(2,1)}, u32[]{:S(2)}) copy-start(bf16[256,256]{1,0:T(8,128)(2,1)} %refs_7_.3) | copy-start | bytes 393220
  21.2 1.0 %copy-start.2 = (bf16[256,256]{1,0:T(8,128)(2,1)S(1)}, bf16[256,256]{1,0:T(8,128)(2,1)}, u32[]{:S(2)}) copy-start(bf16[256,256]{1,0:T(8,128)(2,1)} %refs_8_.3) | copy-start | bytes 393220
  21.4 2.7 %collective-permute-start.6 = (bf16[4,8,64,256]{3,2,1,0:T(8,128)(2,1)S(1)}, bf16[4,8,64,256]{3,2,1,0:T(8,128)(2,1)S(1)}, u32[]{:S(2)}, u32[]{:S(2)}) collective-permute-start(bf16[4,8,64,256]{3,2,1,0:T(8,128)(2,1)S(1)} %pad_maximum_fusion), channel_id=1, source_target_pairs={{0,1},{1,0},{2,3},{3,2},{4,5},{5,4},{6,7},{7,6},{8,9},{9,8},{10,11... | collective-permute-start | bytes 3145736 | tf_op jit(solution)/shard_map/ppermute | solution.py:358
  21.4 0.8 copy-start.8
  23.5 1.5 %copy-start.3 = (bf16[256,256]{1,0:T(8,128)(2,1)S(1)}, bf16[256,256]{1,0:T(8,128)(2,1)}, u32[]{:S(2)}) copy-start(bf16[256,256]{1,0:T(8,128)(2,1)} %refs_13_.1) | copy-start | bytes 393220
  23.6 1.5 %collective-permute-start.9 = (bf16[4,64,256]{2,1,0:T(8,128)(2,1)S(1)}, bf16[4,64,256]{2,1,0:T(8,128)(2,1)S(1)}, u32[]{:S(2)}, u32[]{:S(2)}) collective-permute-start(bf16[4,64,256]{2,1,0:T(8,128)(2,1)S(1)} %broadcast_select_fusion.1.refs_4_), channel_id=1, source_target_pairs={{0,1},{1,0},{2,3},{3,2},{4,5},{5,4},{6,7},{7,6},{8,9},{9,8},{10,11... | collective-permute-start | bytes 393224 | tf_op jit(solution)/shard_map/ppermute | solution.py:358
  31.7 16.0 %collective-permute-start.13 = (bf16[4,8,8,256]{3,2,1,0:T(8,128)(2,1)S(1)}, bf16[4,8,8,256]{3,2,1,0:T(8,128)(2,1)S(1)}, u32[]{:S(2)}, u32[]{:S(2)}) collective-permute-start(bf16[4,8,8,256]{3,2,1,0:T(8,128)(2,1)S(1)} %get-tuple-element.60), channel_id=1, source_target_pairs={{0,24},{8,16},{16,8},{24,0},{1,25},{9,17},{17,9},{25,1},{2,26},{10... | collective-permute-start | bytes 393224 | tf_op jit(solution)/shard_map/ppermute | solution.py:358
  36.9 11.1 %collective-permute-start.14 = (bf16[4,8,8,256]{3,2,1,0:T(8,128)(2,1)S(1)}, bf16[4,8,8,256]{3,2,1,0:T(8,128)(2,1)S(1)}, u32[]{:S(2)}, u32[]{:S(2)}) collective-permute-start(bf16[4,8,8,256]{3,2,1,0:T(8,128)(2,1)S(1)} %get-tuple-element.61), channel_id=1, source_target_pairs={{0,16},{8,24},{16,0},{24,8},{1,17},{9,25},{17,1},{25,9},{2,18},{10... | collective-permute-start | bytes 393224 | tf_op jit(solution)/shard_map/ppermute | solution.py:358
  36.9 11.1 %collective-permute-start.15 = (bf16[4,8,8,256]{3,2,1,0:T(8,128)(2,1)S(1)}, bf16[4,8,8,256]{3,2,1,0:T(8,128)(2,1)S(1)}, u32[]{:S(2)}, u32[]{:S(2)}) collective-permute-start(bf16[4,8,8,256]{3,2,1,0:T(8,128)(2,1)S(1)} %get-tuple-element.62), channel_id=1, source_target_pairs={{0,8},{8,0},{16,24},{24,16},{1,9},{9,1},{17,25},{25,17},{2,10},{10... | collective-permute-start | bytes 393224 | tf_op jit(solution)/shard_map/ppermute | solution.py:358
  37.5 18.6 %copy-start.6 = (bf16[256,256]{1,0:T(8,128)(2,1)S(1)}, bf16[256,256]{1,0:T(8,128)(2,1)}, u32[]{:S(2)}) copy-start(bf16[256,256]{1,0:T(8,128)(2,1)} %refs_10_.3) | copy-start | bytes 393220
  37.5 18.6 %copy-start.7 = (bf16[256,256]{1,0:T(8,128)(2,1)S(1)}, bf16[256,256]{1,0:T(8,128)(2,1)}, u32[]{:S(2)}) copy-start(bf16[256,256]{1,0:T(8,128)(2,1)} %refs_11_.3) | copy-start | bytes 393220
  43.9 8.3 %collective-permute-start.10 = (bf16[4,8,8,256]{3,2,1,0:T(8,128)(2,1)S(1)}, bf16[4,8,8,256]{3,2,1,0:T(8,128)(2,1)S(1)}, u32[]{:S(2)}, u32[]{:S(2)}) collective-permute-start(bf16[4,8,8,256]{3,2,1,0:T(8,128)(2,1)S(1)} %get-tuple-element.56), channel_id=1, source_target_pairs={{0,24},{8,16},{16,8},{24,0},{1,25},{9,17},{17,9},{25,1},{2,26},{10... | collective-permute-start | bytes 393224 | tf_op jit(solution)/shard_map/ppermute | solution.py:358
  47.7 7.1 %collective-permute-start.12 = (bf16[4,8,8,256]{3,2,1,0:T(8,128)(2,1)S(1)}, bf16[4,8,8,256]{3,2,1,0:T(8,128)(2,1)S(1)}, u32[]{:S(2)}, u32[]{:S(2)}) collective-permute-start(bf16[4,8,8,256]{3,2,1,0:T(8,128)(2,1)S(1)} %get-tuple-element.58), channel_id=1, source_target_pairs={{0,8},{8,0},{16,24},{24,16},{1,9},{9,1},{17,25},{25,17},{2,10},{10... | collective-permute-start | bytes 393224 | tf_op jit(solution)/shard_map/ppermute | solution.py:358
  48.1 7.0 %collective-permute-start.18 = (bf16[4,64,256]{2,1,0:T(8,128)(2,1)S(1)}, bf16[4,64,256]{2,1,0:T(8,128)(2,1)S(1)}, u32[]{:S(2)}, u32[]{:S(2)}) collective-permute-start(bf16[4,64,256]{2,1,0:T(8,128)(2,1)S(1)} %pad_maximum_fusion.8), channel_id=1, source_target_pairs={{0,6},{1,7},{2,4},{3,5},{4,2},{5,3},{6,0},{7,1},{8,14},{9,15},{10,... | collective-permute-start | bytes 393224 | tf_op jit(solution)/shard_map/ppermute | solution.py:358
  49.8 6.3 %collective-permute-start.17 = (bf16[4,64,256]{2,1,0:T(8,128)(2,1)S(1)}, bf16[4,64,256]{2,1,0:T(8,128)(2,1)S(1)}, u32[]{:S(2)}, u32[]{:S(2)}) collective-permute-start(bf16[4,64,256]{2,1,0:T(8,128)(2,1)S(1)} %pad_maximum_fusion.7), channel_id=1, source_target_pairs={{0,4},{1,5},{2,6},{3,7},{4,0},{5,1},{6,2},{7,3},{8,12},{9,13},{10,... | collective-permute-start | bytes 393224 | tf_op jit(solution)/shard_map/ppermute | solution.py:358
  50.4 5.7 %copy-start.4 = (bf16[256,256]{1,0:T(8,128)(2,1)S(1)}, bf16[256,256]{1,0:T(8,128)(2,1)}, u32[]{:S(2)}) copy-start(bf16[256,256]{1,0:T(8,128)(2,1)} %refs_8_.5) | copy-start | bytes 393220
  50.4 5.7 %copy-start.5 = (bf16[256,256]{1,0:T(8,128)(2,1)S(1)}, bf16[256,256]{1,0:T(8,128)(2,1)}, u32[]{:S(2)}) copy-start(bf16[256,256]{1,0:T(8,128)(2,1)} %refs_9_.5) | copy-start | bytes 393220
  50.4 5.7 %collective-permute-start.16 = (bf16[4,64,256]{2,1,0:T(8,128)(2,1)S(1)}, bf16[4,64,256]{2,1,0:T(8,128)(2,1)S(1)}, u32[]{:S(2)}, u32[]{:S(2)}) collective-permute-start(bf16[4,64,256]{2,1,0:T(8,128)(2,1)S(1)} %pad_maximum_fusion.6), channel_id=1, source_target_pairs={{0,2},{1,3},{2,0},{3,1},{4,6},{5,7},{6,4},{7,5},{8,10},{9,11},{10,... | collective-permute-start | bytes 393224 | tf_op jit(solution)/shard_map/ppermute | solution.py:358
  52.2 8.2 %collective-permute-start.11 = (bf16[4,8,8,256]{3,2,1,0:T(8,128)(2,1)S(1)}, bf16[4,8,8,256]{3,2,1,0:T(8,128)(2,1)S(1)}, u32[]{:S(2)}, u32[]{:S(2)}) collective-permute-start(bf16[4,8,8,256]{3,2,1,0:T(8,128)(2,1)S(1)} %get-tuple-element.57), channel_id=1, source_target_pairs={{0,16},{8,24},{16,0},{24,8},{1,17},{9,25},{17,1},{25,9},{2,18},{10... | collective-permute-start | bytes 393224 | tf_op jit(solution)/shard_map/ppermute | solution.py:358
  56.1 0.7 copy-start.9
  60.5 6.3 %collective-permute-start.21 = (bf16[4,64,256]{2,1,0:T(8,128)(2,1)S(1)}, bf16[4,64,256]{2,1,0:T(8,128)(2,1)S(1)}, u32[]{:S(2)}, u32[]{:S(2)}) collective-permute-start(bf16[4,64,256]{2,1,0:T(8,128)(2,1)S(1)} %pad_maximum_fusion.11), channel_id=1, source_target_pairs={{0,6},{1,7},{2,4},{3,5},{4,2},{5,3},{6,0},{7,1},{8,14},{9,15},{10,... | collective-permute-start | bytes 393224 | tf_op jit(solution)/shard_map/ppermute | solution.py:358
  62.2 6.4 %collective-permute-start.20 = (bf16[4,64,256]{2,1,0:T(8,128)(2,1)S(1)}, bf16[4,64,256]{2,1,0:T(8,128)(2,1)S(1)}, u32[]{:S(2)}, u32[]{:S(2)}) collective-permute-start(bf16[4,64,256]{2,1,0:T(8,128)(2,1)S(1)} %pad_maximum_fusion.10), channel_id=1, source_target_pairs={{0,4},{1,5},{2,6},{3,7},{4,0},{5,1},{6,2},{7,3},{8,12},{9,13},{10,... | collective-permute-start | bytes 393224 | tf_op jit(solution)/shard_map/ppermute | solution.py:358
  62.8 5.8 %collective-permute-start.19 = (bf16[4,64,256]{2,1,0:T(8,128)(2,1)S(1)}, bf16[4,64,256]{2,1,0:T(8,128)(2,1)S(1)}, u32[]{:S(2)}, u32[]{:S(2)}) collective-permute-start(bf16[4,64,256]{2,1,0:T(8,128)(2,1)S(1)} %pad_maximum_fusion.9), channel_id=1, source_target_pairs={{0,2},{1,3},{2,0},{3,1},{4,6},{5,7},{6,4},{7,5},{8,10},{9,11},{10,... | collective-permute-start | bytes 393224 | tf_op jit(solution)/shard_map/ppermute | solution.py:358
  64.2 8.9 %collective-permute-start.25 = (bf16[4,64,256]{2,1,0:T(8,128)(2,1)S(1)}, bf16[4,64,256]{2,1,0:T(8,128)(2,1)S(1)}, u32[]{:S(2)}, u32[]{:S(2)}) collective-permute-start(bf16[4,64,256]{2,1,0:T(8,128)(2,1)S(1)} %get-tuple-element.71), channel_id=1, source_target_pairs={{0,24},{8,16},{16,8},{24,0},{1,25},{9,17},{17,9},{25,1},{2,26},{10... | collective-permute-start | bytes 393224 | tf_op jit(solution)/shard_map/ppermute | solution.py:358
  66.8 14.8 %collective-permute-start.26 = (bf16[4,64,256]{2,1,0:T(8,128)(2,1)S(1)}, bf16[4,64,256]{2,1,0:T(8,128)(2,1)S(1)}, u32[]{:S(2)}, u32[]{:S(2)}) collective-permute-start(bf16[4,64,256]{2,1,0:T(8,128)(2,1)S(1)} %get-tuple-element.72), channel_id=1, source_target_pairs={{0,16},{8,24},{16,0},{24,8},{1,17},{9,25},{17,1},{25,9},{2,18},{10... | collective-permute-start | bytes 393224 | tf_op jit(solution)/shard_map/ppermute | solution.py:358
  66.8 14.8 %collective-permute-start.27 = (bf16[4,64,256]{2,1,0:T(8,128)(2,1)S(1)}, bf16[4,64,256]{2,1,0:T(8,128)(2,1)S(1)}, u32[]{:S(2)}, u32[]{:S(2)}) collective-permute-start(bf16[4,64,256]{2,1,0:T(8,128)(2,1)S(1)} %get-tuple-element.73), channel_id=1, source_target_pairs={{0,8},{8,0},{16,24},{24,16},{1,9},{9,1},{17,25},{25,17},{2,10},{10... | collective-permute-start | bytes 393224 | tf_op jit(solution)/shard_map/ppermute | solution.py:358
  70.5 12.5 %collective-permute-start.22 = (bf16[4,64,256]{2,1,0:T(8,128)(2,1)S(1)}, bf16[4,64,256]{2,1,0:T(8,128)(2,1)S(1)}, u32[]{:S(2)}, u32[]{:S(2)}) collective-permute-start(bf16[4,64,256]{2,1,0:T(8,128)(2,1)S(1)} %get-tuple-element.82), channel_id=1, source_target_pairs={{0,24},{8,16},{16,8},{24,0},{1,25},{9,17},{17,9},{25,1},{2,26},{10... | collective-permute-start | bytes 393224 | tf_op jit(solution)/shard_map/ppermute | solution.py:358
  73.1 13.0 %collective-permute-start.23 = (bf16[4,64,256]{2,1,0:T(8,128)(2,1)S(1)}, bf16[4,64,256]{2,1,0:T(8,128)(2,1)S(1)}, u32[]{:S(2)}, u32[]{:S(2)}) collective-permute-start(bf16[4,64,256]{2,1,0:T(8,128)(2,1)S(1)} %get-tuple-element.83), channel_id=1, source_target_pairs={{0,16},{8,24},{16,0},{24,8},{1,17},{9,25},{17,1},{25,9},{2,18},{10... | collective-permute-start | bytes 393224 | tf_op jit(solution)/shard_map/ppermute | solution.py:358
  73.1 13.0 %collective-permute-start.24 = (bf16[4,64,256]{2,1,0:T(8,128)(2,1)S(1)}, bf16[4,64,256]{2,1,0:T(8,128)(2,1)S(1)}, u32[]{:S(2)}, u32[]{:S(2)}) collective-permute-start(bf16[4,64,256]{2,1,0:T(8,128)(2,1)S(1)} %get-tuple-element.84), channel_id=1, source_target_pairs={{0,8},{8,0},{16,24},{24,16},{1,9},{9,1},{17,25},{25,17},{2,10},{10... | collective-permute-start | bytes 393224 | tf_op jit(solution)/shard_map/ppermute | solution.py:358

commit v5 on v4

--- a/solution.py
+++ b/solution.py
@@ -239,11 +239,11 @@
             piece = own[i][...] if j == 0 else came[j - 1][i]
             put(x_s, pl.ds((t * chips + s) * block, block), piece.astype(jnp.float32))
     gain = gain_ref[...]
-    for p in range(share):
-        n = normed(take(x_s, pl.ds(p, frames, stride=share)), gain).astype(jnp.bfloat16)
-        q_s[p] = (dot(n, wq_ref[...]) * (depth**-0.5 * LOG2E)).astype(jnp.bfloat16)
-        k_s[p] = dot(n, wk_ref[...]).astype(jnp.bfloat16)
-        v_s[p] = dot(n, wv_ref[...]).astype(jnp.bfloat16)
+    n = [normed(take(x_s, pl.ds(p, frames, stride=share)), gain) for p in range(share)]
+    n = jnp.concatenate([v.astype(jnp.bfloat16) for v in n], axis=0)
+    q_s[...] = (dot(n, wq_ref[...]) * (depth**-0.5 * LOG2E)).astype(jnp.bfloat16).reshape(q_s.shape)
+    k_s[...] = dot(n, wk_ref[...]).astype(jnp.bfloat16).reshape(k_s.shape)
+    v_s[...] = dot(n, wv_ref[...]).astype(jnp.bfloat16).reshape(v_s.shape)
     lane = lax.broadcasted_iota(jnp.int32, (frames, half), 1)
     low, high = lane < depth, lane >= depth
     ones = [c.astype(jnp.float32).astype(jnp.bfloat16) for c in (low, high)]
@@ -272,10 +272,11 @@
         )
         r = dot(w, v)
         parts.append(r[:, :half] / r[:, half:])
+    a = [jnp.concatenate(parts[2 * p : 2 * p + 2], axis=1).astype(jnp.bfloat16) for p in range(share)]
+    mixed = dot(jnp.concatenate(a, axis=0), wo_ref[...])
     for p in range(share):
-        a = jnp.concatenate(parts[2 * p : 2 * p + 2], axis=1).astype(jnp.bfloat16)
         rows = pl.ds(p, frames, stride=share)
-        put(a_s, rows, take(x_s, rows) + dot(a, wo_ref[...]))
+        put(a_s, rows, take(x_s, rows) + mixed[p * frames : (p + 1) * frames])
     for t in range(shards):
         for s in range(chips):
             outs[t][s] = take(a_s, pl.ds((t * chips + s) * block, block)).astype(jnp.bfloat16)
@@ -393,11 +394,11 @@
     early = over_chips(early)
     late = over_chips([cut(s, 1) for s in range(chips)])
     found = jnp.stack([e[half] for e in early])
-    hop = shards // 2
-    while hop:
-        sent = lax.ppermute(found, "frame", [(i, i + hop) for i in range(0, shards, 2 * hop)])
-        found = jnp.where(zf % (2 * hop) == hop, sent, found)
-        hop //= 2
+    hop = 1
+    while hop < shards:
+        sent = lax.ppermute(found, "frame", [(i, i + hop) for i in range(hop)])
+        found = jnp.where((zf >= hop) & (zf < 2 * hop), sent, found)
+        hop *= 2
     mine = [jnp.concatenate([e[:half], l], axis=0) for e, l in zip(early, late)]
     saved = spatial_ready(mine, row(gain_one), query_one, key_one, value_one, turns)
     rest = spatial_rest(

time: 87.9 us -> 87.3 us (level)
  starting transfers between devices: 44.5 us -> 40.9 us
  waiting for transfers between devices: 16.7 us -> 19.7 us
    ppermute x26, waiting for transfers between devices: 12.9 us -> 15.9 us  [swap(): return lax.ppermute(value, axis, [(i, i ^ mask) for i in range(size)])]
    ppermute x26, starting transfers between devices: 38.7 us -> 36.1 us  [swap(): return lax.ppermute(value, axis, [(i, i ^ mask) for i in range(size)])]
    ppermute x2, starting transfers between devices: 5.8 us -> 4.79 us  [shards_fn(): sent = lax.ppermute(found, 'frame', [(i, i + hop) for i in range(hop)])]
  transfers between devices with their start and end apart: 28 -> 28, of which waited for: 11 -> 13; matrix products, arithmetic and copies ran while one was open for 2% -> 2% of each run, Pallas kernels for 15% -> 16%
where the time goes in v5:
time: 87.3 us; the launch traced here: 87 us
  starting transfers between devices  40.9 us (47%)
  Pallas kernels  21.6 us (25%)
  waiting for transfers between devices  19.7 us (23%)
  local copies, waits for them, and re-layouts  3.74 us (4%)
    ppermute x26, starting transfers between devices, swap(): return lax.ppermute(value, axis, [(i, i ^ mask) for i in range(size)])  36.1 us
    ppermute x26, waiting for transfers between devices, swap(): return lax.ppermute(value, axis, [(i, i ^ mask) for i in range(size)])  15.9 us
    pallas_call x1, Pallas kernels, spatial_first(): pl.pallas_call(functools.partial(first_kernel, chips, shards, turns), in_...  6.63 us
    pallas_call x1, Pallas kernels, spatial_later(): pl.pallas_call(functools.partial(later_kernel, chips, turns, turn), in_sp...  6.32 us
    ppermute x2, starting transfers between devices, shards_fn(): sent = lax.ppermute(found, 'frame', [(i, i + hop) for i in range(hop)])  4.79 us
    ppermute x2, waiting for transfers between devices, shards_fn(): sent = lax.ppermute(found, 'frame', [(i, i + hop) for i in range(hop)])  3.79 us
    pallas_call x2, Pallas kernels, temporal(): pl.pallas_call(functools.partial(temporal_kernel, chips, shards, share, b...  3.68 us
    pallas_call x2, Pallas kernels, assemble(): pl.pallas_call(functools.partial(assemble_kernel, turn), in_specs=[pl.Blo...  2.82 us
  transfers between devices with their start and end apart: 28, of which 13 were waited for; matrix products, arithmetic and copies ran while one was open for 2% of the time, Pallas kernels for 16%

profile of v5, /device:TPU:0, one launch (start us, length us, event | category | flops | bytes accessed | tf_op | source)
XLA Modules:
  0.0 87.0 jit_solution(6310455433469366599)
XLA Ops:
  0.0 0.8 constant_dynamic-slice_fusion.1
  0.9 3.0 %collective-permute-start = (bf16[2,64,256]{2,1,0:T(8,128)(2,1)S(1)}, bf16[2,64,256]{2,1,0:T(8,128)(2,1)S(1)}, u32[]{:S(2)}, u32[]{:S(2)}) collective-permute-start(bf16[2,64,256]{2,1,0:T(8,128)(2,1)S(1)} %get-tuple-element.142), channel_id=1, source_target_pairs={{0,2},{1,3},{2,0},{3,1},{4,6},{5,7},{6,4},{7,5},{8,10},{9,11},{10,... | collective-permute-start | bytes 196616 | tf_op jit(solution)/shard_map/ppermute | solution.py:359
  3.9 1.5 %collective-permute-start.2 = (bf16[2,64,256]{2,1,0:T(8,128)(2,1)S(1)}, bf16[2,64,256]{2,1,0:T(8,128)(2,1)S(1)}, u32[]{:S(2)}, u32[]{:S(2)}) collective-permute-start(bf16[2,64,256]{2,1,0:T(8,128)(2,1)S(1)} %get-tuple-element.141), channel_id=1, source_target_pairs={{0,4},{1,5},{2,6},{3,7},{4,0},{5,1},{6,2},{7,3},{8,12},{9,13},{10,... | collective-permute-start | bytes 196616 | tf_op jit(solution)/shard_map/ppermute | solution.py:359
  5.4 1.3 %constant_dynamic-slice_fusion = (bf16[7,64,256]{2,1,0:T(8,128)(2,1)S(1)}, bf16[7,64,256]{2,1,0:T(8,128)(2,1)S(1)}, bf16[7,64,256]{2,1,0:T(8,128)(2,1)S(1)}, bf16[7,64,256]{2,1,0:T(8,128)(2,1)S(1)}) fusion(bf16[32,64,256]{2,1,0:T(8,128)(2,1)} %param.11, s32[]{:T(128)S(6)} %select_n.51, s32[]{:T(128)S(6)} %select_n.49, s32[]{:T(128)S(6)} %select_n.47, ...), kind=kLoop, calls=%fused_computation.49 | loop fusion | bytes 1835024 | tf_op jit(solution)/shard_map/dynamic_slice | solution.py:390
  6.8 3.0 %collective-permute-start.5 = (bf16[7,64,256]{2,1,0:T(8,128)(2,1)S(1)}, bf16[7,64,256]{2,1,0:T(8,128)(2,1)S(1)}, u32[]{:S(2)}, u32[]{:S(2)}) collective-permute-start(bf16[7,64,256]{2,1,0:T(8,128)(2,1)S(1)} %get-tuple-element.90), channel_id=1, source_target_pairs={{0,6},{1,7},{2,4},{3,5},{4,2},{5,3},{6,0},{7,1},{8,14},{9,15},{10,... | collective-permute-start | bytes 688136 | tf_op jit(solution)/shard_map/ppermute | solution.py:359
  9.7 0.5 collective-permute-start.3
  10.2 0.1 collective-permute-start.1
  10.4 0.9 %collective-permute-done.4 = bf16[2,64,256]{2,1,0:T(8,128)(2,1)S(1)} collective-permute-done((bf16[2,64,256]{2,1,0:T(8,128)(2,1)S(1)}, bf16[2,64,256]{2,1,0:T(8,128)(2,1)S(1)}, u32[]{:S(2)}, u32[]{:S(2)}) %collective-permute-start.4) | collective-permute-done | bytes 65568 | tf_op jit(solution)/shard_map/ppermute | solution.py:359
  11.3 3.5 %collective-permute-start.7 = (bf16[4,64,256]{2,1,0:T(8,128)(2,1)S(1)}, bf16[4,64,256]{2,1,0:T(8,128)(2,1)S(1)}, u32[]{:S(2)}, u32[]{:S(2)}) collective-permute-start(bf16[4,64,256]{2,1,0:T(8,128)(2,1)S(1)} %pad_maximum_fusion.5), channel_id=1, source_target_pairs={{0,8},{1,9},{2,10},{3,11},{4,12},{5,13},{6,14},{7,15}} | collective-permute-start | bytes 393224 | tf_op jit(solution)/shard_map/ppermute | solution.py:399
  14.9 3.7 %collective-permute-done.7 = bf16[4,64,256]{2,1,0:T(8,128)(2,1)S(1)} collective-permute-done((bf16[4,64,256]{2,1,0:T(8,128)(2,1)S(1)}, bf16[4,64,256]{2,1,0:T(8,128)(2,1)S(1)}, u32[]{:S(2)}, u32[]{:S(2)}) %collective-permute-start.7) | collective-permute-done | bytes 131104 | tf_op jit(solution)/shard_map/ppermute | solution.py:399
  18.7 1.3 %collective-permute-start.8 = (bf16[4,64,256]{2,1,0:T(8,128)(2,1)S(1)}, bf16[4,64,256]{2,1,0:T(8,128)(2,1)S(1)}, u32[]{:S(2)}, u32[]{:S(2)}) collective-permute-start(bf16[4,64,256]{2,1,0:T(8,128)(2,1)S(1)} %broadcast_select_fusion), channel_id=1, source_target_pairs={{0,16},{8,24},{1,17},{9,25},{2,18},{10,26},{3,19},{11,27},{4,20},{... | collective-permute-start | bytes 393224 | tf_op jit(solution)/shard_map/ppermute | solution.py:399
  20.3 0.1 pad_maximum_fusion
  20.4 0.1 collective-permute-start.6
  20.5 0.6 copy-done
  21.3 1.2 %spatial_ready.1 = (bf16[8,256,256]{2,1,0:T(8,128)(2,1)S(1)}, bf16[8,256,256]{2,1,0:T(8,128)(2,1)S(1)}, bf16[8,256,256]{2,1,0:T(8,128)(2,1)S(1)}) custom-call(bf16[8,64,256]{2,1,0:T(8,128)(2,1)S(1)} %get-tuple-element.95.refs_0_, bf16[8,64,256]{2,1,0:T(8,128)(2,1)S(1)} %get-tuple-element.97.refs_1_, bf16[8,64,256]{2,1,0:T(8,128)(2,1)S(1)} %get-tuple-element.99.refs_2_, ...), custom_call_target="tpu_custom_call" | custom-call | flops 40000000000 | bytes 144000000 | tf_op jit(solution)/shard_map/spatial_ready/pallas_call | solution.py:154
  22.5 0.5 collective-permute-start.9
  23.0 0.1 collective-permute-done.6.other
  23.1 0.9 %spatial_rest.1 = (bf16[8,256,256]{2,1,0:T(8,128)(2,1)S(1)}, bf16[8,256,256]{2,1,0:T(8,128)(2,1)S(1)}) custom-call(bf16[4,8,64,256]{3,2,1,0:T(8,128)(2,1)S(1)} %collective-permute-done.6.other, f32[1,256]{1,0:T(1,128)S(1)} %bitcast.91, bf16[256,256]{1,0:T(8,128)(2,1)S(1)} %copy-done.1, bf16[256,256]{1,0:T(8,128)(2,1)S(1)} %copy-done.2), custom_call_target="tpu_custom_call" | custom-call | flops 40000000000 | bytes 144000000 | tf_op jit(solution)/shard_map/spatial_rest/pallas_call | solution.py:168
  24.1 6.6 %spatial_first.1 = (bf16[4,8,8,256]{3,2,1,0:T(8,128)(2,1)S(1)}, bf16[4,8,8,256]{3,2,1,0:T(8,128)(2,1)S(1)}, bf16[4,8,8,256]{3,2,1,0:T(8,128)(2,1)S(1)}, bf16[4,8...) custom-call(s32[2]{0:T(128)S(1)} %pad_add_fusion.ids_ref, ...), custom_call_target="tpu_custom_call" | custom-call | flops 6499999744 | bytes 23400000 | tf_op jit(solution)/shard_map/spatial_first/pallas_call | solution.py:185
  30.7 5.6 %collective-permute-start.13 = (bf16[4,8,8,256]{3,2,1,0:T(8,128)(2,1)S(1)}, bf16[4,8,8,256]{3,2,1,0:T(8,128)(2,1)S(1)}, u32[]{:S(2)}, u32[]{:S(2)}) collective-permute-start(bf16[4,8,8,256]{3,2,1,0:T(8,128)(2,1)S(1)} %get-tuple-element.60), channel_id=1, source_target_pairs={{0,24},{8,16},{16,8},{24,0},{1,25},{9,17},{17,9},{25,1},{2,26},{10... | collective-permute-start | bytes 393224 | tf_op jit(solution)/shard_map/ppermute | solution.py:359
  36.3 0.6 collective-permute-start.15
  36.9 6.3 %spatial_later.1 = (bf16[4,8,8,256]{3,2,1,0:T(8,128)(2,1)S(1)}, bf16[4,8,8,256]{3,2,1,0:T(8,128)(2,1)S(1)}, bf16[4,8,8,256]{3,2,1,0:T(8,128)(2,1)S(1)}, bf16[4,8,8,256]{3,2,1,0:T(8,128)(2,1)S(1)}) custom-call(s32[2]{0:T(128)S(1)} %pad_add_fusion.ids_ref, bf16[8,64,256]{2,1,0:T(8,128)(2,1)S(1)} %get-tuple-element.95.refs_0_, ...), custom_call_target="tpu_custom_call" | custom-call | flops 6400000000 | bytes 23040000 | tf_op jit(solution)/shard_map/spatial_later/pallas_call | solution.py:203
  43.3 3.8 %collective-permute-start.10 = (bf16[4,8,8,256]{3,2,1,0:T(8,128)(2,1)S(1)}, bf16[4,8,8,256]{3,2,1,0:T(8,128)(2,1)S(1)}, u32[]{:S(2)}, u32[]{:S(2)}) collective-permute-start(bf16[4,8,8,256]{3,2,1,0:T(8,128)(2,1)S(1)} %get-tuple-element.56), channel_id=1, source_target_pairs={{0,24},{8,16},{16,8},{24,0},{1,25},{9,17},{17,9},{25,1},{2,26},{10... | collective-permute-start | bytes 393224 | tf_op jit(solution)/shard_map/ppermute | solution.py:359
  47.1 0.3 collective-permute-done.14
  47.5 1.7 %collective-permute-start.18 = (bf16[4,64,256]{2,1,0:T(8,128)(2,1)S(1)}, bf16[4,64,256]{2,1,0:T(8,128)(2,1)S(1)}, u32[]{:S(2)}, u32[]{:S(2)}) collective-permute-start(bf16[4,64,256]{2,1,0:T(8,128)(2,1)S(1)} %pad_maximum_fusion.8), channel_id=1, source_target_pairs={{0,6},{1,7},{2,4},{3,5},{4,2},{5,3},{6,0},{7,1},{8,14},{9,15},{10,... | collective-permute-start | bytes 393224 | tf_op jit(solution)/shard_map/ppermute | solution.py:359
  49.2 0.6 collective-permute-start.17
  49.8 1.4 %collective-permute-start.16 = (bf16[4,64,256]{2,1,0:T(8,128)(2,1)S(1)}, bf16[4,64,256]{2,1,0:T(8,128)(2,1)S(1)}, u32[]{:S(2)}, u32[]{:S(2)}) collective-permute-start(bf16[4,64,256]{2,1,0:T(8,128)(2,1)S(1)} %pad_maximum_fusion.6), channel_id=1, source_target_pairs={{0,2},{1,3},{2,0},{3,1},{4,6},{5,7},{6,4},{7,5},{8,10},{9,11},{10,... | collective-permute-start | bytes 393224 | tf_op jit(solution)/shard_map/ppermute | solution.py:359
  51.2 0.4 collective-permute-done.10
  51.6 1.3 %collective-permute-start.11 = (bf16[4,8,8,256]{3,2,1,0:T(8,128)(2,1)S(1)}, bf16[4,8,8,256]{3,2,1,0:T(8,128)(2,1)S(1)}, u32[]{:S(2)}, u32[]{:S(2)}) collective-permute-start(bf16[4,8,8,256]{3,2,1,0:T(8,128)(2,1)S(1)} %get-tuple-element.57), channel_id=1, source_target_pairs={{0,16},{8,24},{16,0},{24,8},{1,17},{9,25},{17,1},{25,9},{2,18},{10... | collective-permute-start | bytes 393224 | tf_op jit(solution)/shard_map/ppermute | solution.py:359
  52.9 1.6 %collective-permute-done.12 = bf16[4,8,8,256]{3,2,1,0:T(8,128)(2,1)S(1)} collective-permute-done((bf16[4,8,8,256]{3,2,1,0:T(8,128)(2,1)S(1)}, bf16[4,8,8,256]{3,2,1,0:T(8,128)(2,1)S(1)}, u32[]{:S(2)}, u32[]{:S(2)}) %collective-permute-start.12) | collective-permute-done | bytes 131104 | tf_op jit(solution)/shard_map/ppermute | solution.py:359
  54.4 0.1 collective-permute-done.18.refs_6_
  54.6 0.9 %collective-permute-done.17.refs_5_ = bf16[4,64,256]{2,1,0:T(8,128)(2,1)S(1)} collective-permute-done((bf16[4,64,256]{2,1,0:T(8,128)(2,1)S(1)}, bf16[4,64,256]{2,1,0:T(8,128)(2,1)S(1)}, u32[]{:S(2)}, u32[]{:S(2)}) %collective-permute-start.17) | collective-permute-done | bytes 131104 | tf_op jit(solution)/shard_map/ppermute | solution.py:359
  55.5 0.6 copy-done.9
  56.2 1.8 %temporal.2 = (bf16[4,64,256]{2,1,0:T(8,128)(2,1)S(1)}, bf16[4,64,256]{2,1,0:T(8,128)(2,1)S(1)}, bf16[4,64,256]{2,1,0:T(8,128)(2,1)S(1)}, bf16[4,64,256]{2,1,0:T(8,128)(2,1)S(1)}) custom-call(bf16[64,256]{1,0:T(8,128)(2,1)S(1)} %get-tuple-element.147.refs_0_, bf16[64,256]{1,0:T(8,128)(2,1)S(1)} %get-tuple-element.125.refs_1_, ...), custom_call_target="tpu_custom_call" | custom-call | flops 1900000000 | bytes 6840000 | tf_op jit(solution)/shard_map/temporal/pallas_call | solution.py:292
  58.0 1.8 %collective-permute-done.11 = bf16[4,8,8,256]{3,2,1,0:T(8,128)(2,1)S(1)} collective-permute-done((bf16[4,8,8,256]{3,2,1,0:T(8,128)(2,1)S(1)}, bf16[4,8,8,256]{3,2,1,0:T(8,128)(2,1)S(1)}, u32[]{:S(2)}, u32[]{:S(2)}) %collective-permute-start.11) | collective-permute-done | bytes 131104 | tf_op jit(solution)/shard_map/ppermute | solution.py:359
  59.9 1.7 %collective-permute-start.21 = (bf16[4,64,256]{2,1,0:T(8,128)(2,1)S(1)}, bf16[4,64,256]{2,1,0:T(8,128)(2,1)S(1)}, u32[]{:S(2)}, u32[]{:S(2)}) collective-permute-start(bf16[4,64,256]{2,1,0:T(8,128)(2,1)S(1)} %pad_maximum_fusion.11), channel_id=1, source_target_pairs={{0,6},{1,7},{2,4},{3,5},{4,2},{5,3},{6,0},{7,1},{8,14},{9,15},{10,... | collective-permute-start | bytes 393224 | tf_op jit(solution)/shard_map/ppermute | solution.py:359
  61.6 0.6 collective-permute-start.20
  62.2 1.4 %collective-permute-start.19 = (bf16[4,64,256]{2,1,0:T(8,128)(2,1)S(1)}, bf16[4,64,256]{2,1,0:T(8,128)(2,1)S(1)}, u32[]{:S(2)}, u32[]{:S(2)}) collective-permute-start(bf16[4,64,256]{2,1,0:T(8,128)(2,1)S(1)} %pad_maximum_fusion.9), channel_id=1, source_target_pairs={{0,2},{1,3},{2,0},{3,1},{4,6},{5,7},{6,4},{7,5},{8,10},{9,11},{10,... | collective-permute-start | bytes 393224 | tf_op jit(solution)/shard_map/ppermute | solution.py:359
  63.6 1.7 %collective-permute-start.25 = (bf16[4,64,256]{2,1,0:T(8,128)(2,1)S(1)}, bf16[4,64,256]{2,1,0:T(8,128)(2,1)S(1)}, u32[]{:S(2)}, u32[]{:S(2)}) collective-permute-start(bf16[4,64,256]{2,1,0:T(8,128)(2,1)S(1)} %get-tuple-element.71), channel_id=1, source_target_pairs={{0,24},{8,16},{16,8},{24,0},{1,25},{9,17},{17,9},{25,1},{2,26},{10... | collective-permute-start | bytes 393224 | tf_op jit(solution)/shard_map/ppermute | solution.py:359
  65.3 0.6 collective-permute-done.21.refs_6_
  65.8 2.1 %collective-permute-start.27 = (bf16[4,64,256]{2,1,0:T(8,128)(2,1)S(1)}, bf16[4,64,256]{2,1,0:T(8,128)(2,1)S(1)}, u32[]{:S(2)}, u32[]{:S(2)}) collective-permute-start(bf16[4,64,256]{2,1,0:T(8,128)(2,1)S(1)} %get-tuple-element.73), channel_id=1, source_target_pairs={{0,8},{8,0},{16,24},{24,16},{1,9},{9,1},{17,25},{25,17},{2,10},{10... | collective-permute-start | bytes 393224 | tf_op jit(solution)/shard_map/ppermute | solution.py:359
  68.0 1.8 %temporal.3 = (bf16[4,64,256]{2,1,0:T(8,128)(2,1)S(1)}, bf16[4,64,256]{2,1,0:T(8,128)(2,1)S(1)}, bf16[4,64,256]{2,1,0:T(8,128)(2,1)S(1)}, bf16[4,64,256]{2,1,0:T(8,128)(2,1)S(1)}) custom-call(bf16[64,256]{1,0:T(8,128)(2,1)S(1)} %get-tuple-element.105.refs_0_, bf16[64,256]{1,0:T(8,128)(2,1)S(1)} %get-tuple-element.109.refs_1_, ...), custom_call_target="tpu_custom_call" | custom-call | flops 1900000000 | bytes 6840000 | tf_op jit(solution)/shard_map/temporal/pallas_call | solution.py:292
  69.8 1.8 %collective-permute-start.22 = (bf16[4,64,256]{2,1,0:T(8,128)(2,1)S(1)}, bf16[4,64,256]{2,1,0:T(8,128)(2,1)S(1)}, u32[]{:S(2)}, u32[]{:S(2)}) collective-permute-start(bf16[4,64,256]{2,1,0:T(8,128)(2,1)S(1)} %get-tuple-element.82), channel_id=1, source_target_pairs={{0,24},{8,16},{16,8},{24,0},{1,25},{9,17},{17,9},{25,1},{2,26},{10... | collective-permute-start | bytes 393224 | tf_op jit(solution)/shard_map/ppermute | solution.py:359
  71.6 3.0 %collective-permute-start.24 = (bf16[4,64,256]{2,1,0:T(8,128)(2,1)S(1)}, bf16[4,64,256]{2,1,0:T(8,128)(2,1)S(1)}, u32[]{:S(2)}, u32[]{:S(2)}) collective-permute-start(bf16[4,64,256]{2,1,0:T(8,128)(2,1)S(1)} %get-tuple-element.84), channel_id=1, source_target_pairs={{0,8},{8,0},{16,24},{24,16},{1,9},{9,1},{17,25},{25,17},{2,10},{10... | collective-permute-start | bytes 393224 | tf_op jit(solution)/shard_map/ppermute | solution.py:359
  74.7 6.5 %collective-permute-done.26 = bf16[4,64,256]{2,1,0:T(8,128)(2,1)S(1)} collective-permute-done((bf16[4,64,256]{2,1,0:T(8,128)(2,1)S(1)}, bf16[4,64,256]{2,1,0:T(8,128)(2,1)S(1)}, u32[]{:S(2)}, u32[]{:S(2)}) %collective-permute-start.26) | collective-permute-done | bytes 131104 | tf_op jit(solution)/shard_map/ppermute | solution.py:359
  81.2 1.4 %assemble.2.refs_4_ = bf16[32,64,256]{2,1,0:T(8,128)(2,1)} custom-call(s32[2]{0:T(128)S(1)} %pad_add_fusion.ids_ref, bf16[4,8,8,256]{3,2,1,0:T(8,128)(2,1)S(1)} %bitcast.95, bf16[4,8,8,256]{3,2,1,0:T(8,128)(2,1)S(1)} %bitcast.84, bf16[4,8,8,256]{3,2,1,0:T(8,128)(2,1)S(1)} %bitcast.85, ...), custom_call_target="tpu_custom_call", output_to_operand_aliasing={{}: (5, {})} | custom-call | flops 60000002048 | bytes 216000000 | tf_op jit(solution)/shard_map/assemble/pallas_call | solution.py:331
  82.6 2.8 %collective-permute-done.23 = bf16[4,64,256]{2,1,0:T(8,128)(2,1)S(1)} collective-permute-done((bf16[4,64,256]{2,1,0:T(8,128)(2,1)S(1)}, bf16[4,64,256]{2,1,0:T(8,128)(2,1)S(1)}, u32[]{:S(2)}, u32[]{:S(2)}) %collective-permute-start.23) | collective-permute-done | bytes 131104 | tf_op jit(solution)/shard_map/ppermute | solution.py:359
  85.4 1.4 %assemble.3 = bf16[32,64,256]{2,1,0:T(8,128)(2,1)} custom-call(s32[2]{0:T(128)S(1)} %pad_add_fusion.ids_ref, bf16[4,8,8,256]{3,2,1,0:T(8,128)(2,1)S(1)} %bitcast.96, bf16[4,8,8,256]{3,2,1,0:T(8,128)(2,1)S(1)} %bitcast.87, bf16[4,8,8,256]{3,2,1,0:T(8,128)(2,1)S(1)} %bitcast.88, bf16[4,8,8,256]{3,2,1,0:T(8,128)(2,1)S(1)} %bitcast.89, ...), custom_call_target="tpu_custom_call", output_to_operand_aliasing={{}: (5, {})} | custom-call | flops 1000000000 | bytes 3600000 | tf_op jit(solution)/shard_map/assemble/pallas_call | solution.py:331
  (64 shorter events, 0.9 us)
Async XLA Ops:
  0.9 9.4 %collective-permute-start = (bf16[2,64,256]{2,1,0:T(8,128)(2,1)S(1)}, bf16[2,64,256]{2,1,0:T(8,128)(2,1)S(1)}, u32[]{:S(2)}, u32[]{:S(2)}) collective-permute-start(bf16[2,64,256]{2,1,0:T(8,128)(2,1)S(1)} %get-tuple-element.142), channel_id=1, source_target_pairs={{0,2},{1,3},{2,0},{3,1},{4,6},{5,7},{6,4},{7,5},{8,10},{9,11},{10,... | collective-permute-start | bytes 196616 | tf_op jit(solution)/shard_map/ppermute | solution.py:359
  3.9 6.5 %collective-permute-start.2 = (bf16[2,64,256]{2,1,0:T(8,128)(2,1)S(1)}, bf16[2,64,256]{2,1,0:T(8,128)(2,1)S(1)}, u32[]{:S(2)}, u32[]{:S(2)}) collective-permute-start(bf16[2,64,256]{2,1,0:T(8,128)(2,1)S(1)} %get-tuple-element.141), channel_id=1, source_target_pairs={{0,4},{1,5},{2,6},{3,7},{4,0},{5,1},{6,2},{7,3},{8,12},{9,13},{10,... | collective-permute-start | bytes 196616 | tf_op jit(solution)/shard_map/ppermute | solution.py:359
  5.4 5.9 %collective-permute-start.4 = (bf16[2,64,256]{2,1,0:T(8,128)(2,1)S(1)}, bf16[2,64,256]{2,1,0:T(8,128)(2,1)S(1)}, u32[]{:S(2)}, u32[]{:S(2)}) collective-permute-start(bf16[2,64,256]{2,1,0:T(8,128)(2,1)S(1)} %get-tuple-element.140), channel_id=1, source_target_pairs={{0,6},{1,7},{2,4},{3,5},{4,2},{5,3},{6,0},{7,1},{8,14},{9,15},{10,... | collective-permute-start | bytes 196616 | tf_op jit(solution)/shard_map/ppermute | solution.py:359
  6.8 13.2 %collective-permute-start.5 = (bf16[7,64,256]{2,1,0:T(8,128)(2,1)S(1)}, bf16[7,64,256]{2,1,0:T(8,128)(2,1)S(1)}, u32[]{:S(2)}, u32[]{:S(2)}) collective-permute-start(bf16[7,64,256]{2,1,0:T(8,128)(2,1)S(1)} %get-tuple-element.90), channel_id=1, source_target_pairs={{0,6},{1,7},{2,4},{3,5},{4,2},{5,3},{6,0},{7,1},{8,14},{9,15},{10,... | collective-permute-start | bytes 688136 | tf_op jit(solution)/shard_map/ppermute | solution.py:359
  9.7 10.4 %collective-permute-start.3 = (bf16[7,64,256]{2,1,0:T(8,128)(2,1)S(1)}, bf16[7,64,256]{2,1,0:T(8,128)(2,1)S(1)}, u32[]{:S(2)}, u32[]{:S(2)}) collective-permute-start(bf16[7,64,256]{2,1,0:T(8,128)(2,1)S(1)} %get-tuple-element.91), channel_id=1, source_target_pairs={{0,4},{1,5},{2,6},{3,7},{4,0},{5,1},{6,2},{7,3},{8,12},{9,13},{10,... | collective-permute-start | bytes 688136 | tf_op jit(solution)/shard_map/ppermute | solution.py:359
  10.2 9.9 %collective-permute-start.1 = (bf16[7,64,256]{2,1,0:T(8,128)(2,1)S(1)}, bf16[7,64,256]{2,1,0:T(8,128)(2,1)S(1)}, u32[]{:S(2)}, u32[]{:S(2)}) collective-permute-start(bf16[7,64,256]{2,1,0:T(8,128)(2,1)S(1)} %get-tuple-element.92), channel_id=1, source_target_pairs={{0,2},{1,3},{2,0},{3,1},{4,6},{5,7},{6,4},{7,5},{8,10},{9,11},{10,... | collective-permute-start | bytes 688136 | tf_op jit(solution)/shard_map/ppermute | solution.py:359
  11.3 7.4 %collective-permute-start.7 = (bf16[4,64,256]{2,1,0:T(8,128)(2,1)S(1)}, bf16[4,64,256]{2,1,0:T(8,128)(2,1)S(1)}, u32[]{:S(2)}, u32[]{:S(2)}) collective-permute-start(bf16[4,64,256]{2,1,0:T(8,128)(2,1)S(1)} %pad_maximum_fusion.5), channel_id=1, source_target_pairs={{0,8},{1,9},{2,10},{3,11},{4,12},{5,13},{6,14},{7,15}} | collective-permute-start | bytes 393224 | tf_op jit(solution)/shard_map/ppermute | solution.py:399
  18.7 3.8 %collective-permute-start.8 = (bf16[4,64,256]{2,1,0:T(8,128)(2,1)S(1)}, bf16[4,64,256]{2,1,0:T(8,128)(2,1)S(1)}, u32[]{:S(2)}, u32[]{:S(2)}) collective-permute-start(bf16[4,64,256]{2,1,0:T(8,128)(2,1)S(1)} %broadcast_select_fusion), channel_id=1, source_target_pairs={{0,16},{8,24},{1,17},{9,25},{2,18},{10,26},{3,19},{11,27},{4,20},{... | collective-permute-start | bytes 393224 | tf_op jit(solution)/shard_map/ppermute | solution.py:399
  20.2 0.9 %copy-start = (bf16[256,256]{1,0:T(8,128)(2,1)S(1)}, bf16[256,256]{1,0:T(8,128)(2,1)}, u32[]{:S(2)}) copy-start(bf16[256,256]{1,0:T(8,128)(2,1)} %refs_5_.1) | copy-start | bytes 393220
  20.2 1.0 %copy-start.1 = (bf16[256,256]{1,0:T(8,128)(2,1)S(1)}, bf16[256,256]{1,0:T(8,128)(2,1)}, u32[]{:S(2)}) copy-start(bf16[256,256]{1,0:T(8,128)(2,1)} %refs_7_.3) | copy-start | bytes 393220
  20.3 1.0 %copy-start.2 = (bf16[256,256]{1,0:T(8,128)(2,1)S(1)}, bf16[256,256]{1,0:T(8,128)(2,1)}, u32[]{:S(2)}) copy-start(bf16[256,256]{1,0:T(8,128)(2,1)} %refs_8_.3) | copy-start | bytes 393220
  20.4 2.7 %collective-permute-start.6 = (bf16[4,8,64,256]{3,2,1,0:T(8,128)(2,1)S(1)}, bf16[4,8,64,256]{3,2,1,0:T(8,128)(2,1)S(1)}, u32[]{:S(2)}, u32[]{:S(2)}) collective-permute-start(bf16[4,8,64,256]{3,2,1,0:T(8,128)(2,1)S(1)} %pad_maximum_fusion), channel_id=1, source_target_pairs={{0,1},{1,0},{2,3},{3,2},{4,5},{5,4},{6,7},{7,6},{8,9},{9,8},{10,11... | collective-permute-start | bytes 3145736 | tf_op jit(solution)/shard_map/ppermute | solution.py:359
  20.5 0.8 copy-start.8
  22.5 1.5 %copy-start.3 = (bf16[256,256]{1,0:T(8,128)(2,1)S(1)}, bf16[256,256]{1,0:T(8,128)(2,1)}, u32[]{:S(2)}) copy-start(bf16[256,256]{1,0:T(8,128)(2,1)} %refs_13_.1) | copy-start | bytes 393220
  22.5 1.5 %collective-permute-start.9 = (bf16[4,64,256]{2,1,0:T(8,128)(2,1)S(1)}, bf16[4,64,256]{2,1,0:T(8,128)(2,1)S(1)}, u32[]{:S(2)}, u32[]{:S(2)}) collective-permute-start(bf16[4,64,256]{2,1,0:T(8,128)(2,1)S(1)} %broadcast_select_fusion.1.refs_4_), channel_id=1, source_target_pairs={{0,1},{1,0},{2,3},{3,2},{4,5},{5,4},{6,7},{7,6},{8,9},{9,8},{10,11... | collective-permute-start | bytes 393224 | tf_op jit(solution)/shard_map/ppermute | solution.py:359
  30.7 16.4 %collective-permute-start.13 = (bf16[4,8,8,256]{3,2,1,0:T(8,128)(2,1)S(1)}, bf16[4,8,8,256]{3,2,1,0:T(8,128)(2,1)S(1)}, u32[]{:S(2)}, u32[]{:S(2)}) collective-permute-start(bf16[4,8,8,256]{3,2,1,0:T(8,128)(2,1)S(1)} %get-tuple-element.60), channel_id=1, source_target_pairs={{0,24},{8,16},{16,8},{24,0},{1,25},{9,17},{17,9},{25,1},{2,26},{10... | collective-permute-start | bytes 393224 | tf_op jit(solution)/shard_map/ppermute | solution.py:359
  36.3 11.1 %collective-permute-start.14 = (bf16[4,8,8,256]{3,2,1,0:T(8,128)(2,1)S(1)}, bf16[4,8,8,256]{3,2,1,0:T(8,128)(2,1)S(1)}, u32[]{:S(2)}, u32[]{:S(2)}) collective-permute-start(bf16[4,8,8,256]{3,2,1,0:T(8,128)(2,1)S(1)} %get-tuple-element.61), channel_id=1, source_target_pairs={{0,16},{8,24},{16,0},{24,8},{1,17},{9,25},{17,1},{25,9},{2,18},{10... | collective-permute-start | bytes 393224 | tf_op jit(solution)/shard_map/ppermute | solution.py:359
  36.3 11.1 %collective-permute-start.15 = (bf16[4,8,8,256]{3,2,1,0:T(8,128)(2,1)S(1)}, bf16[4,8,8,256]{3,2,1,0:T(8,128)(2,1)S(1)}, u32[]{:S(2)}, u32[]{:S(2)}) collective-permute-start(bf16[4,8,8,256]{3,2,1,0:T(8,128)(2,1)S(1)} %get-tuple-element.62), channel_id=1, source_target_pairs={{0,8},{8,0},{16,24},{24,16},{1,9},{9,1},{17,25},{25,17},{2,10},{10... | collective-permute-start | bytes 393224 | tf_op jit(solution)/shard_map/ppermute | solution.py:359
  36.9 18.5 %copy-start.6 = (bf16[256,256]{1,0:T(8,128)(2,1)S(1)}, bf16[256,256]{1,0:T(8,128)(2,1)}, u32[]{:S(2)}) copy-start(bf16[256,256]{1,0:T(8,128)(2,1)} %refs_10_.3) | copy-start | bytes 393220
  36.9 18.5 %copy-start.7 = (bf16[256,256]{1,0:T(8,128)(2,1)S(1)}, bf16[256,256]{1,0:T(8,128)(2,1)}, u32[]{:S(2)}) copy-start(bf16[256,256]{1,0:T(8,128)(2,1)} %refs_11_.3) | copy-start | bytes 393220
  43.3 8.3 %collective-permute-start.10 = (bf16[4,8,8,256]{3,2,1,0:T(8,128)(2,1)S(1)}, bf16[4,8,8,256]{3,2,1,0:T(8,128)(2,1)S(1)}, u32[]{:S(2)}, u32[]{:S(2)}) collective-permute-start(bf16[4,8,8,256]{3,2,1,0:T(8,128)(2,1)S(1)} %get-tuple-element.56), channel_id=1, source_target_pairs={{0,24},{8,16},{16,8},{24,0},{1,25},{9,17},{17,9},{25,1},{2,26},{10... | collective-permute-start | bytes 393224 | tf_op jit(solution)/shard_map/ppermute | solution.py:359
  47.1 7.4 %collective-permute-start.12 = (bf16[4,8,8,256]{3,2,1,0:T(8,128)(2,1)S(1)}, bf16[4,8,8,256]{3,2,1,0:T(8,128)(2,1)S(1)}, u32[]{:S(2)}, u32[]{:S(2)}) collective-permute-start(bf16[4,8,8,256]{3,2,1,0:T(8,128)(2,1)S(1)} %get-tuple-element.58), channel_id=1, source_target_pairs={{0,8},{8,0},{16,24},{24,16},{1,9},{9,1},{17,25},{25,17},{2,10},{10... | collective-permute-start | bytes 393224 | tf_op jit(solution)/shard_map/ppermute | solution.py:359
  47.5 7.1 %collective-permute-start.18 = (bf16[4,64,256]{2,1,0:T(8,128)(2,1)S(1)}, bf16[4,64,256]{2,1,0:T(8,128)(2,1)S(1)}, u32[]{:S(2)}, u32[]{:S(2)}) collective-permute-start(bf16[4,64,256]{2,1,0:T(8,128)(2,1)S(1)} %pad_maximum_fusion.8), channel_id=1, source_target_pairs={{0,6},{1,7},{2,4},{3,5},{4,2},{5,3},{6,0},{7,1},{8,14},{9,15},{10,... | collective-permute-start | bytes 393224 | tf_op jit(solution)/shard_map/ppermute | solution.py:359
  49.2 6.3 %collective-permute-start.17 = (bf16[4,64,256]{2,1,0:T(8,128)(2,1)S(1)}, bf16[4,64,256]{2,1,0:T(8,128)(2,1)S(1)}, u32[]{:S(2)}, u32[]{:S(2)}) collective-permute-start(bf16[4,64,256]{2,1,0:T(8,128)(2,1)S(1)} %pad_maximum_fusion.7), channel_id=1, source_target_pairs={{0,4},{1,5},{2,6},{3,7},{4,0},{5,1},{6,2},{7,3},{8,12},{9,13},{10,... | collective-permute-start | bytes 393224 | tf_op jit(solution)/shard_map/ppermute | solution.py:359
  49.8 5.7 %copy-start.4 = (bf16[256,256]{1,0:T(8,128)(2,1)S(1)}, bf16[256,256]{1,0:T(8,128)(2,1)}, u32[]{:S(2)}) copy-start(bf16[256,256]{1,0:T(8,128)(2,1)} %refs_8_.5) | copy-start | bytes 393220
  49.8 5.8 %copy-start.5 = (bf16[256,256]{1,0:T(8,128)(2,1)S(1)}, bf16[256,256]{1,0:T(8,128)(2,1)}, u32[]{:S(2)}) copy-start(bf16[256,256]{1,0:T(8,128)(2,1)} %refs_9_.5) | copy-start | bytes 393220
  49.8 5.7 %collective-permute-start.16 = (bf16[4,64,256]{2,1,0:T(8,128)(2,1)S(1)}, bf16[4,64,256]{2,1,0:T(8,128)(2,1)S(1)}, u32[]{:S(2)}, u32[]{:S(2)}) collective-permute-start(bf16[4,64,256]{2,1,0:T(8,128)(2,1)S(1)} %pad_maximum_fusion.6), channel_id=1, source_target_pairs={{0,2},{1,3},{2,0},{3,1},{4,6},{5,7},{6,4},{7,5},{8,10},{9,11},{10,... | collective-permute-start | bytes 393224 | tf_op jit(solution)/shard_map/ppermute | solution.py:359
  51.6 8.2 %collective-permute-start.11 = (bf16[4,8,8,256]{3,2,1,0:T(8,128)(2,1)S(1)}, bf16[4,8,8,256]{3,2,1,0:T(8,128)(2,1)S(1)}, u32[]{:S(2)}, u32[]{:S(2)}) collective-permute-start(bf16[4,8,8,256]{3,2,1,0:T(8,128)(2,1)S(1)} %get-tuple-element.57), channel_id=1, source_target_pairs={{0,16},{8,24},{16,0},{24,8},{1,17},{9,25},{17,1},{25,9},{2,18},{10... | collective-permute-start | bytes 393224 | tf_op jit(solution)/shard_map/ppermute | solution.py:359
  55.5 0.7 copy-start.9
  59.9 6.0 %collective-permute-start.21 = (bf16[4,64,256]{2,1,0:T(8,128)(2,1)S(1)}, bf16[4,64,256]{2,1,0:T(8,128)(2,1)S(1)}, u32[]{:S(2)}, u32[]{:S(2)}) collective-permute-start(bf16[4,64,256]{2,1,0:T(8,128)(2,1)S(1)} %pad_maximum_fusion.11), channel_id=1, source_target_pairs={{0,6},{1,7},{2,4},{3,5},{4,2},{5,3},{6,0},{7,1},{8,14},{9,15},{10,... | collective-permute-start | bytes 393224 | tf_op jit(solution)/shard_map/ppermute | solution.py:359
  61.6 6.4 %collective-permute-start.20 = (bf16[4,64,256]{2,1,0:T(8,128)(2,1)S(1)}, bf16[4,64,256]{2,1,0:T(8,128)(2,1)S(1)}, u32[]{:S(2)}, u32[]{:S(2)}) collective-permute-start(bf16[4,64,256]{2,1,0:T(8,128)(2,1)S(1)} %pad_maximum_fusion.10), channel_id=1, source_target_pairs={{0,4},{1,5},{2,6},{3,7},{4,0},{5,1},{6,2},{7,3},{8,12},{9,13},{10,... | collective-permute-start | bytes 393224 | tf_op jit(solution)/shard_map/ppermute | solution.py:359
  62.2 5.8 %collective-permute-start.19 = (bf16[4,64,256]{2,1,0:T(8,128)(2,1)S(1)}, bf16[4,64,256]{2,1,0:T(8,128)(2,1)S(1)}, u32[]{:S(2)}, u32[]{:S(2)}) collective-permute-start(bf16[4,64,256]{2,1,0:T(8,128)(2,1)S(1)} %pad_maximum_fusion.9), channel_id=1, source_target_pairs={{0,2},{1,3},{2,0},{3,1},{4,6},{5,7},{6,4},{7,5},{8,10},{9,11},{10,... | collective-permute-start | bytes 393224 | tf_op jit(solution)/shard_map/ppermute | solution.py:359
  63.6 8.1 %collective-permute-start.25 = (bf16[4,64,256]{2,1,0:T(8,128)(2,1)S(1)}, bf16[4,64,256]{2,1,0:T(8,128)(2,1)S(1)}, u32[]{:S(2)}, u32[]{:S(2)}) collective-permute-start(bf16[4,64,256]{2,1,0:T(8,128)(2,1)S(1)} %get-tuple-element.71), channel_id=1, source_target_pairs={{0,24},{8,16},{16,8},{24,0},{1,25},{9,17},{17,9},{25,1},{2,26},{10... | collective-permute-start | bytes 393224 | tf_op jit(solution)/shard_map/ppermute | solution.py:359
  65.3 15.9 %collective-permute-start.26 = (bf16[4,64,256]{2,1,0:T(8,128)(2,1)S(1)}, bf16[4,64,256]{2,1,0:T(8,128)(2,1)S(1)}, u32[]{:S(2)}, u32[]{:S(2)}) collective-permute-start(bf16[4,64,256]{2,1,0:T(8,128)(2,1)S(1)} %get-tuple-element.72), channel_id=1, source_target_pairs={{0,16},{8,24},{16,0},{24,8},{1,17},{9,25},{17,1},{25,9},{2,18},{10... | collective-permute-start | bytes 393224 | tf_op jit(solution)/shard_map/ppermute | solution.py:359
  65.8 15.4 %collective-permute-start.27 = (bf16[4,64,256]{2,1,0:T(8,128)(2,1)S(1)}, bf16[4,64,256]{2,1,0:T(8,128)(2,1)S(1)}, u32[]{:S(2)}, u32[]{:S(2)}) collective-permute-start(bf16[4,64,256]{2,1,0:T(8,128)(2,1)S(1)} %get-tuple-element.73), channel_id=1, source_target_pairs={{0,8},{8,0},{16,24},{24,16},{1,9},{9,1},{17,25},{25,17},{2,10},{10... | collective-permute-start | bytes 393224 | tf_op jit(solution)/shard_map/ppermute | solution.py:359
  69.8 12.8 %collective-permute-start.22 = (bf16[4,64,256]{2,1,0:T(8,128)(2,1)S(1)}, bf16[4,64,256]{2,1,0:T(8,128)(2,1)S(1)}, u32[]{:S(2)}, u32[]{:S(2)}) collective-permute-start(bf16[4,64,256]{2,1,0:T(8,128)(2,1)S(1)} %get-tuple-element.82), channel_id=1, source_target_pairs={{0,24},{8,16},{16,8},{24,0},{1,25},{9,17},{17,9},{25,1},{2,26},{10... | collective-permute-start | bytes 393224 | tf_op jit(solution)/shard_map/ppermute | solution.py:359
  71.6 13.8 %collective-permute-start.23 = (bf16[4,64,256]{2,1,0:T(8,128)(2,1)S(1)}, bf16[4,64,256]{2,1,0:T(8,128)(2,1)S(1)}, u32[]{:S(2)}, u32[]{:S(2)}) collective-permute-start(bf16[4,64,256]{2,1,0:T(8,128)(2,1)S(1)} %get-tuple-element.83), channel_id=1, source_target_pairs={{0,16},{8,24},{16,0},{24,8},{1,17},{9,25},{17,1},{25,9},{2,18},{10... | collective-permute-start | bytes 393224 | tf_op jit(solution)/shard_map/ppermute | solution.py:359
  71.6 13.8 %collective-permute-start.24 = (bf16[4,64,256]{2,1,0:T(8,128)(2,1)S(1)}, bf16[4,64,256]{2,1,0:T(8,128)(2,1)S(1)}, u32[]{:S(2)}, u32[]{:S(2)}) collective-permute-start(bf16[4,64,256]{2,1,0:T(8,128)(2,1)S(1)} %get-tuple-element.84), channel_id=1, source_target_pairs={{0,8},{8,0},{16,24},{24,16},{1,9},{9,1},{17,25},{25,17},{2,10},{10... | collective-permute-start | bytes 393224 | tf_op jit(solution)/shard_map/ppermute | solution.py:359

commit v6 on v5

--- a/solution.py
+++ b/solution.py
@@ -310,19 +310,24 @@
     pieces, (_, out_ref, held, sem) = refs[:shards], refs[shards:]
     chips, frames, step, _ = pieces[0].shape
     run = shards * step
+
+    def put_back(s):
+        at = pl.ds((s ^ ids_ref[1]) * frames, frames)
+        return pltpu.make_async_copy(
+            held.at[s], out_ref.at[at, pl.ds(turn * run, run), :], sem.at[s]
+        )
+
     for z in range(shards):
 
         @pl.when(ids_ref[0] == z)
         def _():
             for s in range(chips):
                 got = [pieces[mask(g ^ z, shards)][s].astype(jnp.float32) for g in range(shards)]
-                held[pl.ds((s ^ ids_ref[1]) * frames, frames)] = jnp.concatenate(got, axis=1).astype(
-                    jnp.bfloat16
-                )
-
-    copy = pltpu.make_async_copy(held, out_ref.at[:, pl.ds(turn * run, run), :], sem)
-    copy.start()
-    copy.wait()
+                held[s] = jnp.concatenate(got, axis=1).astype(jnp.bfloat16)
+                put_back(s).start()
+
+    for s in range(chips):
+        put_back(s).wait()
 
 
 def assemble(ids, pieces, whole, turn):
@@ -336,8 +341,8 @@
         out_specs=pl.BlockSpec(memory_space=pl.ANY),
         out_shape=jax.ShapeDtypeStruct(whole.shape, whole.dtype),
         scratch_shapes=[
-            pltpu.VMEM((chips * frames, shards * step, width), jnp.bfloat16),
-            pltpu.SemaphoreType.DMA(()),
+            pltpu.VMEM((chips, frames, shards * step, width), jnp.bfloat16),
+            pltpu.SemaphoreType.DMA((chips,)),
         ],
         input_output_aliases={shards + 1: 0},
         compiler_params=params(),

time: 87.3 us -> 87.3 us (level)
  no operation moved by 1% of the time
where the time goes in v6:
time: 87.3 us; the launch traced here: 87 us
  starting transfers between devices  40.9 us (47%)
  Pallas kernels  21.5 us (25%)
  waiting for transfers between devices  19.8 us (23%)
  local copies, waits for them, and re-layouts  3.74 us (4%)
    ppermute x26, starting transfers between devices, swap(): return lax.ppermute(value, axis, [(i, i ^ mask) for i in range(size)])  36.1 us
    ppermute x26, waiting for transfers between devices, swap(): return lax.ppermute(value, axis, [(i, i ^ mask) for i in range(size)])  16 us
    pallas_call x1, Pallas kernels, spatial_first(): pl.pallas_call(functools.partial(first_kernel, chips, shards, turns), in_...  6.63 us
    pallas_call x1, Pallas kernels, spatial_later(): pl.pallas_call(functools.partial(later_kernel, chips, turns, turn), in_sp...  6.32 us
    ppermute x2, starting transfers between devices, shards_fn(): sent = lax.ppermute(found, 'frame', [(i, i + hop) for i in range(hop)])  4.79 us
    ppermute x2, waiting for transfers between devices, shards_fn(): sent = lax.ppermute(found, 'frame', [(i, i + hop) for i in range(hop)])  3.79 us
    pallas_call x2, Pallas kernels, temporal(): pl.pallas_call(functools.partial(temporal_kernel, chips, shards, share, b...  3.68 us
    pallas_call x2, Pallas kernels, assemble(): pl.pallas_call(functools.partial(assemble_kernel, turn), in_specs=[pl.Blo...  2.75 us
  transfers between devices with their start and end apart: 28, of which 13 were waited for; matrix products, arithmetic and copies ran while one was open for 2% of the time, Pallas kernels for 16%

profile of v6, /device:TPU:0, one launch (start us, length us, event | category | flops | bytes accessed | tf_op | source)
XLA Modules:
  0.0 87.0 jit_solution(8854211126202499986)
XLA Ops:
  0.0 0.8 constant_dynamic-slice_fusion.1
  0.9 3.0 %collective-permute-start = (bf16[2,64,256]{2,1,0:T(8,128)(2,1)S(1)}, bf16[2,64,256]{2,1,0:T(8,128)(2,1)S(1)}, u32[]{:S(2)}, u32[]{:S(2)}) collective-permute-start(bf16[2,64,256]{2,1,0:T(8,128)(2,1)S(1)} %get-tuple-element.142), channel_id=1, source_target_pairs={{0,2},{1,3},{2,0},{3,1},{4,6},{5,7},{6,4},{7,5},{8,10},{9,11},{10,... | collective-permute-start | bytes 196616 | tf_op jit(solution)/shard_map/ppermute | solution.py:364
  3.9 1.5 %collective-permute-start.2 = (bf16[2,64,256]{2,1,0:T(8,128)(2,1)S(1)}, bf16[2,64,256]{2,1,0:T(8,128)(2,1)S(1)}, u32[]{:S(2)}, u32[]{:S(2)}) collective-permute-start(bf16[2,64,256]{2,1,0:T(8,128)(2,1)S(1)} %get-tuple-element.141), channel_id=1, source_target_pairs={{0,4},{1,5},{2,6},{3,7},{4,0},{5,1},{6,2},{7,3},{8,12},{9,13},{10,... | collective-permute-start | bytes 196616 | tf_op jit(solution)/shard_map/ppermute | solution.py:364
  5.4 1.3 %constant_dynamic-slice_fusion = (bf16[7,64,256]{2,1,0:T(8,128)(2,1)S(1)}, bf16[7,64,256]{2,1,0:T(8,128)(2,1)S(1)}, bf16[7,64,256]{2,1,0:T(8,128)(2,1)S(1)}, bf16[7,64,256]{2,1,0:T(8,128)(2,1)S(1)}) fusion(bf16[32,64,256]{2,1,0:T(8,128)(2,1)} %param.11, s32[]{:T(128)S(6)} %select_n.51, s32[]{:T(128)S(6)} %select_n.49, s32[]{:T(128)S(6)} %select_n.47, ...), kind=kLoop, calls=%fused_computation.49 | loop fusion | bytes 1835024 | tf_op jit(solution)/shard_map/dynamic_slice | solution.py:395
  6.8 3.0 %collective-permute-start.5 = (bf16[7,64,256]{2,1,0:T(8,128)(2,1)S(1)}, bf16[7,64,256]{2,1,0:T(8,128)(2,1)S(1)}, u32[]{:S(2)}, u32[]{:S(2)}) collective-permute-start(bf16[7,64,256]{2,1,0:T(8,128)(2,1)S(1)} %get-tuple-element.90), channel_id=1, source_target_pairs={{0,6},{1,7},{2,4},{3,5},{4,2},{5,3},{6,0},{7,1},{8,14},{9,15},{10,... | collective-permute-start | bytes 688136 | tf_op jit(solution)/shard_map/ppermute | solution.py:364
  9.7 0.5 collective-permute-start.3
  10.2 0.1 collective-permute-start.1
  10.4 0.9 %collective-permute-done.4 = bf16[2,64,256]{2,1,0:T(8,128)(2,1)S(1)} collective-permute-done((bf16[2,64,256]{2,1,0:T(8,128)(2,1)S(1)}, bf16[2,64,256]{2,1,0:T(8,128)(2,1)S(1)}, u32[]{:S(2)}, u32[]{:S(2)}) %collective-permute-start.4) | collective-permute-done | bytes 65568 | tf_op jit(solution)/shard_map/ppermute | solution.py:364
  11.3 3.5 %collective-permute-start.7 = (bf16[4,64,256]{2,1,0:T(8,128)(2,1)S(1)}, bf16[4,64,256]{2,1,0:T(8,128)(2,1)S(1)}, u32[]{:S(2)}, u32[]{:S(2)}) collective-permute-start(bf16[4,64,256]{2,1,0:T(8,128)(2,1)S(1)} %pad_maximum_fusion.5), channel_id=1, source_target_pairs={{0,8},{1,9},{2,10},{3,11},{4,12},{5,13},{6,14},{7,15}} | collective-permute-start | bytes 393224 | tf_op jit(solution)/shard_map/ppermute | solution.py:404
  14.9 3.7 %collective-permute-done.7 = bf16[4,64,256]{2,1,0:T(8,128)(2,1)S(1)} collective-permute-done((bf16[4,64,256]{2,1,0:T(8,128)(2,1)S(1)}, bf16[4,64,256]{2,1,0:T(8,128)(2,1)S(1)}, u32[]{:S(2)}, u32[]{:S(2)}) %collective-permute-start.7) | collective-permute-done | bytes 131104 | tf_op jit(solution)/shard_map/ppermute | solution.py:404
  18.7 1.3 %collective-permute-start.8 = (bf16[4,64,256]{2,1,0:T(8,128)(2,1)S(1)}, bf16[4,64,256]{2,1,0:T(8,128)(2,1)S(1)}, u32[]{:S(2)}, u32[]{:S(2)}) collective-permute-start(bf16[4,64,256]{2,1,0:T(8,128)(2,1)S(1)} %broadcast_select_fusion), channel_id=1, source_target_pairs={{0,16},{8,24},{1,17},{9,25},{2,18},{10,26},{3,19},{11,27},{4,20},{... | collective-permute-start | bytes 393224 | tf_op jit(solution)/shard_map/ppermute | solution.py:404
  20.3 0.1 pad_maximum_fusion
  20.4 0.1 collective-permute-start.6
  20.5 0.6 copy-done
  21.3 1.2 %spatial_ready.1 = (bf16[8,256,256]{2,1,0:T(8,128)(2,1)S(1)}, bf16[8,256,256]{2,1,0:T(8,128)(2,1)S(1)}, bf16[8,256,256]{2,1,0:T(8,128)(2,1)S(1)}) custom-call(bf16[8,64,256]{2,1,0:T(8,128)(2,1)S(1)} %get-tuple-element.95.refs_0_, bf16[8,64,256]{2,1,0:T(8,128)(2,1)S(1)} %get-tuple-element.97.refs_1_, bf16[8,64,256]{2,1,0:T(8,128)(2,1)S(1)} %get-tuple-element.99.refs_2_, ...), custom_call_target="tpu_custom_call" | custom-call | flops 40000000000 | bytes 144000000 | tf_op jit(solution)/shard_map/spatial_ready/pallas_call | solution.py:154
  22.5 0.5 collective-permute-start.9
  23.0 0.1 collective-permute-done.6.other
  23.1 0.9 %spatial_rest.1 = (bf16[8,256,256]{2,1,0:T(8,128)(2,1)S(1)}, bf16[8,256,256]{2,1,0:T(8,128)(2,1)S(1)}) custom-call(bf16[4,8,64,256]{3,2,1,0:T(8,128)(2,1)S(1)} %collective-permute-done.6.other, f32[1,256]{1,0:T(1,128)S(1)} %bitcast.91, bf16[256,256]{1,0:T(8,128)(2,1)S(1)} %copy-done.1, bf16[256,256]{1,0:T(8,128)(2,1)S(1)} %copy-done.2), custom_call_target="tpu_custom_call" | custom-call | flops 40000000000 | bytes 144000000 | tf_op jit(solution)/shard_map/spatial_rest/pallas_call | solution.py:168
  24.1 6.6 %spatial_first.1 = (bf16[4,8,8,256]{3,2,1,0:T(8,128)(2,1)S(1)}, bf16[4,8,8,256]{3,2,1,0:T(8,128)(2,1)S(1)}, bf16[4,8,8,256]{3,2,1,0:T(8,128)(2,1)S(1)}, bf16[4,8...) custom-call(s32[2]{0:T(128)S(1)} %pad_add_fusion.ids_ref, ...), custom_call_target="tpu_custom_call" | custom-call | flops 6499999744 | bytes 23400000 | tf_op jit(solution)/shard_map/spatial_first/pallas_call | solution.py:185
  30.7 5.6 %collective-permute-start.13 = (bf16[4,8,8,256]{3,2,1,0:T(8,128)(2,1)S(1)}, bf16[4,8,8,256]{3,2,1,0:T(8,128)(2,1)S(1)}, u32[]{:S(2)}, u32[]{:S(2)}) collective-permute-start(bf16[4,8,8,256]{3,2,1,0:T(8,128)(2,1)S(1)} %get-tuple-element.60), channel_id=1, source_target_pairs={{0,24},{8,16},{16,8},{24,0},{1,25},{9,17},{17,9},{25,1},{2,26},{10... | collective-permute-start | bytes 393224 | tf_op jit(solution)/shard_map/ppermute | solution.py:364
  36.3 0.6 collective-permute-start.15
  36.9 6.3 %spatial_later.1 = (bf16[4,8,8,256]{3,2,1,0:T(8,128)(2,1)S(1)}, bf16[4,8,8,256]{3,2,1,0:T(8,128)(2,1)S(1)}, bf16[4,8,8,256]{3,2,1,0:T(8,128)(2,1)S(1)}, bf16[4,8,8,256]{3,2,1,0:T(8,128)(2,1)S(1)}) custom-call(s32[2]{0:T(128)S(1)} %pad_add_fusion.ids_ref, bf16[8,64,256]{2,1,0:T(8,128)(2,1)S(1)} %get-tuple-element.95.refs_0_, ...), custom_call_target="tpu_custom_call" | custom-call | flops 6400000000 | bytes 23040000 | tf_op jit(solution)/shard_map/spatial_later/pallas_call | solution.py:203
  43.3 3.8 %collective-permute-start.10 = (bf16[4,8,8,256]{3,2,1,0:T(8,128)(2,1)S(1)}, bf16[4,8,8,256]{3,2,1,0:T(8,128)(2,1)S(1)}, u32[]{:S(2)}, u32[]{:S(2)}) collective-permute-start(bf16[4,8,8,256]{3,2,1,0:T(8,128)(2,1)S(1)} %get-tuple-element.56), channel_id=1, source_target_pairs={{0,24},{8,16},{16,8},{24,0},{1,25},{9,17},{17,9},{25,1},{2,26},{10... | collective-permute-start | bytes 393224 | tf_op jit(solution)/shard_map/ppermute | solution.py:364
  47.1 0.3 collective-permute-done.14
  47.5 1.7 %collective-permute-start.18 = (bf16[4,64,256]{2,1,0:T(8,128)(2,1)S(1)}, bf16[4,64,256]{2,1,0:T(8,128)(2,1)S(1)}, u32[]{:S(2)}, u32[]{:S(2)}) collective-permute-start(bf16[4,64,256]{2,1,0:T(8,128)(2,1)S(1)} %pad_maximum_fusion.8), channel_id=1, source_target_pairs={{0,6},{1,7},{2,4},{3,5},{4,2},{5,3},{6,0},{7,1},{8,14},{9,15},{10,... | collective-permute-start | bytes 393224 | tf_op jit(solution)/shard_map/ppermute | solution.py:364
  49.2 0.6 collective-permute-start.17
  49.8 1.4 %collective-permute-start.16 = (bf16[4,64,256]{2,1,0:T(8,128)(2,1)S(1)}, bf16[4,64,256]{2,1,0:T(8,128)(2,1)S(1)}, u32[]{:S(2)}, u32[]{:S(2)}) collective-permute-start(bf16[4,64,256]{2,1,0:T(8,128)(2,1)S(1)} %pad_maximum_fusion.6), channel_id=1, source_target_pairs={{0,2},{1,3},{2,0},{3,1},{4,6},{5,7},{6,4},{7,5},{8,10},{9,11},{10,... | collective-permute-start | bytes 393224 | tf_op jit(solution)/shard_map/ppermute | solution.py:364
  51.2 0.4 collective-permute-done.10
  51.6 1.3 %collective-permute-start.11 = (bf16[4,8,8,256]{3,2,1,0:T(8,128)(2,1)S(1)}, bf16[4,8,8,256]{3,2,1,0:T(8,128)(2,1)S(1)}, u32[]{:S(2)}, u32[]{:S(2)}) collective-permute-start(bf16[4,8,8,256]{3,2,1,0:T(8,128)(2,1)S(1)} %get-tuple-element.57), channel_id=1, source_target_pairs={{0,16},{8,24},{16,0},{24,8},{1,17},{9,25},{17,1},{25,9},{2,18},{10... | collective-permute-start | bytes 393224 | tf_op jit(solution)/shard_map/ppermute | solution.py:364
  52.9 1.6 %collective-permute-done.12 = bf16[4,8,8,256]{3,2,1,0:T(8,128)(2,1)S(1)} collective-permute-done((bf16[4,8,8,256]{3,2,1,0:T(8,128)(2,1)S(1)}, bf16[4,8,8,256]{3,2,1,0:T(8,128)(2,1)S(1)}, u32[]{:S(2)}, u32[]{:S(2)}) %collective-permute-start.12) | collective-permute-done | bytes 131104 | tf_op jit(solution)/shard_map/ppermute | solution.py:364
  54.4 0.1 collective-permute-done.18.refs_6_
  54.6 0.9 %collective-permute-done.17.refs_5_ = bf16[4,64,256]{2,1,0:T(8,128)(2,1)S(1)} collective-permute-done((bf16[4,64,256]{2,1,0:T(8,128)(2,1)S(1)}, bf16[4,64,256]{2,1,0:T(8,128)(2,1)S(1)}, u32[]{:S(2)}, u32[]{:S(2)}) %collective-permute-start.17) | collective-permute-done | bytes 131104 | tf_op jit(solution)/shard_map/ppermute | solution.py:364
  55.5 0.6 copy-done.9
  56.2 1.8 %temporal.2 = (bf16[4,64,256]{2,1,0:T(8,128)(2,1)S(1)}, bf16[4,64,256]{2,1,0:T(8,128)(2,1)S(1)}, bf16[4,64,256]{2,1,0:T(8,128)(2,1)S(1)}, bf16[4,64,256]{2,1,0:T(8,128)(2,1)S(1)}) custom-call(bf16[64,256]{1,0:T(8,128)(2,1)S(1)} %get-tuple-element.147.refs_0_, bf16[64,256]{1,0:T(8,128)(2,1)S(1)} %get-tuple-element.125.refs_1_, ...), custom_call_target="tpu_custom_call" | custom-call | flops 1900000000 | bytes 6840000 | tf_op jit(solution)/shard_map/temporal/pallas_call | solution.py:292
  58.0 1.8 %collective-permute-done.11 = bf16[4,8,8,256]{3,2,1,0:T(8,128)(2,1)S(1)} collective-permute-done((bf16[4,8,8,256]{3,2,1,0:T(8,128)(2,1)S(1)}, bf16[4,8,8,256]{3,2,1,0:T(8,128)(2,1)S(1)}, u32[]{:S(2)}, u32[]{:S(2)}) %collective-permute-start.11) | collective-permute-done | bytes 131104 | tf_op jit(solution)/shard_map/ppermute | solution.py:364
  59.9 1.7 %collective-permute-start.21 = (bf16[4,64,256]{2,1,0:T(8,128)(2,1)S(1)}, bf16[4,64,256]{2,1,0:T(8,128)(2,1)S(1)}, u32[]{:S(2)}, u32[]{:S(2)}) collective-permute-start(bf16[4,64,256]{2,1,0:T(8,128)(2,1)S(1)} %pad_maximum_fusion.11), channel_id=1, source_target_pairs={{0,6},{1,7},{2,4},{3,5},{4,2},{5,3},{6,0},{7,1},{8,14},{9,15},{10,... | collective-permute-start | bytes 393224 | tf_op jit(solution)/shard_map/ppermute | solution.py:364
  61.6 0.6 collective-permute-start.20
  62.2 1.4 %collective-permute-start.19 = (bf16[4,64,256]{2,1,0:T(8,128)(2,1)S(1)}, bf16[4,64,256]{2,1,0:T(8,128)(2,1)S(1)}, u32[]{:S(2)}, u32[]{:S(2)}) collective-permute-start(bf16[4,64,256]{2,1,0:T(8,128)(2,1)S(1)} %pad_maximum_fusion.9), channel_id=1, source_target_pairs={{0,2},{1,3},{2,0},{3,1},{4,6},{5,7},{6,4},{7,5},{8,10},{9,11},{10,... | collective-permute-start | bytes 393224 | tf_op jit(solution)/shard_map/ppermute | solution.py:364
  63.6 1.7 %collective-permute-start.25 = (bf16[4,64,256]{2,1,0:T(8,128)(2,1)S(1)}, bf16[4,64,256]{2,1,0:T(8,128)(2,1)S(1)}, u32[]{:S(2)}, u32[]{:S(2)}) collective-permute-start(bf16[4,64,256]{2,1,0:T(8,128)(2,1)S(1)} %get-tuple-element.71), channel_id=1, source_target_pairs={{0,24},{8,16},{16,8},{24,0},{1,25},{9,17},{17,9},{25,1},{2,26},{10... | collective-permute-start | bytes 393224 | tf_op jit(solution)/shard_map/ppermute | solution.py:364
  65.3 0.6 collective-permute-done.21.refs_6_
  65.8 2.1 %collective-permute-start.27 = (bf16[4,64,256]{2,1,0:T(8,128)(2,1)S(1)}, bf16[4,64,256]{2,1,0:T(8,128)(2,1)S(1)}, u32[]{:S(2)}, u32[]{:S(2)}) collective-permute-start(bf16[4,64,256]{2,1,0:T(8,128)(2,1)S(1)} %get-tuple-element.73), channel_id=1, source_target_pairs={{0,8},{8,0},{16,24},{24,16},{1,9},{9,1},{17,25},{25,17},{2,10},{10... | collective-permute-start | bytes 393224 | tf_op jit(solution)/shard_map/ppermute | solution.py:364
  68.0 1.8 %temporal.3 = (bf16[4,64,256]{2,1,0:T(8,128)(2,1)S(1)}, bf16[4,64,256]{2,1,0:T(8,128)(2,1)S(1)}, bf16[4,64,256]{2,1,0:T(8,128)(2,1)S(1)}, bf16[4,64,256]{2,1,0:T(8,128)(2,1)S(1)}) custom-call(bf16[64,256]{1,0:T(8,128)(2,1)S(1)} %get-tuple-element.105.refs_0_, bf16[64,256]{1,0:T(8,128)(2,1)S(1)} %get-tuple-element.109.refs_1_, ...), custom_call_target="tpu_custom_call" | custom-call | flops 1900000000 | bytes 6840000 | tf_op jit(solution)/shard_map/temporal/pallas_call | solution.py:292
  69.8 1.8 %collective-permute-start.22 = (bf16[4,64,256]{2,1,0:T(8,128)(2,1)S(1)}, bf16[4,64,256]{2,1,0:T(8,128)(2,1)S(1)}, u32[]{:S(2)}, u32[]{:S(2)}) collective-permute-start(bf16[4,64,256]{2,1,0:T(8,128)(2,1)S(1)} %get-tuple-element.82), channel_id=1, source_target_pairs={{0,24},{8,16},{16,8},{24,0},{1,25},{9,17},{17,9},{25,1},{2,26},{10... | collective-permute-start | bytes 393224 | tf_op jit(solution)/shard_map/ppermute | solution.py:364
  71.6 3.0 %collective-permute-start.24 = (bf16[4,64,256]{2,1,0:T(8,128)(2,1)S(1)}, bf16[4,64,256]{2,1,0:T(8,128)(2,1)S(1)}, u32[]{:S(2)}, u32[]{:S(2)}) collective-permute-start(bf16[4,64,256]{2,1,0:T(8,128)(2,1)S(1)} %get-tuple-element.84), channel_id=1, source_target_pairs={{0,8},{8,0},{16,24},{24,16},{1,9},{9,1},{17,25},{25,17},{2,10},{10... | collective-permute-start | bytes 393224 | tf_op jit(solution)/shard_map/ppermute | solution.py:364
  74.7 6.5 %collective-permute-done.26 = bf16[4,64,256]{2,1,0:T(8,128)(2,1)S(1)} collective-permute-done((bf16[4,64,256]{2,1,0:T(8,128)(2,1)S(1)}, bf16[4,64,256]{2,1,0:T(8,128)(2,1)S(1)}, u32[]{:S(2)}, u32[]{:S(2)}) %collective-permute-start.26) | collective-permute-done | bytes 131104 | tf_op jit(solution)/shard_map/ppermute | solution.py:364
  81.2 1.4 %assemble.2.refs_4_ = bf16[32,64,256]{2,1,0:T(8,128)(2,1)} custom-call(s32[2]{0:T(128)S(1)} %pad_add_fusion.ids_ref, bf16[4,8,8,256]{3,2,1,0:T(8,128)(2,1)S(1)} %bitcast.95, bf16[4,8,8,256]{3,2,1,0:T(8,128)(2,1)S(1)} %bitcast.84, bf16[4,8,8,256]{3,2,1,0:T(8,128)(2,1)S(1)} %bitcast.85, ...), custom_call_target="tpu_custom_call", output_to_operand_aliasing={{}: (5, {})} | custom-call | flops 60000002048 | bytes 216000000 | tf_op jit(solution)/shard_map/assemble/pallas_call | solution.py:336
  82.6 2.8 %collective-permute-done.23 = bf16[4,64,256]{2,1,0:T(8,128)(2,1)S(1)} collective-permute-done((bf16[4,64,256]{2,1,0:T(8,128)(2,1)S(1)}, bf16[4,64,256]{2,1,0:T(8,128)(2,1)S(1)}, u32[]{:S(2)}, u32[]{:S(2)}) %collective-permute-start.23) | collective-permute-done | bytes 131104 | tf_op jit(solution)/shard_map/ppermute | solution.py:364
  85.4 1.4 %assemble.3 = bf16[32,64,256]{2,1,0:T(8,128)(2,1)} custom-call(s32[2]{0:T(128)S(1)} %pad_add_fusion.ids_ref, bf16[4,8,8,256]{3,2,1,0:T(8,128)(2,1)S(1)} %bitcast.96, bf16[4,8,8,256]{3,2,1,0:T(8,128)(2,1)S(1)} %bitcast.87, bf16[4,8,8,256]{3,2,1,0:T(8,128)(2,1)S(1)} %bitcast.88, bf16[4,8,8,256]{3,2,1,0:T(8,128)(2,1)S(1)} %bitcast.89, ...), custom_call_target="tpu_custom_call", output_to_operand_aliasing={{}: (5, {})} | custom-call | flops 1000000000 | bytes 3600000 | tf_op jit(solution)/shard_map/assemble/pallas_call | solution.py:336
  (64 shorter events, 0.9 us)
Async XLA Ops:
  0.9 9.4 %collective-permute-start = (bf16[2,64,256]{2,1,0:T(8,128)(2,1)S(1)}, bf16[2,64,256]{2,1,0:T(8,128)(2,1)S(1)}, u32[]{:S(2)}, u32[]{:S(2)}) collective-permute-start(bf16[2,64,256]{2,1,0:T(8,128)(2,1)S(1)} %get-tuple-element.142), channel_id=1, source_target_pairs={{0,2},{1,3},{2,0},{3,1},{4,6},{5,7},{6,4},{7,5},{8,10},{9,11},{10,... | collective-permute-start | bytes 196616 | tf_op jit(solution)/shard_map/ppermute | solution.py:364
  3.9 6.5 %collective-permute-start.2 = (bf16[2,64,256]{2,1,0:T(8,128)(2,1)S(1)}, bf16[2,64,256]{2,1,0:T(8,128)(2,1)S(1)}, u32[]{:S(2)}, u32[]{:S(2)}) collective-permute-start(bf16[2,64,256]{2,1,0:T(8,128)(2,1)S(1)} %get-tuple-element.141), channel_id=1, source_target_pairs={{0,4},{1,5},{2,6},{3,7},{4,0},{5,1},{6,2},{7,3},{8,12},{9,13},{10,... | collective-permute-start | bytes 196616 | tf_op jit(solution)/shard_map/ppermute | solution.py:364
  5.4 5.9 %collective-permute-start.4 = (bf16[2,64,256]{2,1,0:T(8,128)(2,1)S(1)}, bf16[2,64,256]{2,1,0:T(8,128)(2,1)S(1)}, u32[]{:S(2)}, u32[]{:S(2)}) collective-permute-start(bf16[2,64,256]{2,1,0:T(8,128)(2,1)S(1)} %get-tuple-element.140), channel_id=1, source_target_pairs={{0,6},{1,7},{2,4},{3,5},{4,2},{5,3},{6,0},{7,1},{8,14},{9,15},{10,... | collective-permute-start | bytes 196616 | tf_op jit(solution)/shard_map/ppermute | solution.py:364
  6.8 13.2 %collective-permute-start.5 = (bf16[7,64,256]{2,1,0:T(8,128)(2,1)S(1)}, bf16[7,64,256]{2,1,0:T(8,128)(2,1)S(1)}, u32[]{:S(2)}, u32[]{:S(2)}) collective-permute-start(bf16[7,64,256]{2,1,0:T(8,128)(2,1)S(1)} %get-tuple-element.90), channel_id=1, source_target_pairs={{0,6},{1,7},{2,4},{3,5},{4,2},{5,3},{6,0},{7,1},{8,14},{9,15},{10,... | collective-permute-start | bytes 688136 | tf_op jit(solution)/shard_map/ppermute | solution.py:364
  9.7 10.4 %collective-permute-start.3 = (bf16[7,64,256]{2,1,0:T(8,128)(2,1)S(1)}, bf16[7,64,256]{2,1,0:T(8,128)(2,1)S(1)}, u32[]{:S(2)}, u32[]{:S(2)}) collective-permute-start(bf16[7,64,256]{2,1,0:T(8,128)(2,1)S(1)} %get-tuple-element.91), channel_id=1, source_target_pairs={{0,4},{1,5},{2,6},{3,7},{4,0},{5,1},{6,2},{7,3},{8,12},{9,13},{10,... | collective-permute-start | bytes 688136 | tf_op jit(solution)/shard_map/ppermute | solution.py:364
  10.2 9.9 %collective-permute-start.1 = (bf16[7,64,256]{2,1,0:T(8,128)(2,1)S(1)}, bf16[7,64,256]{2,1,0:T(8,128)(2,1)S(1)}, u32[]{:S(2)}, u32[]{:S(2)}) collective-permute-start(bf16[7,64,256]{2,1,0:T(8,128)(2,1)S(1)} %get-tuple-element.92), channel_id=1, source_target_pairs={{0,2},{1,3},{2,0},{3,1},{4,6},{5,7},{6,4},{7,5},{8,10},{9,11},{10,... | collective-permute-start | bytes 688136 | tf_op jit(solution)/shard_map/ppermute | solution.py:364
  11.3 7.4 %collective-permute-start.7 = (bf16[4,64,256]{2,1,0:T(8,128)(2,1)S(1)}, bf16[4,64,256]{2,1,0:T(8,128)(2,1)S(1)}, u32[]{:S(2)}, u32[]{:S(2)}) collective-permute-start(bf16[4,64,256]{2,1,0:T(8,128)(2,1)S(1)} %pad_maximum_fusion.5), channel_id=1, source_target_pairs={{0,8},{1,9},{2,10},{3,11},{4,12},{5,13},{6,14},{7,15}} | collective-permute-start | bytes 393224 | tf_op jit(solution)/shard_map/ppermute | solution.py:404
  18.7 3.8 %collective-permute-start.8 = (bf16[4,64,256]{2,1,0:T(8,128)(2,1)S(1)}, bf16[4,64,256]{2,1,0:T(8,128)(2,1)S(1)}, u32[]{:S(2)}, u32[]{:S(2)}) collective-permute-start(bf16[4,64,256]{2,1,0:T(8,128)(2,1)S(1)} %broadcast_select_fusion), channel_id=1, source_target_pairs={{0,16},{8,24},{1,17},{9,25},{2,18},{10,26},{3,19},{11,27},{4,20},{... | collective-permute-start | bytes 393224 | tf_op jit(solution)/shard_map/ppermute | solution.py:404
  20.2 0.9 %copy-start = (bf16[256,256]{1,0:T(8,128)(2,1)S(1)}, bf16[256,256]{1,0:T(8,128)(2,1)}, u32[]{:S(2)}) copy-start(bf16[256,256]{1,0:T(8,128)(2,1)} %refs_5_.1) | copy-start | bytes 393220
  20.2 1.0 %copy-start.1 = (bf16[256,256]{1,0:T(8,128)(2,1)S(1)}, bf16[256,256]{1,0:T(8,128)(2,1)}, u32[]{:S(2)}) copy-start(bf16[256,256]{1,0:T(8,128)(2,1)} %refs_7_.3) | copy-start | bytes 393220
  20.3 1.0 %copy-start.2 = (bf16[256,256]{1,0:T(8,128)(2,1)S(1)}, bf16[256,256]{1,0:T(8,128)(2,1)}, u32[]{:S(2)}) copy-start(bf16[256,256]{1,0:T(8,128)(2,1)} %refs_8_.3) | copy-start | bytes 393220
  20.4 2.7 %collective-permute-start.6 = (bf16[4,8,64,256]{3,2,1,0:T(8,128)(2,1)S(1)}, bf16[4,8,64,256]{3,2,1,0:T(8,128)(2,1)S(1)}, u32[]{:S(2)}, u32[]{:S(2)}) collective-permute-start(bf16[4,8,64,256]{3,2,1,0:T(8,128)(2,1)S(1)} %pad_maximum_fusion), channel_id=1, source_target_pairs={{0,1},{1,0},{2,3},{3,2},{4,5},{5,4},{6,7},{7,6},{8,9},{9,8},{10,11... | collective-permute-start | bytes 3145736 | tf_op jit(solution)/shard_map/ppermute | solution.py:364
  20.5 0.8 copy-start.8
  22.5 1.5 %copy-start.3 = (bf16[256,256]{1,0:T(8,128)(2,1)S(1)}, bf16[256,256]{1,0:T(8,128)(2,1)}, u32[]{:S(2)}) copy-start(bf16[256,256]{1,0:T(8,128)(2,1)} %refs_13_.1) | copy-start | bytes 393220
  22.5 1.5 %collective-permute-start.9 = (bf16[4,64,256]{2,1,0:T(8,128)(2,1)S(1)}, bf16[4,64,256]{2,1,0:T(8,128)(2,1)S(1)}, u32[]{:S(2)}, u32[]{:S(2)}) collective-permute-start(bf16[4,64,256]{2,1,0:T(8,128)(2,1)S(1)} %broadcast_select_fusion.1.refs_4_), channel_id=1, source_target_pairs={{0,1},{1,0},{2,3},{3,2},{4,5},{5,4},{6,7},{7,6},{8,9},{9,8},{10,11... | collective-permute-start | bytes 393224 | tf_op jit(solution)/shard_map/ppermute | solution.py:364
  30.7 16.4 %collective-permute-start.13 = (bf16[4,8,8,256]{3,2,1,0:T(8,128)(2,1)S(1)}, bf16[4,8,8,256]{3,2,1,0:T(8,128)(2,1)S(1)}, u32[]{:S(2)}, u32[]{:S(2)}) collective-permute-start(bf16[4,8,8,256]{3,2,1,0:T(8,128)(2,1)S(1)} %get-tuple-element.60), channel_id=1, source_target_pairs={{0,24},{8,16},{16,8},{24,0},{1,25},{9,17},{17,9},{25,1},{2,26},{10... | collective-permute-start | bytes 393224 | tf_op jit(solution)/shard_map/ppermute | solution.py:364
  36.3 11.1 %collective-permute-start.14 = (bf16[4,8,8,256]{3,2,1,0:T(8,128)(2,1)S(1)}, bf16[4,8,8,256]{3,2,1,0:T(8,128)(2,1)S(1)}, u32[]{:S(2)}, u32[]{:S(2)}) collective-permute-start(bf16[4,8,8,256]{3,2,1,0:T(8,128)(2,1)S(1)} %get-tuple-element.61), channel_id=1, source_target_pairs={{0,16},{8,24},{16,0},{24,8},{1,17},{9,25},{17,1},{25,9},{2,18},{10... | collective-permute-start | bytes 393224 | tf_op jit(solution)/shard_map/ppermute | solution.py:364
  36.3 11.1 %collective-permute-start.15 = (bf16[4,8,8,256]{3,2,1,0:T(8,128)(2,1)S(1)}, bf16[4,8,8,256]{3,2,1,0:T(8,128)(2,1)S(1)}, u32[]{:S(2)}, u32[]{:S(2)}) collective-permute-start(bf16[4,8,8,256]{3,2,1,0:T(8,128)(2,1)S(1)} %get-tuple-element.62), channel_id=1, source_target_pairs={{0,8},{8,0},{16,24},{24,16},{1,9},{9,1},{17,25},{25,17},{2,10},{10... | collective-permute-start | bytes 393224 | tf_op jit(solution)/shard_map/ppermute | solution.py:364
  36.9 18.5 %copy-start.6 = (bf16[256,256]{1,0:T(8,128)(2,1)S(1)}, bf16[256,256]{1,0:T(8,128)(2,1)}, u32[]{:S(2)}) copy-start(bf16[256,256]{1,0:T(8,128)(2,1)} %refs_10_.3) | copy-start | bytes 393220
  36.9 18.5 %copy-start.7 = (bf16[256,256]{1,0:T(8,128)(2,1)S(1)}, bf16[256,256]{1,0:T(8,128)(2,1)}, u32[]{:S(2)}) copy-start(bf16[256,256]{1,0:T(8,128)(2,1)} %refs_11_.3) | copy-start | bytes 393220
  43.3 8.3 %collective-permute-start.10 = (bf16[4,8,8,256]{3,2,1,0:T(8,128)(2,1)S(1)}, bf16[4,8,8,256]{3,2,1,0:T(8,128)(2,1)S(1)}, u32[]{:S(2)}, u32[]{:S(2)}) collective-permute-start(bf16[4,8,8,256]{3,2,1,0:T(8,128)(2,1)S(1)} %get-tuple-element.56), channel_id=1, source_target_pairs={{0,24},{8,16},{16,8},{24,0},{1,25},{9,17},{17,9},{25,1},{2,26},{10... | collective-permute-start | bytes 393224 | tf_op jit(solution)/shard_map/ppermute | solution.py:364
  47.1 7.4 %collective-permute-start.12 = (bf16[4,8,8,256]{3,2,1,0:T(8,128)(2,1)S(1)}, bf16[4,8,8,256]{3,2,1,0:T(8,128)(2,1)S(1)}, u32[]{:S(2)}, u32[]{:S(2)}) collective-permute-start(bf16[4,8,8,256]{3,2,1,0:T(8,128)(2,1)S(1)} %get-tuple-element.58), channel_id=1, source_target_pairs={{0,8},{8,0},{16,24},{24,16},{1,9},{9,1},{17,25},{25,17},{2,10},{10... | collective-permute-start | bytes 393224 | tf_op jit(solution)/shard_map/ppermute | solution.py:364
  47.5 7.1 %collective-permute-start.18 = (bf16[4,64,256]{2,1,0:T(8,128)(2,1)S(1)}, bf16[4,64,256]{2,1,0:T(8,128)(2,1)S(1)}, u32[]{:S(2)}, u32[]{:S(2)}) collective-permute-start(bf16[4,64,256]{2,1,0:T(8,128)(2,1)S(1)} %pad_maximum_fusion.8), channel_id=1, source_target_pairs={{0,6},{1,7},{2,4},{3,5},{4,2},{5,3},{6,0},{7,1},{8,14},{9,15},{10,... | collective-permute-start | bytes 393224 | tf_op jit(solution)/shard_map/ppermute | solution.py:364
  49.2 6.3 %collective-permute-start.17 = (bf16[4,64,256]{2,1,0:T(8,128)(2,1)S(1)}, bf16[4,64,256]{2,1,0:T(8,128)(2,1)S(1)}, u32[]{:S(2)}, u32[]{:S(2)}) collective-permute-start(bf16[4,64,256]{2,1,0:T(8,128)(2,1)S(1)} %pad_maximum_fusion.7), channel_id=1, source_target_pairs={{0,4},{1,5},{2,6},{3,7},{4,0},{5,1},{6,2},{7,3},{8,12},{9,13},{10,... | collective-permute-start | bytes 393224 | tf_op jit(solution)/shard_map/ppermute | solution.py:364
  49.8 5.7 %copy-start.4 = (bf16[256,256]{1,0:T(8,128)(2,1)S(1)}, bf16[256,256]{1,0:T(8,128)(2,1)}, u32[]{:S(2)}) copy-start(bf16[256,256]{1,0:T(8,128)(2,1)} %refs_8_.5) | copy-start | bytes 393220
  49.8 5.8 %copy-start.5 = (bf16[256,256]{1,0:T(8,128)(2,1)S(1)}, bf16[256,256]{1,0:T(8,128)(2,1)}, u32[]{:S(2)}) copy-start(bf16[256,256]{1,0:T(8,128)(2,1)} %refs_9_.5) | copy-start | bytes 393220
  49.8 5.7 %collective-permute-start.16 = (bf16[4,64,256]{2,1,0:T(8,128)(2,1)S(1)}, bf16[4,64,256]{2,1,0:T(8,128)(2,1)S(1)}, u32[]{:S(2)}, u32[]{:S(2)}) collective-permute-start(bf16[4,64,256]{2,1,0:T(8,128)(2,1)S(1)} %pad_maximum_fusion.6), channel_id=1, source_target_pairs={{0,2},{1,3},{2,0},{3,1},{4,6},{5,7},{6,4},{7,5},{8,10},{9,11},{10,... | collective-permute-start | bytes 393224 | tf_op jit(solution)/shard_map/ppermute | solution.py:364
  51.6 8.2 %collective-permute-start.11 = (bf16[4,8,8,256]{3,2,1,0:T(8,128)(2,1)S(1)}, bf16[4,8,8,256]{3,2,1,0:T(8,128)(2,1)S(1)}, u32[]{:S(2)}, u32[]{:S(2)}) collective-permute-start(bf16[4,8,8,256]{3,2,1,0:T(8,128)(2,1)S(1)} %get-tuple-element.57), channel_id=1, source_target_pairs={{0,16},{8,24},{16,0},{24,8},{1,17},{9,25},{17,1},{25,9},{2,18},{10... | collective-permute-start | bytes 393224 | tf_op jit(solution)/shard_map/ppermute | solution.py:364
  55.5 0.7 copy-start.9
  59.9 6.0 %collective-permute-start.21 = (bf16[4,64,256]{2,1,0:T(8,128)(2,1)S(1)}, bf16[4,64,256]{2,1,0:T(8,128)(2,1)S(1)}, u32[]{:S(2)}, u32[]{:S(2)}) collective-permute-start(bf16[4,64,256]{2,1,0:T(8,128)(2,1)S(1)} %pad_maximum_fusion.11), channel_id=1, source_target_pairs={{0,6},{1,7},{2,4},{3,5},{4,2},{5,3},{6,0},{7,1},{8,14},{9,15},{10,... | collective-permute-start | bytes 393224 | tf_op jit(solution)/shard_map/ppermute | solution.py:364
  61.6 6.4 %collective-permute-start.20 = (bf16[4,64,256]{2,1,0:T(8,128)(2,1)S(1)}, bf16[4,64,256]{2,1,0:T(8,128)(2,1)S(1)}, u32[]{:S(2)}, u32[]{:S(2)}) collective-permute-start(bf16[4,64,256]{2,1,0:T(8,128)(2,1)S(1)} %pad_maximum_fusion.10), channel_id=1, source_target_pairs={{0,4},{1,5},{2,6},{3,7},{4,0},{5,1},{6,2},{7,3},{8,12},{9,13},{10,... | collective-permute-start | bytes 393224 | tf_op jit(solution)/shard_map/ppermute | solution.py:364
  62.2 5.8 %collective-permute-start.19 = (bf16[4,64,256]{2,1,0:T(8,128)(2,1)S(1)}, bf16[4,64,256]{2,1,0:T(8,128)(2,1)S(1)}, u32[]{:S(2)}, u32[]{:S(2)}) collective-permute-start(bf16[4,64,256]{2,1,0:T(8,128)(2,1)S(1)} %pad_maximum_fusion.9), channel_id=1, source_target_pairs={{0,2},{1,3},{2,0},{3,1},{4,6},{5,7},{6,4},{7,5},{8,10},{9,11},{10,... | collective-permute-start | bytes 393224 | tf_op jit(solution)/shard_map/ppermute | solution.py:364
  63.6 8.1 %collective-permute-start.25 = (bf16[4,64,256]{2,1,0:T(8,128)(2,1)S(1)}, bf16[4,64,256]{2,1,0:T(8,128)(2,1)S(1)}, u32[]{:S(2)}, u32[]{:S(2)}) collective-permute-start(bf16[4,64,256]{2,1,0:T(8,128)(2,1)S(1)} %get-tuple-element.71), channel_id=1, source_target_pairs={{0,24},{8,16},{16,8},{24,0},{1,25},{9,17},{17,9},{25,1},{2,26},{10... | collective-permute-start | bytes 393224 | tf_op jit(solution)/shard_map/ppermute | solution.py:364
  65.3 15.9 %collective-permute-start.26 = (bf16[4,64,256]{2,1,0:T(8,128)(2,1)S(1)}, bf16[4,64,256]{2,1,0:T(8,128)(2,1)S(1)}, u32[]{:S(2)}, u32[]{:S(2)}) collective-permute-start(bf16[4,64,256]{2,1,0:T(8,128)(2,1)S(1)} %get-tuple-element.72), channel_id=1, source_target_pairs={{0,16},{8,24},{16,0},{24,8},{1,17},{9,25},{17,1},{25,9},{2,18},{10... | collective-permute-start | bytes 393224 | tf_op jit(solution)/shard_map/ppermute | solution.py:364
  65.8 15.4 %collective-permute-start.27 = (bf16[4,64,256]{2,1,0:T(8,128)(2,1)S(1)}, bf16[4,64,256]{2,1,0:T(8,128)(2,1)S(1)}, u32[]{:S(2)}, u32[]{:S(2)}) collective-permute-start(bf16[4,64,256]{2,1,0:T(8,128)(2,1)S(1)} %get-tuple-element.73), channel_id=1, source_target_pairs={{0,8},{8,0},{16,24},{24,16},{1,9},{9,1},{17,25},{25,17},{2,10},{10... | collective-permute-start | bytes 393224 | tf_op jit(solution)/shard_map/ppermute | solution.py:364
  69.8 12.8 %collective-permute-start.22 = (bf16[4,64,256]{2,1,0:T(8,128)(2,1)S(1)}, bf16[4,64,256]{2,1,0:T(8,128)(2,1)S(1)}, u32[]{:S(2)}, u32[]{:S(2)}) collective-permute-start(bf16[4,64,256]{2,1,0:T(8,128)(2,1)S(1)} %get-tuple-element.82), channel_id=1, source_target_pairs={{0,24},{8,16},{16,8},{24,0},{1,25},{9,17},{17,9},{25,1},{2,26},{10... | collective-permute-start | bytes 393224 | tf_op jit(solution)/shard_map/ppermute | solution.py:364
  71.6 13.8 %collective-permute-start.23 = (bf16[4,64,256]{2,1,0:T(8,128)(2,1)S(1)}, bf16[4,64,256]{2,1,0:T(8,128)(2,1)S(1)}, u32[]{:S(2)}, u32[]{:S(2)}) collective-permute-start(bf16[4,64,256]{2,1,0:T(8,128)(2,1)S(1)} %get-tuple-element.83), channel_id=1, source_target_pairs={{0,16},{8,24},{16,0},{24,8},{1,17},{9,25},{17,1},{25,9},{2,18},{10... | collective-permute-start | bytes 393224 | tf_op jit(solution)/shard_map/ppermute | solution.py:364
  71.6 13.8 %collective-permute-start.24 = (bf16[4,64,256]{2,1,0:T(8,128)(2,1)S(1)}, bf16[4,64,256]{2,1,0:T(8,128)(2,1)S(1)}, u32[]{:S(2)}, u32[]{:S(2)}) collective-permute-start(bf16[4,64,256]{2,1,0:T(8,128)(2,1)S(1)} %get-tuple-element.84), channel_id=1, source_target_pairs={{0,8},{8,0},{16,24},{24,16},{1,9},{9,1},{17,25},{25,17},{2,10},{10... | collective-permute-start | bytes 393224 | tf_op jit(solution)/shard_map/ppermute | solution.py:364
